TPU v7x, 256 devices: a whole 4x4x8 slice. The times are simulated.
256 devices in a mesh: ctx: 16 (over z, core), grp: 4 (over y), dp: 4 (over x).
Axes of the slice: x: 4, y: 4, z: 8, core: 2. Of those that a mesh axis runs over, the one named last changes fastest.
Arguments:
- hidden_in: bfloat16 [4, 2048, 8192], P('dp', 'ctx'), may hold values from -6 to 6
- teacher_queries: bfloat16 [4, 2048, 8192], P('dp', 'ctx', 'grp'), may hold values from -5 to 5
- teacher_keys: bfloat16 [4, 2048, 1024], P('dp', 'ctx', 'grp'), may hold values from -5 to 5
- teacher_values: bfloat16 [4, 2048, 1024], P('dp', 'ctx', 'grp'), may hold values from -5 to 5
- doc_lengths: int32 [4, 4], P('dp'), may hold values from 1 to 1024, 2048 in all within a row
- dt_weight: bfloat16 [8192, 64], P(None, 'grp'), may hold values from -0.0625 to 0.0625
- dt_bias: float32 [64], P('grp'), may hold values from -2 to 1
- decay_log: float32 [64], P('grp')
- skip_gain: float32 [64], P('grp'), may hold values from 0.5 to 2
- norm_gain: float32 [8192], P('grp'), may hold values from 0.1 to 1.9
Outputs:
- student_out: bfloat16 [4, 2048, 8192], P('dp', 'ctx', 'grp')
- grad_dt_weight: float32 [8192, 64], P(None, 'grp')
- grad_dt_bias: float32 [64], P('grp')
- grad_decay_log: float32 [64], P('grp')
- grad_skip_gain: float32 [64], P('grp')
- grad_norm_gain: float32 [8192], P('grp')
Inputs may be any that keep to these rules, and one draw needn't show every extreme that they name: `doc_lengths`: each row sums to 2048; its longest document has exactly 1024 positions.
All inputs are finite; a program needn't handle non-finite values.
Results may differ from a plain program's by a relative error of at most 0.0028.
Values may be sent and summed in bfloat16 or wider, within the bound.
No kernel may reach another device: no remote copies, remote signals or barrier semaphores. Data moves between devices by JAX's collectives and lax.ppermute only.
A program may use at most 128 MiB of HBM per device.

v0:
```python
import math

import jax
import jax.numpy as jnp
from jax import lax
from jax.sharding import PartitionSpec as P

HEADS = 64
HDIM = 128


EPSILON = 1e-05


def entering_2(value, axis, join, neutral, backward):
    count, mine = (lax.axis_size(axis), lax.axis_index(axis))
    pieces = jax.tree.map(lambda part: lax.all_gather(part, axis), value)
    if backward:
        pieces = jax.tree.map(lambda part: part[::-1], pieces)
        mine = count - 1 - mine
    total = jax.tree.map(
        lambda part, zero: jnp.full_like(part, 0) + jnp.asarray(zero, part.dtype), value, neutral
    )

    def hop(position, total):
        longer = join(total, jax.tree.map(lambda part: part[position], pieces))
        return jax.tree.map(lambda new, old: jnp.where(position < mine, new, old), longer, total)

    return lax.fori_loop(0, count - 1, hop, total)


def segment_of(positions, lengths_row):
    starts = jnp.cumsum(lengths_row) - lengths_row
    return jnp.sum((positions[:, None] >= starts[None, 1:]).astype(jnp.int32), axis=1)


def block_output(
    query_block,
    key_block,
    value_block,
    step_size,
    decay_rate,
    skip_gain,
    segment_block,
    before,
    state_in,
):
    row_count = step_size.shape[0]
    head_count = step_size.shape[1]
    kv_count = key_block.shape[1] // HDIM
    group_size = head_count // kv_count
    query_low = query_block.reshape(row_count, kv_count, group_size, HDIM)
    key_low = key_block.reshape(row_count, kv_count, HDIM)
    value_low = value_block.reshape(row_count, kv_count, HDIM)
    cumulative = jnp.cumsum(-(decay_rate[None, :] * step_size), axis=0)
    cum_split = cumulative.T.reshape(kv_count, group_size, row_count)
    row_order = jnp.arange(row_count, dtype=jnp.int32)
    allowed = (segment_block[:, None] == segment_block[None, :]) & (
        row_order[None, :] <= row_order[:, None]
    )
    log_gaps = jnp.where(allowed, cum_split[:, :, :, None] - cum_split[:, :, None, :], 0.0)
    mixing = jnp.where(allowed, jnp.exp(log_gaps), 0.0) * step_size.T.reshape(
        kv_count, group_size, 1, row_count
    )
    intersection = jnp.einsum(
        "tgrp,ugp->grtu", query_low, key_low, preferred_element_type=jnp.float32
    )
    within = jnp.einsum(
        "grtu,ugp->tgrp",
        intersection * mixing,
        value_low.astype(jnp.float32),
        precision=lax.Precision.HIGH,
    )
    carried = jnp.where(segment_block == before, 1.0, 0.0).astype(step_size.dtype)
    entering = jnp.exp(cumulative).reshape(row_count, kv_count, group_size) * carried[:, None, None]
    state_split = state_in.reshape(kv_count, group_size, HDIM, HDIM)
    entering_term = (
        jnp.einsum(
            "tgrn,grnp->tgrp",
            query_low.astype(jnp.float32),
            state_split,
            precision=lax.Precision.HIGH,
        )
        * entering[..., None]
    )
    direct = (
        skip_gain.reshape(kv_count, group_size)[None, :, :, None]
        * value_low.astype(jnp.float32)[:, :, None, :]
    )
    return (within + entering_term + direct).reshape(row_count, head_count * HDIM)


def block_state(key_block, value_block, step_size, decay_rate, segment_block, before):
    row_count = step_size.shape[0]
    head_count = step_size.shape[1]
    kv_count = key_block.shape[1] // HDIM
    group_size = head_count // kv_count
    key_low = key_block.reshape(row_count, kv_count, HDIM)
    value_low = value_block.reshape(row_count, kv_count, HDIM)
    cumulative = jnp.cumsum(-(decay_rate[None, :] * step_size), axis=0)
    final_log = cumulative[row_count - 1]
    same_final = segment_block == segment_block[row_count - 1]
    tail_weight = (
        jnp.where(
            same_final[:, None],
            jnp.exp(jnp.where(same_final[:, None], final_log[None, :] - cumulative, 0.0)),
            0.0,
        )
        * step_size
    )
    tail_split = tail_weight.T.reshape(kv_count, group_size, row_count)
    weighted = tail_split[:, :, :, None] * jnp.transpose(key_low, (1, 0, 2))[:, None, :, :]
    local_state = jnp.einsum(
        "grun,ugp->grnp", weighted, value_low.astype(jnp.float32), precision=lax.Precision.HIGH
    )
    carried = jnp.where(segment_block[row_count - 1] == before, 1.0, 0.0).astype(step_size.dtype)
    decay_all = jnp.exp(final_log) * carried
    return (decay_all, local_state.reshape(head_count, HDIM, HDIM))


def chain_combine(earlier, later):
    return (earlier[0] * later[0], later[0][:, None, None] * earlier[1] + later[1])


def attend_block(
    running, query_split, query_pos, query_seg, key_split, value_split, key_pos, key_seg, key_form
):
    maxima, totals, accumulated = running
    scores = jnp.einsum(
        "tgrp," + key_form + "->grtu", query_split, key_split, preferred_element_type=jnp.float32
    ) * (1.0 / math.sqrt(HDIM))
    allowed = (key_pos[None, :] <= query_pos[:, None]) & (key_seg[None, :] == query_seg[:, None])
    masked = jnp.where(allowed, scores, -1e30)
    new_max = jnp.maximum(maxima, jnp.max(masked, axis=-1))
    weights = jnp.where(allowed, jnp.exp(scores - new_max[..., None]), 0.0)
    rescale = jnp.exp(maxima - new_max)
    totals = totals * rescale + jnp.sum(weights, axis=-1)
    update = jnp.einsum(
        "grtu," + key_form + "->tgrp",
        weights.astype(jnp.bfloat16),
        value_split,
        preferred_element_type=jnp.float32,
    )
    accumulated = accumulated * jnp.transpose(rescale, (2, 0, 1))[..., None] + update
    return (new_max, totals, accumulated)


def finish_attention(running):
    maxima, totals, accumulated = running
    return (accumulated / jnp.transpose(totals, (2, 0, 1))[..., None]).astype(jnp.bfloat16)


def body(
    hidden_in,
    teacher_queries,
    teacher_keys,
    teacher_values,
    doc_lengths,
    dt_weight,
    dt_bias,
    decay_log,
    skip_gain,
    norm_gain,
):
    row_count = teacher_queries.shape[1]
    head_count = dt_weight.shape[1]
    kv_count = teacher_keys.shape[2] // HDIM
    group_size = head_count // kv_count
    ctx_count = lax.axis_size("ctx")
    first_row = lax.axis_index("ctx") * row_count
    seq_len = row_count * ctx_count
    lengths_row = doc_lengths[0]
    local_positions = first_row + jnp.arange(row_count, dtype=jnp.int32)
    segment_local = segment_of(local_positions, lengths_row)
    before_position = jnp.reshape(jnp.maximum(first_row - 1, 0), (1,))
    segment_before = jnp.where(first_row > 0, segment_of(before_position, lengths_row)[0], -1)
    query_rows = teacher_queries[0]
    key_rows = teacher_keys[0]
    value_rows = teacher_values[0]
    query_split = query_rows.reshape(row_count, kv_count, group_size, HDIM)
    initial = (
        jnp.full((kv_count, group_size, row_count), -1e30, jnp.float32),
        jnp.zeros((kv_count, group_size, row_count), jnp.float32),
        jnp.zeros((row_count, kv_count, group_size, HDIM), jnp.float32),
    )
    kv_piece = (
        lax.all_gather(key_rows, "ctx", axis=0, tiled=True),
        lax.all_gather(value_rows, "ctx", axis=0, tiled=True),
    )
    piece_rows = kv_piece[0].shape[0]
    key_pos = jnp.arange(piece_rows, dtype=jnp.int32)
    key_seg = segment_of(key_pos, lengths_row)
    key_split = kv_piece[0].reshape(piece_rows, kv_count, HDIM)
    value_split = kv_piece[1].reshape(piece_rows, kv_count, HDIM)
    folded = attend_block(
        initial,
        query_split,
        local_positions,
        segment_local,
        key_split,
        value_split,
        key_pos,
        key_seg,
        "ugp",
    )
    teacher_out = finish_attention(folded).reshape(row_count, head_count * HDIM)
    pre = jnp.dot(hidden_in[0], dt_weight, preferred_element_type=jnp.float32) + dt_bias
    step_size = jax.nn.softplus(pre)
    decay_rate = jnp.exp(decay_log)

    def state_terms(step_value, rate_value):
        return block_state(
            key_rows, value_rows, step_value, rate_value, segment_local, segment_before
        )

    def output_terms(step_value, rate_value, skip_value, state_value):
        return block_output(
            query_rows,
            key_rows,
            value_rows,
            step_value,
            rate_value,
            skip_value,
            segment_local,
            segment_before,
            state_value,
        )

    (decay_all, local_state), state_pullback = jax.vjp(state_terms, step_size, decay_rate)
    identity = (jnp.ones_like(decay_all), jnp.zeros_like(local_state))
    scanned = entering_2((decay_all, local_state), "ctx", chain_combine, identity, False)
    state_in = scanned[1]
    raw, output_pullback = jax.vjp(output_terms, step_size, decay_rate, skip_gain, state_in)
    square_sum = lax.psum(jnp.sum(raw * raw, axis=1), "grp")
    inverse = lax.rsqrt(square_sum / (HEADS * HDIM) + EPSILON)
    normed = raw * inverse[:, None] * norm_gain
    difference = normed - teacher_out.astype(jnp.float32)
    grad_normed = difference * (2.0 / (lax.axis_size("dp") * seq_len))
    grad_gain = jnp.sum(grad_normed * raw * inverse[:, None], axis=0)
    gained = grad_normed * norm_gain
    inner_sum = lax.psum(jnp.sum(gained * raw, axis=1), "grp")
    grad_raw = (
        inverse[:, None] * gained
        - raw * (inverse * inverse * inverse * inner_sum / (HEADS * HDIM))[:, None]
    )
    grad_step_one, grad_rate_one, grad_skip, grad_state = output_pullback(grad_raw)
    reversed_scan = entering_2((decay_all, grad_state), "ctx", chain_combine, identity, True)
    state_grad_out = reversed_scan[1]
    grad_decay_all = jnp.sum(state_grad_out * state_in, axis=(1, 2))
    grad_step_two, grad_rate_two = state_pullback((grad_decay_all, state_grad_out))
    grad_pre = (grad_step_one + grad_step_two) * jax.nn.sigmoid(pre)
    grad_weight = jnp.einsum(
        "td,th->dh", hidden_in[0], grad_pre.astype(jnp.bfloat16), preferred_element_type=jnp.float32
    )
    grad_bias = jnp.sum(grad_pre, axis=0)
    grad_decay = (grad_rate_one + grad_rate_two) * decay_rate
    summed = lax.psum((grad_weight, grad_bias, grad_decay, grad_skip, grad_gain), ("ctx", "dp"))
    return (
        normed.astype(jnp.bfloat16)[None],
        summed[0],
        summed[1],
        summed[2],
        summed[3],
        summed[4],
    )


def solution(mesh):
    placed = (
        P("dp", "ctx", None),
        P("dp", "ctx", "grp"),
        P("dp", "ctx", "grp"),
        P("dp", "ctx", "grp"),
        P("dp", None),
        P(None, "grp"),
        P("grp"),
        P("grp"),
        P("grp"),
        P("grp"),
    )
    return jax.shard_map(
        body,
        mesh=mesh,
        in_specs=placed,
        out_specs=(P("dp", "ctx", "grp"), P(None, "grp"), P("grp"), P("grp"), P("grp"), P("grp")),
        check_vma=False,
    )
```

profile of v0, /device:TPU:1, one launch (start us, length us, event | category | flops | bytes accessed | tf_op | source)
XLA Modules:
  0.0 595.4 jit_solution(11085915382331593379)
XLA Ops:
  8.0 1.6 copy.118
  14.9 1.6 multiply_negate_fusion
  20.9 1.5 fusion.48
  23.2 2.0 copy.158
  25.1 1.5 copy.115
  26.6 1.3 mul.466
  28.0 22.4 %all-gather.2 = f32[16,1,16]{2,1,0:T(1,128)} all-gather(f32[1,1,16]{2,1,0:T(1,128)} %bitcast.287), channel_id=1, replica_groups=mesh['ctx'=16,'grp'=4,'dp'=4] {'ctx'}, dimensions={0}, use_global_device_ids=true | all-gather | bytes 1088 | tf_op jit(solution)/shard_map/all_gather | solution.py:17
  51.8 1.3 bitcast_multiply_fusion.4
  55.2 1.3 multiply_bitcast_fusion
  57.2 1.4 convolution_bitcast_fusion.1
  58.6 2.5 fusion.50
  62.2 2.3 copy.121
  64.4 26.3 %all-gather.12.cloned.1.call-done = bf16[1,2048,256]{1,2,0:T(8,128)(2,1)} async-done(((bf16[1,128,256]{1,2,0:T(8,128)(2,1)}), bf16[1,2048,256]{1,2,0:T(8,128)(2,1)}) %all-gather.12.cloned.1.call-update) | async-done | bytes 1048592 | tf_op jit(solution)/shard_map/all_gather | solution.py:187
  90.8 9.8 %fusion.2 = (f32[2,8,128]{2,1,0:T(8,128)S(1)}, f32[2,2048,128,8]{2,1,3,0:T(8,128)}) fusion(pred[128,2048]{0,1:T(8,128)(4,1)S(1)} %fusion.55, bf16[2048,2,128,1]{0,2,3,1:T(8,128)(2,1)} %bitcast.274, bf16[128,2,8,128]{3,2,1,0:T(8,128)(2,1)} %bitcast.263), kind=kOutput, calls=%fused_computation.8 | convolution fusion | flops 1086322688 | bytes 18620416 | tf_op jit(solution)/shard_map/tgrp,ugp->grtu/dot_general | solution.py:129
  101.2 9.9 %fusion.5 = f32[2,8,128]{2,1,0:T(8,128)S(1)} fusion(f32[2,2048,128,8]{2,1,3,0:T(8,128)} %get-tuple-element.291, f32[2,8,128]{2,1,0:T(8,128)S(1)} %broadcast_maximum_fusion, pred[128,2048]{0,1:T(8,128)(4,1)S(1)} %fusion.55), kind=kLoop, calls=%fused_computation.11 | loop fusion | flops 16775168 | bytes 17055744 | tf_op jit(solution)/shard_map/reduce_sum | solution.py:137
  112.2 74.9 %all-gather.8.cloned.1.call-done = f32[16,16,128,128]{3,2,1,0:T(8,128)} async-done(((f32[1,16,128,128]{3,2,1,0:T(8,128)}), f32[16,16,128,128]{3,2,1,0:T(8,128)}) %all-gather.8.cloned.1.call-update) | async-done | bytes 16777232 | tf_op jit(solution)/shard_map/all_gather | solution.py:17
  187.2 40.0 %while.28 = (s32[]{:T(128)}, f32[16,128,128]{2,1,0:T(8,128)S(1)}, s32[]{:T(128)}, f32[16,16]{1,0:T(8,128)}, f32[16,16,128,128]{3,2,1,0:T(8,128)}, /*index=5*/s32[]{:T(128)}, s32[]{:T(128)}) while((s32[]{:T(128)}, f32[16,128,128]{2,1,0:T(8,128)S(1)}, s32[]{:T(128)}, f32[16,16]{1,0:T(8,128)}, f32[16,16,128,128]{3,2,1,0:T(8,128)}, ...), condition=%wide.region_5.6_spmd.clone, body=%wide.region_4.5_spmd.clone.sunk | while | flops 1048580 | bytes 3146025 | solution.py:29
  188.3 1.5 fusion.133
  191.0 1.5 fusion.133
  193.7 1.5 fusion.133
  196.3 1.5 fusion.133
  199.0 1.5 fusion.133
  201.7 1.5 fusion.133
  204.3 1.5 fusion.133
  207.0 1.5 fusion.133
  209.7 1.5 fusion.133
  212.3 1.5 fusion.133
  215.0 1.5 fusion.133
  217.7 1.5 fusion.133
  220.3 1.5 fusion.133
  223.0 1.5 fusion.133
  225.7 1.5 fusion.133
  227.1 4.5 multiply_reduce_fusion.5
  231.7 9.2 %psum.49 = f32[128]{0:T(128)} all-reduce(f32[128]{0:T(128)} %get-tuple-element.272), channel_id=1, replica_groups=mesh['ctx'=16,'grp'=4,'dp'=4] {'grp'}, use_global_device_ids=true, to_apply=%region_7.8 | all-reduce | flops 128 | bytes 1024 | tf_op jit(solution)/shard_map/psum | solution.py:234
  241.6 9.7 %multiply_reduce_fusion.4 = (f32[128]{0:T(128)}, bf16[128,2,8,128]{0,3,2,1:T(8,128)(2,1)}, f32[2,8,128,128]{2,3,1,0:T(8,128)}) fusion(f32[128,2,8,128]{0,3,2,1:T(8,128)} %get-tuple-element.273, f32[2,8,128]{2,1,0:T(8,128)} %get-tuple-element.279, f32[2,8,128]{2,1,0:T(8,128)} %bitcast.279, f32[128]{0:T(128)S(1)} %add_rsqrt_fusion, ...), kind=kOutput, calls=%fused_computation.60 | convolution fusion | flops 1093140352 | bytes 20751360 | tf_op jit(solution)/shard_map/grtu,ugp->tgrp/dot_general | solution.py:138
  251.2 6.1 %psum.50 = f32[128]{0:T(128)S(1)} all-reduce(f32[128]{0:T(128)} %get-tuple-element.270), channel_id=1, replica_groups=mesh['ctx'=16,'grp'=4,'dp'=4] {'grp'}, use_global_device_ids=true, to_apply=%region_12.13 | all-reduce | flops 128 | bytes 1024 | tf_op jit(solution)/shard_map/psum | solution.py:241
  258.0 3.1 fusion.28
  262.5 1.3 rev.6
  263.8 3.2 multiply_reduce_fusion.1
  267.0 4.9 fusion.59
  273.9 2.7 copy.117
  276.7 82.6 %all-gather.10.cloned.1.call-done = f32[16,16,128,128]{3,2,1,0:T(8,128)} async-done(((f32[1,16,128,128]{3,2,1,0:T(8,128)}), f32[16,16,128,128]{3,2,1,0:T(8,128)}) %all-gather.10.cloned.1.call-update) | async-done | bytes 16777232 | tf_op jit(solution)/shard_map/all_gather | solution.py:17
  359.3 11.6 %rev.7 = f32[16,16,128,128]{3,2,1,0:T(8,128)} reverse(f32[16,16,128,128]{3,2,1,0:T(8,128)} %all-gather.10.cloned.1.call-done), dimensions={0} | reverse | bytes 33554432 | tf_op jit(solution)/shard_map/rev | solution.py:19
  371.0 32.5 %while.29 = (s32[]{:T(128)}, f32[16,128,128]{2,1,0:T(8,128)S(1)}, s32[]{:T(128)}, f32[16,16]{1,0:T(8,128)}, f32[16,16,128,128]{3,2,1,0:T(8,128)}, /*index=5*/s32[]{:T(128)}, s32[]{:T(128)}) while((s32[]{:T(128)}, f32[16,128,128]{2,1,0:T(8,128)S(1)}, s32[]{:T(128)}, f32[16,16]{1,0:T(8,128)}, f32[16,16,128,128]{3,2,1,0:T(8,128)}, ...), condition=%wide.region_19.20_spmd.clone, body=%wide.region_18.19_spmd.clone.sunk | while | flops 1048580 | bytes 3146025 | solution.py:29
  371.7 1.5 fusion.134
  373.9 1.5 fusion.134
  376.1 1.5 fusion.134
  378.2 1.5 fusion.134
  380.4 1.5 fusion.134
  382.6 1.5 fusion.134
  384.7 1.5 fusion.134
  386.9 1.5 fusion.134
  389.1 1.5 fusion.134
  391.2 1.5 fusion.134
  393.4 1.5 fusion.134
  395.6 1.5 fusion.134
  397.7 1.5 fusion.134
  399.9 1.5 fusion.134
  402.1 1.5 fusion.134
  403.5 1.4 multiply_reduce_fusion.2
  408.8 2.2 multiply_convert_fusion
  411.0 127.4 %all-reduce.1 = (f32[16]{0:T(128)}, f32[16]{0:T(128)}, f32[16]{0:T(128)}, f32[2048]{0:T(1024)}) all-reduce(f32[16]{0:T(128)S(1)} %get-tuple-element.276, f32[16]{0:T(128)S(1)} %add_multiply_fusion, f32[16]{0:T(128)S(1)} %reshape.286, f32[2048]{0:T(1024)S(1)} %bitcast.284), channel_id=1, replica_groups=mesh['ctx'=16,'grp'=4,'dp'=4] {'ctx','dp'}, use_global_device_ids=true, to_apply=%region_26.27 | all-reduce | flops 2096 | bytes 16768 | tf_op jit(solution)/shard_map/psum | solution.py:257
  538.5 48.5 %all-reduce.4.cloned.1.call-done = f32[8192,16]{0,1:T(8,128)} async-done(((f32[8192,16]{0,1:T(8,128)}), f32[8192,16]{0,1:T(8,128)}) %all-reduce.4.cloned.1.call-update) | async-done | bytes 524304 | tf_op jit(solution)/shard_map/psum | solution.py:257
  587.0 1.9 copy.196
  (146 shorter events, 54.0 us)
Async XLA Ops:
  7.2 7.8 %copy-start = (bf16[1,128,8192]{2,1,0:T(8,128)(2,1)S(1)}, bf16[1,128,8192]{2,1,0:T(8,128)(2,1)}, u32[]{:S(2)}) copy-start(bf16[1,128,8192]{2,1,0:T(8,128)(2,1)} %param.14) | copy-start | bytes 6291460
  7.2 55.0 %all-gather.14.cloned.1.call-start = ((), (), s32[]{:S(2)}) async-start(), calls=%async_computation.4 | async-start | bytes 1114112 | tf_op jit(solution)/shard_map/all_gather | solution.py:188
  7.9 82.9 %all-gather.12.cloned.1.call-start = ((), (), s32[]{:S(2)}) async-start(), calls=%async_computation.3 | async-start | bytes 1114112 | tf_op jit(solution)/shard_map/all_gather | solution.py:187
  9.6 177.6 %all-gather.8.cloned.1.call-start = ((), (), s32[]{:S(2)}) async-start(), calls=%async_computation | async-start | bytes 17825792 | tf_op jit(solution)/shard_map/all_gather | solution.py:17
  10.5 48.1 %copy-start.2 = (bf16[128,2,128]{2,1,0:T(2,128)(2,1)}, bf16[128,2,128]{2,1,0:T(2,128)(2,1)S(1)}, u32[]{:S(2)}) copy-start(bf16[128,2,128]{2,1,0:T(2,128)(2,1)S(1)} %reshape_squeeze.14) | copy-start | bytes 196612
  12.2 2.0 copy-start.24
  13.6 0.7 copy-start.22
  13.7 6.1 %copy-start.17 = (s32[128]{0:T(128)}, s32[128]{0:T(128)S(1)}, u32[]{:S(2)}) copy-start(s32[128]{0:T(128)S(1)} %convert_reduce_fusion.1) | copy-start | bytes 1540
  14.9 1.6 copy-start.18
  16.8 41.8 %copy-start.5 = (f32[128,16]{1,0:T(8,128)}, f32[128,16]{1,0:T(8,128)S(1)}, u32[]{:S(2)}) copy-start(f32[128,16]{1,0:T(8,128)S(1)} %reduce_window_sum.38) | copy-start | bytes 24580
  19.1 0.7 copy-start.11
  19.7 0.5 copy-start.14
  22.4 336.9 %all-gather.10.cloned.1.call-start = ((), (), s32[]{:S(2)}) async-start(), calls=%async_computation.1 | async-start | bytes 17825792 | tf_op jit(solution)/shard_map/all_gather | solution.py:17
  51.8 5.4 copy-start.16
  55.2 5.9 copy-start.10
  58.6 2.5 copy-start.4
  100.6 0.6 copy-start.8
  227.1 24.1 %copy-start.1 = (f32[16,128,128]{2,1,0:T(8,128)}, f32[16,128,128]{2,1,0:T(8,128)S(1)}, u32[]{:S(2)}) copy-start(f32[16,128,128]{2,1,0:T(8,128)S(1)} %get-tuple-element.194) | copy-start | bytes 3145732
  241.6 9.7 %copy-start.20 = (f32[128]{0:T(128)}, f32[128]{0:T(128)S(1)}, u32[]{:S(2)}) copy-start(f32[128]{0:T(128)S(1)} %add_rsqrt_fusion) | copy-start | bytes 1540
  251.2 20.8 %copy-start.6 = (f32[128,16]{1,0:T(8,128)S(1)}, f32[128,16]{1,0:T(8,128)}, u32[]{:S(2)}) copy-start(f32[128,16]{1,0:T(8,128)} %copy-done.5) | copy-start | bytes 24580
  262.4 324.6 %all-reduce.4.cloned.1.call-start = ((), (), s32[]{:S(2)}) async-start(), calls=%async_computation.2 | async-start | bytes 1048576 | tf_op jit(solution)/shard_map/psum | solution.py:257
  370.9 34.2 %copy-start.3 = (bf16[128,2,128]{2,1,0:T(2,128)(2,1)S(1)}, bf16[128,2,128]{2,1,0:T(2,128)(2,1)}, u32[]{:S(2)}) copy-start(bf16[128,2,128]{2,1,0:T(2,128)(2,1)} %copy-done.2) | copy-start | bytes 196612
  370.9 34.7 %copy-start.12 = (f32[16]{0:T(128)S(1)}, f32[16]{0:T(128)}, u32[]{:S(2)}) copy-start(f32[16]{0:T(128)} %copy-done.11) | copy-start | bytes 196
  370.9 34.7 %copy-start.15 = (pred[128]{0:T(512)(128)(4,1)S(1)}, pred[128]{0:T(512)(128)(4,1)}, u32[]{:S(2)}) copy-start(pred[128]{0:T(512)(128)(4,1)} %copy-done.14) | copy-start | bytes 388
  370.9 36.4 %copy-start.13 = (f32[2,8,128]{2,1,0:T(8,128)S(1)}, f32[2,8,128]{2,1,0:T(8,128)}, u32[]{:S(2)}) copy-start(f32[2,8,128]{2,1,0:T(8,128)} %get-tuple-element.237) | copy-start | bytes 24580
  370.9 36.4 %copy-start.19 = (f32[16]{0:T(128)S(1)}, f32[16]{0:T(128)}, u32[]{:S(2)}) copy-start(f32[16]{0:T(128)} %copy-done.18) | copy-start | bytes 196
  370.9 37.8 %copy-start.7 = (f32[2048]{0:T(1024)S(1)}, f32[2048]{0:T(1024)}, u32[]{:S(2)}) copy-start(f32[2048]{0:T(1024)} %param.23) | copy-start | bytes 24580
  370.9 37.8 %copy-start.21 = (f32[128]{0:T(128)S(1)}, f32[128]{0:T(128)}, u32[]{:S(2)}) copy-start(f32[128]{0:T(128)} %copy-done.20) | copy-start | bytes 1540
  371.0 40.0 %copy-start.23 = (f32[2,8]{1,0:T(2,128)S(1)}, f32[2,8]{1,0:T(2,128)}, u32[]{:S(2)}) copy-start(f32[2,8]{1,0:T(2,128)} %get-tuple-element.232) | copy-start | bytes 196
  371.0 40.1 %copy-start.25 = (f32[16]{0:T(128)S(1)}, f32[16]{0:T(128)}, u32[]{:S(2)}) copy-start(f32[16]{0:T(128)} %param.21) | copy-start | bytes 196
  371.0 40.1 %copy-start.9 = (f32[2,8,128]{2,1,0:T(8,128)S(1)}, f32[2,8,128]{2,1,0:T(8,128)}, u32[]{:S(2)}) copy-start(f32[2,8,128]{2,1,0:T(8,128)} %get-tuple-element.234) | copy-start | bytes 24580
Sparse Core Ops, SparseCore 0:
  9.8 42.7 all-gather.13
  54.4 36.3 all-gather.11
  92.6 94.5 all-gather.7
  262.6 96.6 all-gather.9
  408.9 178.1 all-reduce.3
where the time goes:
time: 599 us; the launch traced here: 595 us
  waiting for transfers between devices  233 us (39%)
  blocking collectives  165 us (28%)
  other arithmetic  78.7 us (13%)
  local copies, waits for them, and re-layouts  61.6 us (10%)
  matrix products  40.5 us (7%)
  between operations  15.4 us (3%)
    all_gather x2, waiting for transfers between devices, entering_2(): pieces = jax.tree.map(lambda part: lax.all_gather(part, axis), value)  158 us
    psum x1, blocking collectives, body(): lax.psum((grad_weight, grad_bias, grad_decay, grad_skip, grad_gain), ('ct...  127 us
    psum x1, waiting for transfers between devices, body(): lax.psum((grad_weight, grad_bias, grad_decay, grad_skip, grad_gain), ('ct...  48.5 us
    select_n x30, other arithmetic, hop(): jnp.where(position < mine, new, old)  43.6 us
    mul x30, local copies, waits for them, and re-layouts, chain_combine(): later[0][:, None, None] * earlier[1] + later[1]  28.3 us
    all_gather x1, waiting for transfers between devices, body(): lax.all_gather(key_rows, 'ctx', axis=0, tiled=True)  26.3 us
    all_gather x1, blocking collectives, entering_2(): pieces = jax.tree.map(lambda part: lax.all_gather(part, axis), value)  22.4 us
    rev x2, local copies, waits for them, and re-layouts, entering_2(): pieces = jax.tree.map(lambda part: part[::-1], pieces)  12.9 us
  transfers between devices with their start and end apart: 5, of which 4 were waited for; matrix products, arithmetic and copies ran while one was open for 12% of the time, Pallas kernels for 0%

commit v1 on v0

v1 whole, which is shorter than its diff:
```python
import functools
import math

import jax
import jax.numpy as jnp
from jax import lax
from jax.experimental import pallas as pl
from jax.experimental.pallas import tpu as pltpu
from jax.sharding import PartitionSpec as P

HDIM = 128
EPSILON = 1e-05
BACK = 8
NEG = -1e30
LOG2E = math.log2(math.e)
F32 = jnp.float32
BF16 = jnp.bfloat16


def mm(a, b):
    return jnp.dot(a, b, preferred_element_type=F32)


def two_parts(x):
    high = x.astype(BF16)
    return high, (x - high.astype(F32)).astype(BF16)


def mm_two(a, b):
    high, low = two_parts(a)
    return mm(high, b) + mm(low, b)


def mm_right(a, b):
    high, low = two_parts(b)
    return mm(a, high) + mm(a, low)


def iota(shape, dim):
    return lax.broadcasted_iota(jnp.int32, shape, dim)


def to_row(x):
    rows = x.shape[0]
    if rows < 128:
        x = jnp.concatenate([x, jnp.zeros((128 - rows, x.shape[1]), F32)], axis=0)
    return jnp.sum(x.T, axis=0, keepdims=True)


def column_of(values, rows):
    row = iota((rows, 128), 0)
    out = jnp.zeros((rows, 128), F32)
    for h in range(rows):
        out = jnp.where(row == h, values[h], out)
    return out


def place_of(consts, rows):
    core = lax.axis_index("core")
    place = lax.axis_index("z") * lax.axis_size("core") + core
    starts = [consts[i : i + 1, :].astype(jnp.int32) for i in range(3)]
    return (place * rows, *starts, core, place)


def segment_at(pos, info):
    return (
        (pos >= info[1]).astype(jnp.int32)
        + (pos >= info[2]).astype(jnp.int32)
        + (pos >= info[3]).astype(jnp.int32)
    )


def prep_kernel(
    kv, lengths, bias, decay, skip, gain, hidden, weight, keys, values, payload, slope, consts
):
    pre = (
        lax.dot_general(
            weight[...], hidden[...], (((1,), (1,)), ((), ())), preferred_element_type=F32
        )
        + column_of(bias, weight.shape[0])
    )
    step = jnp.maximum(pre, 0.0) + jnp.log1p(jnp.exp(-jnp.abs(pre)))
    slope[...] = 1.0 / (1.0 + jnp.exp(-pre))
    for g in range(kv):
        cols = slice(g * HDIM, (g + 1) * HDIM)
        payload[g * HDIM : (g + 1) * HDIM, :] = keys[:, cols].astype(F32).T.astype(BF16)
        payload[(kv + g) * HDIM : (kv + g + 1) * HDIM, :] = values[:, cols]
    heads = step.shape[0]
    consts[0:heads, :] = jnp.exp(column_of(decay, heads))
    consts[heads : 2 * heads, :] = column_of(skip, heads)
    for h in range(heads):
        consts[2 * heads + h : 2 * heads + h + 1, :] = gain[:, h * HDIM : (h + 1) * HDIM]
    one = lengths[0, 0]
    two = one + lengths[0, 1]
    starts = (one, two, two + lengths[0, 2], 0, 0, 0, 0, 0)
    row = iota((8, 128), 0)
    marks = jnp.zeros((8, 128), jnp.int32)
    for i in range(3):
        marks = jnp.where(row == i, starts[i], marks)
    consts[3 * heads :, :] = marks.astype(F32)
    first = 2 * kv * HDIM
    for part in range(3):
        piece = step.astype(BF16)
        payload[first + part * heads : first + (part + 1) * heads, :] = piece
        step = step - piece.astype(F32)


def masks(info):
    first = info[0]
    before = jnp.where(
        first > 0, segment_at(jnp.maximum(first - 1, 0) + iota((1, 128), 1) * 0, info), -1
    )
    row_pos = first + iota((128, 128), 0)
    col_pos = first + iota((128, 128), 1)
    row_seg = segment_at(row_pos, info)
    allowed = (row_seg == segment_at(col_pos, info)) & (col_pos <= row_pos)
    carried = row_seg == before
    return first, before, allowed, carried


def match_row(info, first, before, d, rows):
    pos = first - 128 * d + iota((rows, 128), 1)
    return (segment_at(pos, info) == before) & (pos >= 0)


PARTS = ((0, 1, 2), (3, 4), (5, 6, 7, 8))


def layout(*sizes):
    starts, total = [], 0
    for size in sizes:
        starts.append(total)
        total += -(-size // 128) * 128
    return starts, total


def carry_rows(heads, kv, blocks, first):
    past = len(blocks) - (1 if first else 0)
    small = heads * (2 + len(blocks) + past)
    turned = 0 if first else kv * len(blocks) * 128
    wide = heads * 128
    return layout(wide, wide, wide, wide, small, 3 * heads + 8 if first else 0, turned, turned)


def keep_rows(heads, kv, blocks):
    turned = kv * len(blocks) * 128
    return layout(heads * 128, heads * 128, kv * 128, turned, turned)


def real_rows(heads, kv):
    count = BACK + 1
    wide = heads * 128
    return layout(wide, wide, wide, 3 * heads + 8, count * heads, BACK * heads, kv * count * 128)


def half_rows(heads, kv):
    return layout(heads * 128, kv * (BACK + 1) * 128)


def slab(start, h):
    return pl.ds(pl.multiple_of(start + h * 128, 128), 128)


def forward_kernel(kv, heads, blocks, first, last, *refs):
    refs = list(refs)

    def take(count):
        out = refs[:count]
        del refs[:count]
        return out

    queries = take(1)[0]
    sources = [take(1 if d % 2 == 0 else 2) for d in blocks]
    if first:
        consts, carry, keep, kt, vv, bias, key32 = refs
    elif not last:
        origin, carry, kt, vv, bias, key32 = refs
        before_carry, before_at = origin, carry_rows(heads, kv, PARTS[0], True)[0]
    else:
        origin, before_carry, keep, real, half, stats, kt, vv, bias, key32, acc = refs
        before_at = carry_rows(heads, kv, PARTS[1], False)[0]
        acc[...] = jnp.zeros_like(acc)
    origin_at = carry_rows(heads, kv, PARTS[0], True)[0]
    keep_at = keep_rows(heads, kv, PARTS[0])[0]
    real_at = real_rows(heads, kv)[0]
    half_at = half_rows(heads, kv)[0]
    carry_at = carry_rows(heads, kv, blocks, first)[0]
    if first:
        constant, base = consts, 0
        carry[carry_at[5] : carry_at[5] + consts.shape[0], :] = consts[...]
        cum_ref = carry
    else:
        constant, base = origin, origin_at[5]
        cum_ref = origin
    cum_at = origin_at[4] + heads
    group = heads // kv
    size = 3 * heads + 8
    info = place_of(constant[base + size - 8 : base + size, :], queries.shape[0])
    even_core = info[4] == 0
    start, before, allowed, carried = masks(info)

    reach = (iota((128, 128), 0) <= iota((128, 128), 1)).astype(BF16)
    if first:
        after = jnp.zeros((heads, 128), F32)
    else:
        after = before_carry[before_at[4] : before_at[4] + heads, :]
    rate = constant[base : base + heads, :]
    own = 1 if first else 0
    past = len(blocks) - own
    steps, fades = [], []
    for i, d in enumerate(blocks):
        at = slice(128 * i, 128 * i + 128)
        near = sources[i]

        def piece(low, high):
            if d % 2 == 0:
                return near[0][low:high, :]
            return jnp.where(even_core, near[0][low:high, :], near[1][low:high, :])

        for g in range(kv):
            block = piece(g * HDIM, (g + 1) * HDIM)
            value = piece((kv + g) * HDIM, (kv + g + 1) * HDIM)
            kt[g, :, at] = block
            vv[g, at, :] = value
            block, value = block.astype(F32), value.astype(F32)
            if last:
                row = (g * (BACK + 1) + d) * 128
                half[half_at[1] + row : half_at[1] + row + 128, :] = kt[g, :, at]
                real[real_at[6] + row : real_at[6] + row + 128, :] = value.T
            else:
                row = (g * len(blocks) + i) * 128
                out, where = (keep, keep_at[3:5]) if first else (carry, carry_at[6:8])
                out[where[0] + row : where[0] + row + 128, :] = block
                out[where[1] + row : where[1] + row + 128, :] = value.T
            if d == 0:
                keep[keep_at[2] + 128 * g : keep_at[2] + 128 * g + 128, :] = value
            else:
                key32[g, :, 128 * (i - own) : 128 * (i - own) + 128] = block
        first_step = 2 * kv * HDIM
        parts = [piece(first_step + k * heads, first_step + (k + 1) * heads) for k in range(3)]
        step = parts[0].astype(F32) + parts[1].astype(F32) + parts[2].astype(F32)
        sums = mm(parts[0], reach) + mm(parts[1], reach) + mm(parts[2], reach)
        steps.append(step)
        if d == 0:
            carry[cum_at : cum_at + heads, :] = sums
            bias[:, at] = jnp.where(allowed, 0.0, NEG)
        else:
            total = jnp.broadcast_to(sums[:, 127:128], (heads, 128))
            left = jnp.maximum(total - sums, 0.0) + after
            found = match_row(info, start, before, d, heads)
            fades.append(jnp.where(found, jnp.exp(-rate * left), 0.0))
            after = after + total
            both = carried & match_row(info, start, before, d, 128)
            bias[:, at] = jnp.where(both, 0.0, NEG)
    if last:
        small, step_at, fade_at = real, real_at[4] + heads * blocks[0], real_at[5]
        fade_at = fade_at + heads * (blocks[0] - 1)
        real[real_at[3] : real_at[3] + size, :] = origin[base : base + size, :]
        for p, source in ((0, origin), (1, before_carry)):
            where = carry_rows(heads, kv, PARTS[p], p == 0)[0]
            count = len(PARTS[p])
            low = where[4] + heads * 2
            rows = heads * count
            to = real_at[4] + heads * PARTS[p][0]
            real[to : to + rows, :] = source[low : low + rows, :]
            low, back = low + rows, count - (1 if p == 0 else 0)
            rows = heads * back
            to = real_at[5] + heads * (max(PARTS[p][0], 1) - 1)
            real[to : to + rows, :] = source[low : low + rows, :]
            turned, where = (keep, keep_at[3:5]) if p == 0 else (source, where[6:8])
            for g in range(kv):
                rows = 128 * count
                low = g * rows
                to = (g * (BACK + 1) + PARTS[p][0]) * 128
                half[half_at[1] + to : half_at[1] + to + rows, :] = turned[
                    where[0] + low : where[0] + low + rows, :
                ].astype(BF16)
                real[real_at[6] + to : real_at[6] + to + rows, :] = turned[
                    where[1] + low : where[1] + low + rows, :
                ]
    else:
        small, step_at = carry, carry_at[4] + heads * 2
        fade_at = step_at + heads * len(blocks)
        carry[carry_at[4] : carry_at[4] + heads, :] = after
    for i, step in enumerate(steps):
        small[step_at + heads * i : step_at + heads * (i + 1), :] = step
    for i, fade in enumerate(fades):
        small[fade_at + heads * i : fade_at + heads * (i + 1), :] = fade

    def one_head(h, unused):
        g = h // group
        query = queries[:, slab(0, h)]
        scores = mm(query, kt[g])
        scaled = scores * (LOG2E / math.sqrt(HDIM)) + bias[...]
        top = jnp.broadcast_to(jnp.max(scaled, axis=1, keepdims=True), (128, 128))
        if not first:
            old = before_carry[slab(before_at[0], h), :]
            top = jnp.maximum(old, top)
        weights = [
            jnp.exp2(scaled[:, 128 * i : 128 * i + 128] - top) for i in range(len(blocks))
        ]
        total = weights[0]
        for other in weights[1:]:
            total = total + other
        total = jnp.broadcast_to(jnp.sum(total, axis=1, keepdims=True), (128, 128))
        mixed = mm(jnp.concatenate([w.astype(BF16) for w in weights], axis=1), vv[g])
        weight_row = jnp.concatenate(
            [
                small[pl.ds(fade_at + heads * i + h, 1), :]
                * small[pl.ds(step_at + heads * (own + i) + h, 1), :]
                for i in range(past)
            ],
            axis=1,
        )
        state = mm_two(key32[g] * weight_row, vv[g, 128 * own :, :])
        if not first:
            scale = jnp.exp2(old - top)
            total = total + before_carry[slab(before_at[1], h), :] * scale
            mixed = mixed + before_carry[slab(before_at[2], h), :] * scale
            state = state + before_carry[slab(before_at[3], h), :]
        if not last:
            carry[slab(carry_at[0], h), :] = top
            carry[slab(carry_at[1], h), :] = total
            carry[slab(carry_at[2], h), :] = mixed
            carry[slab(carry_at[3], h), :] = state
        rate_h = constant[pl.ds(base + h, 1), :]
        if first:
            cum_row = jnp.broadcast_to(cum_ref[pl.ds(cum_at + h, 1), :], (128, 128))
            cum_col = cum_row.T
            decay = jnp.where(
                allowed, jnp.exp(-rate_h * jnp.maximum(cum_col - cum_row, 0.0)), 0.0
            )
            decayed = scores[:, :128] * decay
            keep[slab(keep_at[1], h), :] = decayed
            skipped = (
                constant[pl.ds(base + heads + h, 1), :] * keep[slab(keep_at[2], g), :]
            )
            mixing = decayed * small[pl.ds(step_at + h, 1), :]
            keep[slab(keep_at[0], h), :] = mm_two(mixing, vv[g, :128, :]) + skipped
        if last:
            teach = (mixed / total).astype(BF16)
            half[slab(half_at[0], h), :] = teach
            cum_col = jnp.broadcast_to(cum_ref[pl.ds(cum_at + h, 1), :], (128, 128)).T
            entering = jnp.where(carried, jnp.exp(-rate_h * cum_col), 0.0)
            off = mm_right(query, state) * entering
            raw = keep[slab(keep_at[0], h), :] + off
            real[slab(real_at[0], h), :] = raw
            real[slab(real_at[1], h), :] = off
            real[slab(real_at[2], h), :] = entering
            gained = raw * constant[pl.ds(base + 2 * heads + h, 1), :]
            acc[0] += raw * raw
            acc[1] += gained * gained
            acc[2] += gained * teach.astype(F32)
        return unused

    lax.fori_loop(0, heads, one_head, 0, unroll=4)
    if last:
        stats[...] = jnp.concatenate(
            [to_row(acc[0]), to_row(acc[1]), to_row(acc[2]), jnp.zeros((5, 128), F32)], axis=0
        )


def forward(kv, heads, rows, part, operands):
    blocks = PARTS[part]
    first, last = part == 0, part == len(PARTS) - 1
    wide = 128 * len(blocks)
    past = len(blocks) - (1 if first else 0)
    if last:
        outs = [
            shape((real_rows(heads, kv)[1], 128)),
            shape((half_rows(heads, kv)[1], 128), BF16),
            shape((8, 128)),
        ]
    else:
        outs = [shape((carry_rows(heads, kv, blocks, first)[1], 128))]
    if first:
        outs.append(shape((keep_rows(heads, kv, blocks)[1], 128)))
    scratch = [
        pltpu.VMEM((kv, HDIM, wide), BF16),
        pltpu.VMEM((kv, wide, HDIM), BF16),
        pltpu.VMEM((rows, wide), F32),
        pltpu.VMEM((kv, HDIM, 128 * past), F32),
    ]
    if last:
        scratch.append(pltpu.VMEM((3, rows, HDIM), F32))
    return pl.pallas_call(
        functools.partial(forward_kernel, kv, heads, blocks, first, last),
        out_shape=outs,
        in_specs=vmem(len(operands)),
        out_specs=vmem(len(outs)),
        scratch_shapes=scratch,
        compiler_params=SMALL,
        cost_estimate=pl.CostEstimate(
            flops=len(blocks) * heads * rows * 128 * 128 * 12,
            bytes_accessed=len(blocks) * 3 * 1024 * 1024,
            transcendentals=2 * heads * rows * wide,
        ),
        name="forward_" + "abc"[part],
    )(*operands)


def backward_kernel(kv, heads, features, row_total, *refs):
    queries, keep, real, half, stats, student_out, grads, gain_out, small_out, *refs = refs
    inv_col, coef_col, late, skip_rows, direct_rows, minus_rows, row_sums = refs
    keep_at = keep_rows(heads, kv, PARTS[0])[0]
    real_at = real_rows(heads, kv)[0]
    half_at = half_rows(heads, kv)[0]
    group = heads // kv
    size = 3 * heads + 8
    base = real_at[3]
    info = place_of(real[base + size - 8 : base + size, :], queries.shape[0])
    place, count = info[5], grads.shape[0]
    grads[...] = jnp.zeros_like(grads)
    row_sums[...] = jnp.zeros_like(row_sums)
    share = 2.0 / row_total
    squares, gained_squares, crossed = stats[0:1, :], stats[1:2, :], stats[2:3, :]
    inverse = lax.rsqrt(squares / features + EPSILON)
    inner = share * (inverse * gained_squares - crossed)
    coef = inverse * inverse * inverse * inner / features
    inv_col[...] = jnp.broadcast_to(inverse, (128, 128)).T
    coef_col[...] = jnp.broadcast_to(coef, (128, 128)).T
    row_i, col_i = iota((128, 128), 0), iota((128, 128), 1)
    later = (row_i >= col_i).astype(BF16)
    strict = (row_i < col_i).astype(BF16)

    def one_head(h, unused):
        g = h // group
        cols = slab(0, h)
        query = queries[:, cols]
        raw, off = real[slab(real_at[0], h), :], real[slab(real_at[1], h), :]
        scale = real[pl.ds(base + 2 * heads + h, 1), :]
        inv = inv_col[...]
        normed = raw * inv * scale
        student_out[:, cols] = normed.astype(BF16)
        grad_normed = (normed - half[slab(half_at[0], h), :].astype(F32)) * share
        gain_out[:, cols] = jnp.sum(grad_normed * raw * inv, axis=0, keepdims=True)
        grad = inv * grad_normed * scale - raw * coef_col[...]
        value = keep[slab(keep_at[2], g), :]
        skip_rows[pl.ds(h, 1), :] = jnp.sum(grad * value, axis=0, keepdims=True)
        entering = real[slab(real_at[2], h), :]
        grad_state = mm_two((grad * entering).T, query)
        turned = [slab(g * ((BACK + 1) * 128), d) for d in range(BACK + 1)]
        keys = jnp.concatenate(
            [half[pl.ds(half_at[1] + turned[d].start, 128), :] for d in range(1, BACK + 1)],
            axis=1,
        )
        reached = mm_two(grad_state, keys)
        for d in range(1, BACK + 1):
            values = real[pl.ds(real_at[6] + turned[d].start, 128), :]
            late[d - 1, pl.ds(h, 1), :] = jnp.sum(
                reached[:, 128 * d - 128 : 128 * d] * values, axis=0, keepdims=True
            )
        own_values = real[pl.ds(real_at[6] + turned[0].start, 128), :].astype(BF16)
        pulled = mm_two(grad, own_values)
        pairs = keep[slab(keep_at[1], h), :] * pulled
        direct_rows[pl.ds(h, 1), :] = jnp.sum(pairs, axis=0, keepdims=True)
        pairs = jnp.where(
            row_i > col_i, pairs * real[pl.ds(real_at[4] + h, 1), :], 0.0
        )
        minus_rows[pl.ds(h, 1), :] = jnp.sum(pairs, axis=0, keepdims=True)
        sums = jnp.sum(pairs + grad * off, axis=1, keepdims=True)
        row_sums[...] += jnp.where(col_i == h, jnp.broadcast_to(sums, (128, 128)), 0.0)
        return unused

    lax.fori_loop(0, heads, one_head, 0, unroll=4)

    def summed(x, triangle):
        high, low = two_parts(x)
        rest = (x - high.astype(F32) - low.astype(F32)).astype(BF16)
        return mm(high, triangle) + mm(low, triangle) + mm(rest, triangle)

    rate = real[base : base + heads, :]
    spanned = summed(row_sums[...].T[:heads, :] - minus_rows[...], later)
    grads[place] = direct_rows[...] - rate * spanned
    rate_rows = spanned * real[real_at[4] : real_at[4] + heads, :]
    earlier = jnp.zeros((heads, 128), F32)
    for d in range(BACK, 0, -1):
        step = real[real_at[4] + heads * d : real_at[4] + heads * (d + 1), :]
        fade = real[real_at[5] + heads * (d - 1) : real_at[5] + heads * d, :]
        direct = late[d - 1] * fade
        whole = direct * step
        spanned = summed(whole, strict) + earlier
        grads[lax.rem(place - d + count, count)] = direct - rate * spanned
        rate_rows = rate_rows + spanned * step
        earlier = earlier + jnp.sum(whole, axis=1, keepdims=True)
    small_out[...] = jnp.concatenate(
        [to_row(skip_rows[...]), -to_row(rate_rows * rate), jnp.zeros((6, 128), F32)], axis=0
    )


def weight_kernel(slope, hidden, gain, small, grads, keep, send):
    total = jnp.sum(grads[...], axis=0)
    grad_pre = total * slope[...]
    low = grad_pre.astype(BF16)
    heads = low.shape[0]
    count = keep.shape[0] // (heads + 1)
    tiles = gain.shape[1] // 128
    core = lax.axis_index("core")

    def fill(out, half):
        for j in range(count):
            i = half * count + j
            start = j * (heads + 1)
            out[start : start + heads, :] = mm(low, hidden[:, 128 * i : 128 * i + 128])
            at = slice(start + heads, start + heads + 1)
            if i < tiles:
                out[at, :] = gain[:, 128 * i : 128 * i + 128]
            elif i == tiles:
                out[at, :] = to_row(grad_pre)
            elif i == tiles + 1:
                out[at, :] = small[1:2, :]
            elif i == tiles + 2:
                out[at, :] = small[0:1, :]
            else:
                out[at, :] = jnp.zeros((1, 128), F32)

    for mine in range(2):

        @pl.when(core == mine)
        def _():
            fill(keep, mine)
            fill(send, 1 - mine)


def finish_kernel(mine, other, weight, bias, decay, skip, gain):
    heads = weight.shape[0]
    count = mine.shape[0] // (heads + 1)
    tiles = gain.shape[1] // 128
    core = lax.axis_index("core")

    def place(source, half):
        for j in range(count):
            i = half * count + j
            start = j * (heads + 1)
            weight[:, 128 * i : 128 * i + 128] = source[start : start + heads, :]
            row = source[start + heads : start + heads + 1, :]
            if i < tiles:
                gain[:, 128 * i : 128 * i + 128] = row
            if i == tiles:
                bias[...] = row[:, :heads]
            if i == tiles + 1:
                decay[...] = row[:, :heads]
            if i == tiles + 2:
                skip[...] = row[:, :heads]

    for half in range(2):

        @pl.when(core == half)
        def _():
            place(mine, half)
            place(other, 1 - half)


def vmem(count):
    return [pl.BlockSpec(memory_space=pltpu.VMEM)] * count


def smem(count):
    return [pl.BlockSpec(memory_space=pltpu.SMEM)] * count


def shape(dims, kind=F32):
    return jax.ShapeDtypeStruct(dims, kind)


LARGE = pltpu.CompilerParams(vmem_limit_bytes=56 * 1024 * 1024)
SMALL = pltpu.CompilerParams(vmem_limit_bytes=16 * 1024 * 1024)


def body(
    hidden_in,
    teacher_queries,
    teacher_keys,
    teacher_values,
    doc_lengths,
    dt_weight,
    dt_bias,
    decay_log,
    skip_gain,
    norm_gain,
):
    rows = teacher_queries.shape[1]
    heads = dt_weight.shape[1]
    kv = teacher_keys.shape[2] // HDIM
    width = heads * HDIM
    features = width * lax.axis_size("grp")
    depth = hidden_in.shape[2]
    chips = lax.axis_size("z")
    blocks = 2 * chips
    row_total = lax.axis_size("dp") * rows * blocks
    hidden = hidden_in[0]
    gain = norm_gain[None, :]
    cargo = 2 * kv * HDIM + 3 * heads

    payload, slope, consts = pl.pallas_call(
        functools.partial(prep_kernel, kv),
        out_shape=[
            shape((cargo, 128), BF16),
            shape((heads, 128)),
            shape((3 * heads + 8, 128)),
        ],
        in_specs=smem(4) + vmem(5),
        out_specs=vmem(3),
        compiler_params=LARGE,
        name="prep",
    )(
        doc_lengths, dt_bias, decay_log, skip_gain, gain, hidden, dt_weight.T,
        teacher_keys[0], teacher_values[0],
    )

    swap = [(0, 1), (1, 0)]
    hop = [(i, (i + 1) % chips) for i in range(chips)]
    jump = [(i, (i + 4) % chips) for i in range(chips)]
    queries = teacher_queries[0]
    run = functools.partial(forward, kv, heads, rows)

    def across(part):
        return lax.ppermute(part, "core", swap)

    hop1 = lax.ppermute(payload, "z", hop)
    hop4 = lax.ppermute(payload, "z", jump)
    sib0 = across(payload)
    hop2 = lax.ppermute(hop1, "z", hop)
    sib1 = across(hop1)
    origin, keep = run(0, [queries, payload, sib1, sib0, hop1, consts])
    hop2, hop4, origin = lax.optimization_barrier((hop2, hop4, origin))
    hop3 = lax.ppermute(hop2, "z", hop)
    sib2, sib4 = across(hop2), across(hop4)
    (carry,) = run(1, [queries, sib2, sib1, hop2, origin])
    hop3, carry = lax.optimization_barrier((hop3, carry))
    sib3 = across(hop3)
    real, half, stats = run(
        2, [queries, sib3, sib2, hop3, sib4, sib3, hop4, origin, carry, keep]
    )

    stats = lax.psum(stats, "grp")

    student, grads, grad_gain, small = pl.pallas_call(
        functools.partial(backward_kernel, kv, heads, features, row_total),
        out_shape=[
            shape((rows, width), BF16),
            shape((blocks, heads, 128)),
            shape((1, width)),
            shape((8, 128)),
        ],
        in_specs=vmem(5),
        out_specs=vmem(4),
        scratch_shapes=[
            pltpu.VMEM((rows, 128), F32),
            pltpu.VMEM((rows, 128), F32),
            pltpu.VMEM((BACK, heads, 128), F32),
            pltpu.VMEM((heads, 128), F32),
            pltpu.VMEM((heads, 128), F32),
            pltpu.VMEM((heads, 128), F32),
            pltpu.VMEM((128, 128), F32),
        ],
        compiler_params=SMALL,
        name="backward",
    )(queries, keep, real, half, stats)

    grads = lax.all_to_all(grads, ("z", "core"), 0, 0, tiled=True)

    axes = ("z", "dp")
    count = chips * lax.axis_size("dp")
    part = shape((count * (heads + 1), 128))
    keep, send = pl.pallas_call(
        weight_kernel,
        out_shape=[part, part],
        in_specs=vmem(5),
        out_specs=vmem(2),
        compiler_params=SMALL,
        name="weights",
    )(slope, hidden, grad_gain, small, grads)

    half = keep + lax.ppermute(send, "core", swap)
    half = half.reshape(count, heads + 1, 1, 128)
    got = lax.all_to_all(half, axes, 0, 0, tiled=True)
    summed = jnp.sum(got, axis=0)
    spread = jnp.broadcast_to(summed[None], got.shape)
    mine = lax.all_to_all(spread, axes, 0, 0, tiled=True)
    mine = mine.reshape(count * (heads + 1), 128)
    other = lax.ppermute(mine, "core", swap)
    grad_weight, bias, decay, skip, gained = pl.pallas_call(
        finish_kernel,
        out_shape=[shape((heads, depth))] + [shape((1, heads))] * 3 + [shape((1, width))],
        in_specs=vmem(2),
        out_specs=vmem(5),
        compiler_params=SMALL,
        name="finish",
    )(mine, other)
    return (student[None], grad_weight.T, bias[0], decay[0], skip[0], gained[0])


def solution(mesh):
    sizes = dict(mesh.shape)
    split = jax.sharding.Mesh(
        mesh.devices.reshape(sizes["ctx"] // 2, 2, sizes["grp"], sizes["dp"]),
        ("z", "core", "grp", "dp"),
    )
    ctx = ("z", "core")
    placed = (
        P("dp", ctx, None),
        P("dp", ctx, "grp"),
        P("dp", ctx, "grp"),
        P("dp", ctx, "grp"),
        P("dp", None),
        P(None, "grp"),
        P("grp"),
        P("grp"),
        P("grp"),
        P("grp"),
    )
    return jax.shard_map(
        body,
        mesh=split,
        in_specs=placed,
        out_specs=(P("dp", ctx, "grp"), P(None, "grp"), P("grp"), P("grp"), P("grp"), P("grp")),
        check_vma=False,
    )
```

time: 599 us -> 125 us (0.21)
  waiting for transfers between devices: 233 us -> 12 us
  blocking collectives: 165 us -> 54.8 us
  other arithmetic: 78.7 us -> 0.2 us
  local copies, waits for them, and re-layouts: 61.6 us -> 9.51 us
  matrix products: 40.5 us -> 0 us
  Pallas kernels: 0 us -> 33.4 us
  between operations: 15.4 us -> 0.73 us
  starting transfers between devices: 0.2 us -> 14.2 us
    all_gather x4 -> x0, waiting for transfers between devices: 184 us -> none  [the longest x2 158 us: entering_2(): pieces = jax.tree.map(lambda part: lax.all_gather(part, axis), value)]
    psum x3 -> x1, blocking collectives: 143 us -> 8.69 us  [body(): stats = lax.psum(stats, 'grp')]
    psum x1 -> x0, waiting for transfers between devices: 48.5 us -> none  [body(): lax.psum((grad_weight, grad_bias, grad_decay, grad_skip, grad_gain), ('ct...]
    all_to_all x0 -> x3, blocking collectives: none -> 46.1 us  [the longest x1 16.6 us: body(): got = lax.all_to_all(half, axes, 0, 0, tiled=True)]
    select_n x31 -> x0, other arithmetic: 44.3 us -> none  [the longest x30 43.6 us: hop(): jnp.where(position < mine, new, old)]
    dot_general x11 -> x0, matrix products: 40.5 us -> none  [the longest x1 9.79 us: attend_block(): jnp.einsum('tgrp,' + key_form + '->grtu', query_split, key_split, preferr...]
    pallas_call x0 -> x7, Pallas kernels: none -> 33.4 us  [the longest x3 21.6 us: forward(): pl.pallas_call(functools.partial(forward_kernel, kv, heads, blocks, first...]
    mul x32 -> x0, local copies, waits for them, and re-layouts: 29.7 us -> none  [the longest x30 28.3 us: chain_combine(): later[0][:, None, None] * earlier[1] + later[1]]
  transfers between devices with their start and end apart: 5 -> 11, of which waited for: 4 -> 6; matrix products, arithmetic and copies ran while one was open for 12% -> 0% of each run, Pallas kernels for 0% -> 11%
where the time goes in v1:
time: 125 us
  blocking collectives  54.8 us (44%)
  Pallas kernels  33.4 us (27%)
  starting transfers between devices  14.2 us (11%)
  waiting for transfers between devices  12 us (10%)
  local copies, waits for them, and re-layouts  9.51 us (8%)
    pallas_call x3, Pallas kernels, forward(): pl.pallas_call(functools.partial(forward_kernel, kv, heads, blocks, first...  21.6 us
    all_to_all x1, blocking collectives, body(): got = lax.all_to_all(half, axes, 0, 0, tiled=True)  16.6 us
    all_to_all x1, blocking collectives, body(): mine = lax.all_to_all(spread, axes, 0, 0, tiled=True)  15 us
    all_to_all x1, blocking collectives, body(): grads = lax.all_to_all(grads, ('z', 'core'), 0, 0, tiled=True)  14.5 us
    unnamed x20, local copies, waits for them, and re-layouts  9.37 us
    psum x1, blocking collectives, body(): stats = lax.psum(stats, 'grp')  8.69 us
    pallas_call x1, Pallas kernels, body(): pl.pallas_call(functools.partial(backward_kernel, kv, heads, features, ro...  7.26 us
    ppermute x1, waiting for transfers between devices, body(): hop1 = lax.ppermute(payload, 'z', hop)  6.68 us
  transfers between devices with their start and end apart: 11, of which 6 were waited for; matrix products, arithmetic and copies ran while one was open for 0% of the time, Pallas kernels for 11%

profile of v1, /device:TPU:1, one launch (start us, length us, event | category | flops | bytes accessed | tf_op | source)
XLA Modules:
  0.0 124.8 jit_solution(15034067322372004892)
XLA Ops:
  0.6 0.0 copy-start.2
  0.6 3.0 %prep.1 = (bf16[560,128]{1,0:T(8,128)(2,1)}, f32[16,128]{1,0:T(8,128)}, f32[56,128]{1,0:T(8,128)}) custom-call(s32[1,4]{1,0:T(1,128)} %lengths.1, f32[16]{0:T(128)} %bias.1, f32[16]{0:T(128)} %decay.1, f32[16]{0:T(128)} %skip.1, f32[1,2048]{1,0:T(1,128)} %bitcast.26, bf16[128,8192]{1,0:T(8,128)(2,1)} %bitcast.14, bf16[16,8192]{1,0:T(8,128)(2,1)} %bitcast.23, ...), custom_call_target="tpu_custom_call" | custom-call | tf_op jit(solution)/shard_map/prep/pallas_call | solution.py:595
  3.7 2.5 %collective-permute-start = (bf16[560,128]{1,0:T(8,128)(2,1)}, bf16[560,128]{1,0:T(8,128)(2,1)S(1)}, u32[]{:S(2)}, u32[]{:S(2)}) collective-permute-start(bf16[560,128]{1,0:T(8,128)(2,1)} %get-tuple-element.30.refs_1_), channel_id=1, source_target_pairs={{0,32},{32,64},{64,96},{96,128},{128,160},{160,192},{192,224},{224... | collective-permute-start | bytes 430088 | tf_op jit(solution)/shard_map/ppermute | solution.py:620
  6.2 1.0 collective-permute-start.2
  7.1 6.7 %collective-permute-done.refs_4_ = bf16[560,128]{1,0:T(8,128)(2,1)S(1)} collective-permute-done((bf16[560,128]{1,0:T(8,128)(2,1)}, bf16[560,128]{1,0:T(8,128)(2,1)S(1)}, u32[]{:S(2)}, u32[]{:S(2)}) %collective-permute-start) | collective-permute-done | bytes 143392 | tf_op jit(solution)/shard_map/ppermute | solution.py:620
  13.8 1.2 collective-permute-start.1
  15.0 4.0 %collective-permute-start.4 = (bf16[560,128]{1,0:T(8,128)(2,1)}, bf16[560,128]{1,0:T(8,128)(2,1)S(1)}, u32[]{:S(2)}, u32[]{:S(2)}) collective-permute-start(bf16[560,128]{1,0:T(8,128)(2,1)} %get-tuple-element.30.refs_1_), channel_id=1, source_target_pairs={{0,128},{32,160},{64,192},{96,224},{128,0},{160,32},{192,64},{224,... | collective-permute-start | bytes 430088 | tf_op jit(solution)/shard_map/ppermute | solution.py:621
  19.0 0.0 collective-permute-start.3
  19.0 0.0 collective-permute-done.2.refs_3_
  19.0 0.0 collective-permute-done.1.refs_2_
  19.0 0.0 copy-start.1
  19.0 1.0 copy-done.1
  20.1 0.0 copy-start.8
  20.1 0.9 copy-done.8
  21.0 0.0 copy-start.9
  21.0 0.7 copy-done.9
  21.7 9.8 %forward_a.1 = (f32[8448,128]{1,0:T(8,128)S(1)}, f32[5888,128]{1,0:T(8,128)S(1)}) custom-call(bf16[128,2048]{1,0:T(8,128)(2,1)S(1)} %bitcast.16, bf16[560,128]{1,0:T(8,128)(2,1)S(1)} %copy-done.8, bf16[560,128]{1,0:T(8,128)(2,1)S(1)} %collective-permute-done.1.refs_2_, bf16[560,128]{1,0:T(8,128)(2,1)S(1)} %collective-permute-done.2.refs_3_, ...), custom_call_target="tpu_custom_call" | custom-call | flops 1207959552 | bytes 9437184 | tf_op jit(solution)/shard_map/forward_a/pallas_call | solution.py:386
  31.5 0.0 collective-permute-done.4.refs_6_
  31.5 0.0 collective-permute-done.3.refs_3_
  31.5 0.4 collective-permute-start.6
  31.9 0.6 collective-permute-start.5
  32.5 0.4 collective-permute-start.8
  32.8 0.2 collective-permute-done.6.refs_1_.refs_2_
  33.0 0.0 copy-done.2
  33.0 4.4 %forward_b.1.refs_8_ = f32[9344,128]{1,0:T(8,128)S(1)} custom-call(bf16[128,2048]{1,0:T(8,128)(2,1)S(1)} %bitcast.17, bf16[560,128]{1,0:T(8,128)(2,1)S(1)} %collective-permute-done.6.refs_1_.refs_2_, bf16[560,128]{1,0:T(8,128)(2,1)S(1)} %collective-permute-done.1.refs_2_, bf16[560,128]{1,0:T(8,128)(2,1)S(1)} %collective-permute-done.3.refs_3_, ...), custom_call_target="tpu_custom_call" | custom-call | flops 805306368 | bytes 6291456 | tf_op jit(solution)/shard_map/forward_b/pallas_call | solution.py:386
  37.4 1.4 %collective-permute-done.5.refs_3_ = bf16[560,128]{1,0:T(8,128)(2,1)S(1)} collective-permute-done((bf16[560,128]{1,0:T(8,128)(2,1)S(1)}, bf16[560,128]{1,0:T(8,128)(2,1)S(1)}, u32[]{:S(2)}, u32[]{:S(2)}) %collective-permute-start.5) | collective-permute-done | bytes 143392 | tf_op jit(solution)/shard_map/ppermute | solution.py:627
  38.8 0.7 collective-permute-start.7
  39.6 0.0 collective-permute-done.8.refs_4_
  39.6 1.0 collective-permute-done.7.refs_1_.refs_5_
  40.6 7.4 %forward_c.1 = (f32[8960,128]{1,0:T(8,128)S(1)}, bf16[4352,128]{1,0:T(8,128)(2,1)S(1)}, f32[8,128]{1,0:T(8,128)S(1)}) custom-call(bf16[128,2048]{1,0:T(8,128)(2,1)S(1)} %bitcast.18, bf16[560,128]{1,0:T(8,128)(2,1)S(1)} %collective-permute-done.7.refs_1_.refs_5_, bf16[560,128]{1,0:T(8,128)(2,1)S(1)} %collective-permute-done.6.refs_1_.refs_2_, ...), custom_call_target="tpu_custom_call" | custom-call | flops 1610612736 | bytes 12582912 | tf_op jit(solution)/shard_map/forward_c/pallas_call | solution.py:386
  47.9 0.0 copy-start.3
  47.9 2.1 %copy-done.3 = f32[8960,128]{1,0:T(8,128)} copy-done((f32[8960,128]{1,0:T(8,128)}, f32[8960,128]{1,0:T(8,128)S(1)}, u32[]{:S(2)}) %copy-start.3) | copy-done | bytes 4587544
  50.0 0.0 copy-start.5
  50.0 1.0 copy-done.5
  51.1 8.7 %psum.7.refs_4_ = f32[8,128]{1,0:T(8,128)S(1)} all-reduce(f32[8,128]{1,0:T(8,128)S(1)} %get-tuple-element.41), channel_id=1, replica_groups=mesh['z'=8,'core'=2,'grp'=4,'dp'=4] {'grp'}, use_global_device_ids=true, to_apply=%region_0.0 | all-reduce | flops 1024 | bytes 8192 | tf_op jit(solution)/shard_map/psum | solution.py:636
  59.7 0.0 copy-start.4
  59.7 2.3 %copy-done.4 = f32[8960,128]{1,0:T(8,128)S(1)} copy-done((f32[8960,128]{1,0:T(8,128)S(1)}, f32[8960,128]{1,0:T(8,128)}, u32[]{:S(2)}) %copy-start.4) | copy-done | bytes 4587544
  62.0 0.0 copy-start.6
  62.0 1.2 copy-done.6
  63.3 0.0 copy-start
  63.3 0.0 copy-start.7
  63.3 7.3 %backward.1 = (bf16[128,2048]{1,0:T(8,128)(2,1)}, f32[16,16,128]{2,1,0:T(8,128)S(1)}, f32[1,2048]{1,0:T(1,128)S(1)}, f32[8,128]{1,0:T(8,128)S(1)}) custom-call(bf16[128,2048]{1,0:T(8,128)(2,1)S(1)} %bitcast.19, f32[5888,128]{1,0:T(8,128)S(1)} %get-tuple-element.32.refs_9_.refs_1_, f32[8960,128]{1,0:T(8,128)S(1)} %copy-done.4, ...), custom_call_target="tpu_custom_call" | custom-call | tf_op jit(solution)/shard_map/backward/pallas_call | solution.py:638
  70.6 14.5 %all_to_all.15.grads = f32[16,16,128]{2,1,0:T(8,128)S(1)} all-to-all(f32[16,16,128]{2,1,0:T(8,128)S(1)} %get-tuple-element.46), channel_id=1, replica_groups=mesh['z'=8,'core'=2,'grp'=4,'dp'=4] {'z','core'}, dimensions={0} | all-to-all | bytes 262144 | tf_op jit(solution)/shard_map/all_to_all | solution.py:661
  85.0 0.0 copy-done
  85.0 0.0 copy-done.7
  85.0 0.7 weights.1
  85.7 0.1 collective-permute-start.9
  85.8 1.5 %collective-permute-done.9 = f32[544,128]{1,0:T(8,128)S(1)} collective-permute-done((f32[544,128]{1,0:T(8,128)S(1)}, f32[544,128]{1,0:T(8,128)S(1)}, u32[]{:S(2)}, u32[]{:S(2)}) %collective-permute-start.9) | collective-permute-done | bytes 278560 | tf_op jit(solution)/shard_map/ppermute | solution.py:675
  87.4 16.6 %all_to_all.16 = f32[32,17,1,128]{3,2,1,0:T(1,128)S(1)} all-to-all(f32[32,17,1,128]{3,2,1,0:T(1,128)S(1)} %bitcast.22), channel_id=1, replica_groups=mesh['z'=8,'core'=2,'grp'=4,'dp'=4] {'z','dp'}, dimensions={0} | all-to-all | bytes 557056 | tf_op jit(solution)/shard_map/all_to_all | solution.py:677
  104.0 0.2 reduce_sum.9
  104.2 0.1 broadcast_in_dim.14
  104.3 15.0 %all_to_all.17 = f32[32,17,1,128]{3,2,1,0:T(1,128)S(1)} all-to-all(f32[32,17,1,128]{3,2,1,0:T(1,128)S(1)} %broadcast_in_dim.14), channel_id=1, replica_groups=mesh['z'=8,'core'=2,'grp'=4,'dp'=4] {'z','dp'}, dimensions={0} | all-to-all | bytes 557056 | tf_op jit(solution)/shard_map/all_to_all | solution.py:680
  119.4 3.5 %collective-permute-start.10 = (f32[544,128]{1,0:T(8,128)S(1)}, f32[544,128]{1,0:T(8,128)S(1)}, u32[]{:S(2)}, u32[]{:S(2)}) collective-permute-start(f32[544,128]{1,0:T(8,128)S(1)} %bitcast.20), channel_id=1, source_target_pairs={{0,16},{16,0},{1,17},{17,1},{2,18},{18,2},{3,19},{19,3},{4,20},{20... | collective-permute-start | bytes 835592 | tf_op jit(solution)/shard_map/ppermute | solution.py:682
  122.8 1.2 collective-permute-done.10.other
  124.0 0.8 finish.1
  (1 shorter events, 0.0 us)
Async XLA Ops:
  0.6 32.4 %copy-start.2 = (bf16[1,128,2048]{2,1,0:T(8,128)(2,1)S(1)}, bf16[1,128,2048]{2,1,0:T(8,128)(2,1)}, u32[]{:S(2)}) copy-start(bf16[1,128,2048]{2,1,0:T(8,128)(2,1)} %param.11) | copy-start | bytes 1572868
  3.7 10.1 %collective-permute-start = (bf16[560,128]{1,0:T(8,128)(2,1)}, bf16[560,128]{1,0:T(8,128)(2,1)S(1)}, u32[]{:S(2)}, u32[]{:S(2)}) collective-permute-start(bf16[560,128]{1,0:T(8,128)(2,1)} %get-tuple-element.30.refs_1_), channel_id=1, source_target_pairs={{0,32},{32,64},{64,96},{96,128},{128,160},{160,192},{192,224},{224... | collective-permute-start | bytes 430088 | tf_op jit(solution)/shard_map/ppermute | solution.py:620
  6.2 12.9 %collective-permute-start.2 = (bf16[560,128]{1,0:T(8,128)(2,1)}, bf16[560,128]{1,0:T(8,128)(2,1)S(1)}, u32[]{:S(2)}, u32[]{:S(2)}) collective-permute-start(bf16[560,128]{1,0:T(8,128)(2,1)} %get-tuple-element.30.refs_1_), channel_id=1, source_target_pairs={{0,16},{16,0},{1,17},{17,1},{2,18},{18,2},{3,19},{19,3},{4,20},{20... | collective-permute-start | bytes 430088 | tf_op jit(solution)/shard_map/ppermute | solution.py:618
  13.8 5.2 %collective-permute-start.1 = (bf16[560,128]{1,0:T(8,128)(2,1)S(1)}, bf16[560,128]{1,0:T(8,128)(2,1)S(1)}, u32[]{:S(2)}, u32[]{:S(2)}) collective-permute-start(bf16[560,128]{1,0:T(8,128)(2,1)S(1)} %collective-permute-done.refs_4_), channel_id=1, source_target_pairs={{0,16},{16,0},{1,17},{17,1},{2,18},{18,2},{3,19},{19,3},{4,20},{20... | collective-permute-start | bytes 430088 | tf_op jit(solution)/shard_map/ppermute | solution.py:618
  15.0 16.5 %collective-permute-start.4 = (bf16[560,128]{1,0:T(8,128)(2,1)}, bf16[560,128]{1,0:T(8,128)(2,1)S(1)}, u32[]{:S(2)}, u32[]{:S(2)}) collective-permute-start(bf16[560,128]{1,0:T(8,128)(2,1)} %get-tuple-element.30.refs_1_), channel_id=1, source_target_pairs={{0,128},{32,160},{64,192},{96,224},{128,0},{160,32},{192,64},{224,... | collective-permute-start | bytes 430088 | tf_op jit(solution)/shard_map/ppermute | solution.py:621
  19.0 12.5 %collective-permute-start.3 = (bf16[560,128]{1,0:T(8,128)(2,1)S(1)}, bf16[560,128]{1,0:T(8,128)(2,1)S(1)}, u32[]{:S(2)}, u32[]{:S(2)}) collective-permute-start(bf16[560,128]{1,0:T(8,128)(2,1)S(1)} %collective-permute-done.refs_4_), channel_id=1, source_target_pairs={{0,32},{32,64},{64,96},{96,128},{128,160},{160,192},{192,224},{224... | collective-permute-start | bytes 430088 | tf_op jit(solution)/shard_map/ppermute | solution.py:623
  19.0 1.0 copy-start.1
  20.1 0.9 copy-start.8
  21.0 0.7 copy-start.9
  31.5 1.5 %collective-permute-start.6 = (bf16[560,128]{1,0:T(8,128)(2,1)S(1)}, bf16[560,128]{1,0:T(8,128)(2,1)S(1)}, u32[]{:S(2)}, u32[]{:S(2)}) collective-permute-start(bf16[560,128]{1,0:T(8,128)(2,1)S(1)} %collective-permute-done.3.refs_3_), channel_id=1, source_target_pairs={{0,16},{16,0},{1,17},{17,1},{2,18},{18,2},{3,19},{19,3},{4,20},{20... | collective-permute-start | bytes 430088 | tf_op jit(solution)/shard_map/ppermute | solution.py:618
  31.9 6.9 %collective-permute-start.5 = (bf16[560,128]{1,0:T(8,128)(2,1)S(1)}, bf16[560,128]{1,0:T(8,128)(2,1)S(1)}, u32[]{:S(2)}, u32[]{:S(2)}) collective-permute-start(bf16[560,128]{1,0:T(8,128)(2,1)S(1)} %collective-permute-done.3.refs_3_), channel_id=1, source_target_pairs={{0,32},{32,64},{64,96},{96,128},{128,160},{160,192},{192,224},{224... | collective-permute-start | bytes 430088 | tf_op jit(solution)/shard_map/ppermute | solution.py:627
  32.5 7.1 %collective-permute-start.8 = (bf16[560,128]{1,0:T(8,128)(2,1)S(1)}, bf16[560,128]{1,0:T(8,128)(2,1)S(1)}, u32[]{:S(2)}, u32[]{:S(2)}) collective-permute-start(bf16[560,128]{1,0:T(8,128)(2,1)S(1)} %collective-permute-done.4.refs_6_), channel_id=1, source_target_pairs={{0,16},{16,0},{1,17},{17,1},{2,18},{18,2},{3,19},{19,3},{4,20},{20... | collective-permute-start | bytes 430088 | tf_op jit(solution)/shard_map/ppermute | solution.py:618
  38.8 1.7 %collective-permute-start.7 = (bf16[560,128]{1,0:T(8,128)(2,1)S(1)}, bf16[560,128]{1,0:T(8,128)(2,1)S(1)}, u32[]{:S(2)}, u32[]{:S(2)}) collective-permute-start(bf16[560,128]{1,0:T(8,128)(2,1)S(1)} %collective-permute-done.5.refs_3_), channel_id=1, source_target_pairs={{0,16},{16,0},{1,17},{17,1},{2,18},{18,2},{3,19},{19,3},{4,20},{20... | collective-permute-start | bytes 430088 | tf_op jit(solution)/shard_map/ppermute | solution.py:618
  47.9 2.1 %copy-start.3 = (f32[8960,128]{1,0:T(8,128)}, f32[8960,128]{1,0:T(8,128)S(1)}, u32[]{:S(2)}) copy-start(f32[8960,128]{1,0:T(8,128)S(1)} %get-tuple-element.39.refs_2_) | copy-start | bytes 13762564
  50.0 1.0 copy-start.5
  59.7 2.3 %copy-start.4 = (f32[8960,128]{1,0:T(8,128)S(1)}, f32[8960,128]{1,0:T(8,128)}, u32[]{:S(2)}) copy-start(f32[8960,128]{1,0:T(8,128)} %copy-done.3) | copy-start | bytes 13762564
  62.0 1.2 copy-start.6
  63.3 21.7 %copy-start = (bf16[1,128,8192]{2,1,0:T(8,128)(2,1)S(1)}, bf16[1,128,8192]{2,1,0:T(8,128)(2,1)}, u32[]{:S(2)}) copy-start(bf16[1,128,8192]{2,1,0:T(8,128)(2,1)} %param.10) | copy-start | bytes 6291460
  63.3 21.7 %copy-start.7 = (f32[16,128]{1,0:T(8,128)S(1)}, f32[16,128]{1,0:T(8,128)}, u32[]{:S(2)}) copy-start(f32[16,128]{1,0:T(8,128)} %get-tuple-element.43.slope) | copy-start | bytes 24580
  85.7 1.6 %collective-permute-start.9 = (f32[544,128]{1,0:T(8,128)S(1)}, f32[544,128]{1,0:T(8,128)S(1)}, u32[]{:S(2)}, u32[]{:S(2)}) collective-permute-start(f32[544,128]{1,0:T(8,128)S(1)} %get-tuple-element.48), channel_id=1, source_target_pairs={{0,16},{16,0},{1,17},{17,1},{2,18},{18,2},{3,19},{19,3},{4,20},{20... | collective-permute-start | bytes 835592 | tf_op jit(solution)/shard_map/ppermute | solution.py:675
  119.4 4.6 %collective-permute-start.10 = (f32[544,128]{1,0:T(8,128)S(1)}, f32[544,128]{1,0:T(8,128)S(1)}, u32[]{:S(2)}, u32[]{:S(2)}) collective-permute-start(f32[544,128]{1,0:T(8,128)S(1)} %bitcast.20), channel_id=1, source_target_pairs={{0,16},{16,0},{1,17},{17,1},{2,18},{18,2},{3,19},{19,3},{4,20},{20... | collective-permute-start | bytes 835592 | tf_op jit(solution)/shard_map/ppermute | solution.py:682

commit v2 on v1

--- a/solution.py
+++ b/solution.py
@@ -123,7 +123,7 @@
     return (segment_at(pos, info) == before) & (pos >= 0)
 
 
-PARTS = ((0, 1, 2), (3, 4), (5, 6, 7, 8))
+PARTS = ((0,), (1, 2), (3, 4), (5, 6, 7, 8))
 
 
 def layout(*sizes):
@@ -134,17 +134,17 @@
     return starts, total
 
 
-def carry_rows(heads, kv, blocks, first):
-    past = len(blocks) - (1 if first else 0)
-    small = heads * (2 + len(blocks) + past)
-    turned = 0 if first else kv * len(blocks) * 128
+def carry_rows(heads, kv, part):
+    count = len(PARTS[part])
     wide = heads * 128
-    return layout(wide, wide, wide, wide, small, 3 * heads + 8 if first else 0, turned, turned)
-
-
-def keep_rows(heads, kv, blocks):
-    turned = kv * len(blocks) * 128
-    return layout(heads * 128, heads * 128, kv * 128, turned, turned)
+    if part == 0:
+        return layout(wide, wide, wide, 0, heads * 3, 3 * heads + 8, 0, 0)
+    turned = kv * count * 128
+    return layout(wide, wide, wide, wide, heads * (2 + 2 * count), 0, turned, turned)
+
+
+def keep_rows(heads, kv):
+    return layout(heads * 128, heads * 128, kv * 128, kv * 128, kv * 128)
 
 
 def real_rows(heads, kv):
@@ -161,7 +161,7 @@
     return pl.ds(pl.multiple_of(start + h * 128, 128), 128)
 
 
-def forward_kernel(kv, heads, blocks, first, last, *refs):
+def forward_kernel(kv, heads, part, *refs):
     refs = list(refs)
 
     def take(count):
@@ -169,29 +169,37 @@
         del refs[:count]
         return out
 
+    first, last = part == 0, part == len(PARTS) - 1
+    blocks = PARTS[part]
     queries = take(1)[0]
     sources = [take(1 if d % 2 == 0 else 2) for d in blocks]
     if first:
-        consts, carry, keep, kt, vv, bias, key32 = refs
-    elif not last:
-        origin, carry, kt, vv, bias, key32 = refs
-        before_carry, before_at = origin, carry_rows(heads, kv, PARTS[0], True)[0]
+        consts, carry, keep = take(3)
+        cum_ref, value_ref = refs[-2:]
     else:
-        origin, before_carry, keep, real, half, stats, kt, vv, bias, key32, acc = refs
-        before_at = carry_rows(heads, kv, PARTS[1], False)[0]
+        origin = take(1)[0]
+        carries = [origin] + take(part - 1)
+        before_carry = carries[-1]
+        before_at = carry_rows(heads, kv, part - 1)[0]
+    if last:
+        keep, real, half, stats = take(4)
+        acc = refs[-1]
         acc[...] = jnp.zeros_like(acc)
-    origin_at = carry_rows(heads, kv, PARTS[0], True)[0]
-    keep_at = keep_rows(heads, kv, PARTS[0])[0]
+    elif not first:
+        carry = take(1)[0]
+    kt, vv, bias, step_ref = take(4)
+    if not first:
+        key32, fade_ref = take(2)
+    origin_at = carry_rows(heads, kv, 0)[0]
+    keep_at = keep_rows(heads, kv)[0]
     real_at = real_rows(heads, kv)[0]
     half_at = half_rows(heads, kv)[0]
-    carry_at = carry_rows(heads, kv, blocks, first)[0]
+    carry_at = carry_rows(heads, kv, part)[0]
     if first:
         constant, base = consts, 0
         carry[carry_at[5] : carry_at[5] + consts.shape[0], :] = consts[...]
-        cum_ref = carry
     else:
         constant, base = origin, origin_at[5]
-        cum_ref = origin
     cum_at = origin_at[4] + heads
     group = heads // kv
     size = 3 * heads + 8
@@ -205,9 +213,6 @@
     else:
         after = before_carry[before_at[4] : before_at[4] + heads, :]
     rate = constant[base : base + heads, :]
-    own = 1 if first else 0
-    past = len(blocks) - own
-    steps, fades = [], []
     for i, d in enumerate(blocks):
         at = slice(128 * i, 128 * i + 128)
         near = sources[i]
@@ -232,41 +237,41 @@
                 out, where = (keep, keep_at[3:5]) if first else (carry, carry_at[6:8])
                 out[where[0] + row : where[0] + row + 128, :] = block
                 out[where[1] + row : where[1] + row + 128, :] = value.T
-            if d == 0:
+            if first:
                 keep[keep_at[2] + 128 * g : keep_at[2] + 128 * g + 128, :] = value
+                value_ref[g] = value
             else:
-                key32[g, :, 128 * (i - own) : 128 * (i - own) + 128] = block
+                key32[g, :, at] = block
         first_step = 2 * kv * HDIM
         parts = [piece(first_step + k * heads, first_step + (k + 1) * heads) for k in range(3)]
         step = parts[0].astype(F32) + parts[1].astype(F32) + parts[2].astype(F32)
         sums = mm(parts[0], reach) + mm(parts[1], reach) + mm(parts[2], reach)
-        steps.append(step)
-        if d == 0:
+        step_ref[i] = step
+        if first:
             carry[cum_at : cum_at + heads, :] = sums
+            cum_ref[...] = sums
             bias[:, at] = jnp.where(allowed, 0.0, NEG)
         else:
             total = jnp.broadcast_to(sums[:, 127:128], (heads, 128))
             left = jnp.maximum(total - sums, 0.0) + after
             found = match_row(info, start, before, d, heads)
-            fades.append(jnp.where(found, jnp.exp(-rate * left), 0.0))
+            fade_ref[i] = jnp.where(found, jnp.exp(-rate * left), 0.0)
             after = after + total
             both = carried & match_row(info, start, before, d, 128)
             bias[:, at] = jnp.where(both, 0.0, NEG)
     if last:
-        small, step_at, fade_at = real, real_at[4] + heads * blocks[0], real_at[5]
-        fade_at = fade_at + heads * (blocks[0] - 1)
         real[real_at[3] : real_at[3] + size, :] = origin[base : base + size, :]
-        for p, source in ((0, origin), (1, before_carry)):
-            where = carry_rows(heads, kv, PARTS[p], p == 0)[0]
+        for p, source in enumerate(carries):
+            where = carry_rows(heads, kv, p)[0]
             count = len(PARTS[p])
             low = where[4] + heads * 2
             rows = heads * count
             to = real_at[4] + heads * PARTS[p][0]
             real[to : to + rows, :] = source[low : low + rows, :]
-            low, back = low + rows, count - (1 if p == 0 else 0)
-            rows = heads * back
-            to = real_at[5] + heads * (max(PARTS[p][0], 1) - 1)
-            real[to : to + rows, :] = source[low : low + rows, :]
+            if p > 0:
+                low = low + rows
+                to = real_at[5] + heads * (PARTS[p][0] - 1)
+                real[to : to + rows, :] = source[low : low + rows, :]
             turned, where = (keep, keep_at[3:5]) if p == 0 else (source, where[6:8])
             for g in range(kv):
                 rows = 128 * count
@@ -278,14 +283,16 @@
                 real[real_at[6] + to : real_at[6] + to + rows, :] = turned[
                     where[1] + low : where[1] + low + rows, :
                 ]
+        small, step_at = real, real_at[4] + heads * blocks[0]
+        fade_at = real_at[5] + heads * (blocks[0] - 1)
     else:
         small, step_at = carry, carry_at[4] + heads * 2
         fade_at = step_at + heads * len(blocks)
         carry[carry_at[4] : carry_at[4] + heads, :] = after
-    for i, step in enumerate(steps):
-        small[step_at + heads * i : step_at + heads * (i + 1), :] = step
-    for i, fade in enumerate(fades):
-        small[fade_at + heads * i : fade_at + heads * (i + 1), :] = fade
+    for i in range(len(blocks)):
+        small[step_at + heads * i : step_at + heads * (i + 1), :] = step_ref[i]
+        if not first:
+            small[fade_at + heads * i : fade_at + heads * (i + 1), :] = fade_ref[i]
 
     def one_head(h, unused):
         g = h // group
@@ -304,43 +311,42 @@
             total = total + other
         total = jnp.broadcast_to(jnp.sum(total, axis=1, keepdims=True), (128, 128))
         mixed = mm(jnp.concatenate([w.astype(BF16) for w in weights], axis=1), vv[g])
-        weight_row = jnp.concatenate(
-            [
-                small[pl.ds(fade_at + heads * i + h, 1), :]
-                * small[pl.ds(step_at + heads * (own + i) + h, 1), :]
-                for i in range(past)
-            ],
-            axis=1,
-        )
-        state = mm_two(key32[g] * weight_row, vv[g, 128 * own :, :])
         if not first:
+            weight_row = jnp.concatenate(
+                [
+                    fade_ref[i, pl.ds(h, 1), :] * step_ref[i, pl.ds(h, 1), :]
+                    for i in range(len(blocks))
+                ],
+                axis=1,
+            )
+            state = mm_two(key32[g] * weight_row, vv[g])
             scale = jnp.exp2(old - top)
             total = total + before_carry[slab(before_at[1], h), :] * scale
             mixed = mixed + before_carry[slab(before_at[2], h), :] * scale
-            state = state + before_carry[slab(before_at[3], h), :]
+            if part > 1:
+                state = state + before_carry[slab(before_at[3], h), :]
         if not last:
             carry[slab(carry_at[0], h), :] = top
             carry[slab(carry_at[1], h), :] = total
             carry[slab(carry_at[2], h), :] = mixed
-            carry[slab(carry_at[3], h), :] = state
+            if not first:
+                carry[slab(carry_at[3], h), :] = state
         rate_h = constant[pl.ds(base + h, 1), :]
         if first:
-            cum_row = jnp.broadcast_to(cum_ref[pl.ds(cum_at + h, 1), :], (128, 128))
+            cum_row = jnp.broadcast_to(cum_ref[pl.ds(h, 1), :], (128, 128))
             cum_col = cum_row.T
             decay = jnp.where(
                 allowed, jnp.exp(-rate_h * jnp.maximum(cum_col - cum_row, 0.0)), 0.0
             )
             decayed = scores[:, :128] * decay
             keep[slab(keep_at[1], h), :] = decayed
-            skipped = (
-                constant[pl.ds(base + heads + h, 1), :] * keep[slab(keep_at[2], g), :]
-            )
-            mixing = decayed * small[pl.ds(step_at + h, 1), :]
+            skipped = constant[pl.ds(base + heads + h, 1), :] * value_ref[g]
+            mixing = decayed * step_ref[0, pl.ds(h, 1), :]
             keep[slab(keep_at[0], h), :] = mm_two(mixing, vv[g, :128, :]) + skipped
         if last:
             teach = (mixed / total).astype(BF16)
             half[slab(half_at[0], h), :] = teach
-            cum_col = jnp.broadcast_to(cum_ref[pl.ds(cum_at + h, 1), :], (128, 128)).T
+            cum_col = jnp.broadcast_to(origin[pl.ds(cum_at + h, 1), :], (128, 128)).T
             entering = jnp.where(carried, jnp.exp(-rate_h * cum_col), 0.0)
             off = mm_right(query, state) * entering
             raw = keep[slab(keep_at[0], h), :] + off
@@ -364,7 +370,6 @@
     blocks = PARTS[part]
     first, last = part == 0, part == len(PARTS) - 1
     wide = 128 * len(blocks)
-    past = len(blocks) - (1 if first else 0)
     if last:
         outs = [
             shape((real_rows(heads, kv)[1], 128)),
@@ -372,19 +377,26 @@
             shape((8, 128)),
         ]
     else:
-        outs = [shape((carry_rows(heads, kv, blocks, first)[1], 128))]
+        outs = [shape((carry_rows(heads, kv, part)[1], 128))]
     if first:
-        outs.append(shape((keep_rows(heads, kv, blocks)[1], 128)))
+        outs.append(shape((keep_rows(heads, kv)[1], 128)))
     scratch = [
         pltpu.VMEM((kv, HDIM, wide), BF16),
         pltpu.VMEM((kv, wide, HDIM), BF16),
         pltpu.VMEM((rows, wide), F32),
-        pltpu.VMEM((kv, HDIM, 128 * past), F32),
+        pltpu.VMEM((len(blocks), heads, 128), F32),
     ]
+    if first:
+        scratch += [pltpu.VMEM((heads, 128), F32), pltpu.VMEM((kv, rows, HDIM), F32)]
+    else:
+        scratch += [
+            pltpu.VMEM((kv, HDIM, wide), F32),
+            pltpu.VMEM((len(blocks), heads, 128), F32),
+        ]
     if last:
         scratch.append(pltpu.VMEM((3, rows, HDIM), F32))
     return pl.pallas_call(
-        functools.partial(forward_kernel, kv, heads, blocks, first, last),
+        functools.partial(forward_kernel, kv, heads, part),
         out_shape=outs,
         in_specs=vmem(len(operands)),
         out_specs=vmem(len(outs)),
@@ -395,14 +407,18 @@
             bytes_accessed=len(blocks) * 3 * 1024 * 1024,
             transcendentals=2 * heads * rows * wide,
         ),
-        name="forward_" + "abc"[part],
+        name="forward_" + "abcd"[part],
     )(*operands)
 
 
-def backward_kernel(kv, heads, features, row_total, *refs):
-    queries, keep, real, half, stats, student_out, grads, gain_out, small_out, *refs = refs
+def backward_kernel(kv, heads, groups, features, row_total, *refs):
+    queries, keep, real, half, *refs = refs
+    stats = refs[0][...]
+    for other in refs[1:groups]:
+        stats = stats + other[...]
+    student_out, grads, gain_out, small_out, *refs = refs[groups:]
     inv_col, coef_col, late, skip_rows, direct_rows, minus_rows, row_sums = refs
-    keep_at = keep_rows(heads, kv, PARTS[0])[0]
+    keep_at = keep_rows(heads, kv)[0]
     real_at = real_rows(heads, kv)[0]
     half_at = half_rows(heads, kv)[0]
     group = heads // kv
@@ -620,30 +636,35 @@
     hop1 = lax.ppermute(payload, "z", hop)
     hop4 = lax.ppermute(payload, "z", jump)
     sib0 = across(payload)
+    origin, keep = run(0, [queries, payload, consts])
+    hop1, origin = lax.optimization_barrier((hop1, origin))
     hop2 = lax.ppermute(hop1, "z", hop)
     sib1 = across(hop1)
-    origin, keep = run(0, [queries, payload, sib1, sib0, hop1, consts])
-    hop2, hop4, origin = lax.optimization_barrier((hop2, hop4, origin))
+    (carry1,) = run(1, [queries, sib1, sib0, hop1, origin])
+    hop2, hop4, carry1 = lax.optimization_barrier((hop2, hop4, carry1))
     hop3 = lax.ppermute(hop2, "z", hop)
     sib2, sib4 = across(hop2), across(hop4)
-    (carry,) = run(1, [queries, sib2, sib1, hop2, origin])
-    hop3, carry = lax.optimization_barrier((hop3, carry))
+    (carry2,) = run(2, [queries, sib2, sib1, hop2, origin, carry1])
+    hop3, carry2 = lax.optimization_barrier((hop3, carry2))
     sib3 = across(hop3)
     real, half, stats = run(
-        2, [queries, sib3, sib2, hop3, sib4, sib3, hop4, origin, carry, keep]
-    )
-
-    stats = lax.psum(stats, "grp")
+        3, [queries, sib3, sib2, hop3, sib4, sib3, hop4, origin, carry1, carry2, keep]
+    )
+    groups = lax.axis_size("grp")
+    all_stats = [stats] + [
+        lax.ppermute(stats, "grp", [(i, (i + k) % groups) for i in range(groups)])
+        for k in range(1, groups)
+    ]
 
     student, grads, grad_gain, small = pl.pallas_call(
-        functools.partial(backward_kernel, kv, heads, features, row_total),
+        functools.partial(backward_kernel, kv, heads, groups, features, row_total),
         out_shape=[
             shape((rows, width), BF16),
             shape((blocks, heads, 128)),
             shape((1, width)),
             shape((8, 128)),
         ],
-        in_specs=vmem(5),
+        in_specs=vmem(4 + groups),
         out_specs=vmem(4),
         scratch_shapes=[
             pltpu.VMEM((rows, 128), F32),
@@ -656,7 +677,7 @@
         ],
         compiler_params=SMALL,
         name="backward",
-    )(queries, keep, real, half, stats)
+    )(queries, keep, real, half, *all_stats)
 
     grads = lax.all_to_all(grads, ("z", "core"), 0, 0, tiled=True)
 

time: 125 us -> 116 us (0.928)
  blocking collectives: 54.8 us -> 47.3 us
  local copies, waits for them, and re-layouts: 9.51 us -> 2.85 us
  starting transfers between devices: 14.2 us -> 20.7 us
  Pallas kernels: 33.4 us -> 28.3 us
  waiting for transfers between devices: 12 us -> 16 us
    psum x1 -> x0, blocking collectives: 8.69 us -> none  [body(): stats = lax.psum(stats, 'grp')]
    ppermute x1, waiting for transfers between devices: 6.68 us -> 0.01 us  [body(): hop1 = lax.ppermute(payload, 'z', hop)]
    unnamed x20 -> x10, local copies, waits for them, and re-layouts: 9.37 us -> 2.7 us
    ppermute x1, waiting for transfers between devices: 0.01 us -> 6.42 us  [body(): hop2 = lax.ppermute(hop1, 'z', hop)]
    pallas_call x4 -> x5, Pallas kernels: 28.8 us -> 23.8 us  [the longest x4 16.4 us: forward(): pl.pallas_call(functools.partial(forward_kernel, kv, heads, part), out_sh...]
    ppermute x0 -> x3, starting transfers between devices: none -> 3.84 us  [body(): lax.ppermute(stats, 'grp', [(i, (i + k) % groups) for i in range(groups)])]
    ppermute x0 -> x3, waiting for transfers between devices: none -> 2.98 us  [body(): lax.ppermute(stats, 'grp', [(i, (i + k) % groups) for i in range(groups)])]
  transfers between devices with their start and end apart: 11 -> 14, of which waited for: 6 -> 8; matrix products, arithmetic and copies ran while one was open for 0% -> 0% of each run, Pallas kernels for 11% -> 8%
where the time goes in v2:
time: 116 us
  blocking collectives  47.3 us (41%)
  Pallas kernels  28.3 us (24%)
  starting transfers between devices  20.7 us (18%)
  waiting for transfers between devices  16 us (14%)
  local copies, waits for them, and re-layouts  2.85 us (2%)
    all_to_all x1, blocking collectives, body(): got = lax.all_to_all(half, axes, 0, 0, tiled=True)  16.6 us
    pallas_call x4, Pallas kernels, forward(): pl.pallas_call(functools.partial(forward_kernel, kv, heads, part), out_sh...  16.4 us
    all_to_all x1, blocking collectives, body(): grads = lax.all_to_all(grads, ('z', 'core'), 0, 0, tiled=True)  15.6 us
    all_to_all x1, blocking collectives, body(): mine = lax.all_to_all(spread, axes, 0, 0, tiled=True)  15 us
    pallas_call x1, Pallas kernels, body(): pl.pallas_call(functools.partial(backward_kernel, kv, heads, groups, feat...  7.37 us
    ppermute x1, waiting for transfers between devices, body(): hop2 = lax.ppermute(hop1, 'z', hop)  6.42 us
    ppermute x1, starting transfers between devices, body(): hop4 = lax.ppermute(payload, 'z', jump)  5.24 us
    ppermute x3, starting transfers between devices, body(): lax.ppermute(stats, 'grp', [(i, (i + k) % groups) for i in range(groups)])  3.84 us
  transfers between devices with their start and end apart: 14, of which 8 were waited for; matrix products, arithmetic and copies ran while one was open for 0% of the time, Pallas kernels for 8%

profile of v2, /device:TPU:1, one launch (start us, length us, event | category | flops | bytes accessed | tf_op | source)
XLA Modules:
  0.0 116.0 jit_solution(14505828200391692630)
XLA Ops:
  0.6 3.0 %prep.1 = (bf16[560,128]{1,0:T(8,128)(2,1)}, f32[16,128]{1,0:T(8,128)}, f32[56,128]{1,0:T(8,128)}) custom-call(s32[1,4]{1,0:T(1,128)} %lengths.1, f32[16]{0:T(128)} %bias.1, f32[16]{0:T(128)} %decay.1, f32[16]{0:T(128)} %skip.1, f32[1,2048]{1,0:T(1,128)} %bitcast.27, bf16[128,8192]{1,0:T(8,128)(2,1)} %bitcast.14, bf16[16,8192]{1,0:T(8,128)(2,1)} %bitcast.24, ...), custom_call_target="tpu_custom_call" | custom-call | tf_op jit(solution)/shard_map/prep/pallas_call | solution.py:611
  3.6 2.5 %collective-permute-start = (bf16[560,128]{1,0:T(8,128)(2,1)}, bf16[560,128]{1,0:T(8,128)(2,1)S(1)}, u32[]{:S(2)}, u32[]{:S(2)}) collective-permute-start(bf16[560,128]{1,0:T(8,128)(2,1)} %get-tuple-element.32.refs_1_), channel_id=1, source_target_pairs={{0,32},{32,64},{64,96},{96,128},{128,160},{160,192},{192,224},{224... | collective-permute-start | bytes 430088 | tf_op jit(solution)/shard_map/ppermute | solution.py:636
  6.1 1.0 collective-permute-start.4
  7.0 0.0 copy-start.1
  7.0 1.0 copy-done.1
  8.1 0.0 copy-start.3
  8.1 0.9 copy-done.3
  9.0 0.0 copy-start.4
  9.0 0.7 copy-done.4
  9.7 4.2 %forward_a.1 = (f32[6400,128]{1,0:T(8,128)S(1)}, f32[4864,128]{1,0:T(8,128)S(1)}) custom-call(bf16[128,2048]{1,0:T(8,128)(2,1)S(1)} %bitcast.16, bf16[560,128]{1,0:T(8,128)(2,1)S(1)} %copy-done.3, f32[56,128]{1,0:T(8,128)S(1)} %copy-done.4), custom_call_target="tpu_custom_call" | custom-call | flops 402653184 | bytes 3145728 | tf_op jit(solution)/shard_map/forward_a/pallas_call | solution.py:398
  14.0 0.0 collective-permute-done.refs_3_
  14.0 1.0 collective-permute-start.3
  14.9 5.2 %collective-permute-start.2 = (bf16[560,128]{1,0:T(8,128)(2,1)}, bf16[560,128]{1,0:T(8,128)(2,1)S(1)}, u32[]{:S(2)}, u32[]{:S(2)}) collective-permute-start(bf16[560,128]{1,0:T(8,128)(2,1)} %get-tuple-element.32.refs_1_), channel_id=1, source_target_pairs={{0,128},{32,160},{64,192},{96,224},{128,0},{160,32},{192,64},{224,... | collective-permute-start | bytes 430088 | tf_op jit(solution)/shard_map/ppermute | solution.py:637
  20.2 0.7 collective-permute-start.1
  20.9 0.0 collective-permute-done.4.refs_2_
  20.9 0.0 collective-permute-done.3.refs_1_.refs_2_
  20.9 2.8 %forward_b.1.refs_5_.refs_8_ = f32[9344,128]{1,0:T(8,128)S(1)} custom-call(bf16[128,2048]{1,0:T(8,128)(2,1)S(1)} %bitcast.17, bf16[560,128]{1,0:T(8,128)(2,1)S(1)} %collective-permute-done.3.refs_1_.refs_2_, bf16[560,128]{1,0:T(8,128)(2,1)S(1)} %collective-permute-done.4.refs_2_, bf16[560,128]{1,0:T(8,128)(2,1)S(1)} %collective-permute-done.refs_3_, ...), custom_call_target="tpu_custom_call" | custom-call | flops 805306368 | bytes 6291456 | tf_op jit(solution)/shard_map/forward_b/pallas_call | solution.py:398
  23.7 0.8 collective-permute-done.2.refs_6_
  24.5 6.4 %collective-permute-done.1.refs_3_ = bf16[560,128]{1,0:T(8,128)(2,1)S(1)} collective-permute-done((bf16[560,128]{1,0:T(8,128)(2,1)S(1)}, bf16[560,128]{1,0:T(8,128)(2,1)S(1)}, u32[]{:S(2)}, u32[]{:S(2)}) %collective-permute-start.1) | collective-permute-done | bytes 143392 | tf_op jit(solution)/shard_map/ppermute | solution.py:641
  30.9 0.5 collective-permute-start.6
  31.4 1.4 %collective-permute-start.5 = (bf16[560,128]{1,0:T(8,128)(2,1)S(1)}, bf16[560,128]{1,0:T(8,128)(2,1)S(1)}, u32[]{:S(2)}, u32[]{:S(2)}) collective-permute-start(bf16[560,128]{1,0:T(8,128)(2,1)S(1)} %collective-permute-done.1.refs_3_), channel_id=1, source_target_pairs={{0,32},{32,64},{64,96},{96,128},{128,160},{160,192},{192,224},{224... | collective-permute-start | bytes 430088 | tf_op jit(solution)/shard_map/ppermute | solution.py:645
  32.8 0.3 collective-permute-start.8
  33.0 0.0 collective-permute-done.6.refs_1_.refs_2_
  33.0 2.9 %forward_c.1.refs_9_ = f32[9344,128]{1,0:T(8,128)S(1)} custom-call(bf16[128,2048]{1,0:T(8,128)(2,1)S(1)} %bitcast.18, bf16[560,128]{1,0:T(8,128)(2,1)S(1)} %collective-permute-done.6.refs_1_.refs_2_, bf16[560,128]{1,0:T(8,128)(2,1)S(1)} %collective-permute-done.3.refs_1_.refs_2_, bf16[560,128]{1,0:T(8,128)(2,1)S(1)} %collective-permute-done.1.refs_3_, ...), custom_call_target="tpu_custom_call" | custom-call | flops 805306368 | bytes 6291456 | tf_op jit(solution)/shard_map/forward_c/pallas_call | solution.py:398
  35.9 2.1 %collective-permute-done.5.refs_3_ = bf16[560,128]{1,0:T(8,128)(2,1)S(1)} collective-permute-done((bf16[560,128]{1,0:T(8,128)(2,1)S(1)}, bf16[560,128]{1,0:T(8,128)(2,1)S(1)}, u32[]{:S(2)}, u32[]{:S(2)}) %collective-permute-start.5) | collective-permute-done | bytes 143392 | tf_op jit(solution)/shard_map/ppermute | solution.py:645
  38.0 0.8 collective-permute-start.7
  38.8 0.0 collective-permute-done.8.refs_4_
  38.8 1.0 collective-permute-done.7.refs_1_.refs_5_
  39.8 6.6 %forward_d.1 = (f32[8960,128]{1,0:T(8,128)S(1)}, bf16[4352,128]{1,0:T(8,128)(2,1)S(1)}, f32[8,128]{1,0:T(8,128)S(1)}) custom-call(bf16[128,2048]{1,0:T(8,128)(2,1)S(1)} %bitcast.19, bf16[560,128]{1,0:T(8,128)(2,1)S(1)} %collective-permute-done.7.refs_1_.refs_5_, bf16[560,128]{1,0:T(8,128)(2,1)S(1)} %collective-permute-done.6.refs_1_.refs_2_, ...), custom_call_target="tpu_custom_call" | custom-call | flops 1610612736 | bytes 12582912 | tf_op jit(solution)/shard_map/forward_d/pallas_call | solution.py:398
  46.4 2.8 %collective-permute-start.11 = (f32[8,128]{1,0:T(8,128)S(1)}, f32[8,128]{1,0:T(8,128)S(1)}, u32[]{:S(2)}, u32[]{:S(2)}) collective-permute-start(f32[8,128]{1,0:T(8,128)S(1)} %get-tuple-element.45.refs_4_), channel_id=1, source_target_pairs={{0,12},{4,0},{8,4},{12,8},{1,13},{5,1},{9,5},{13,9},{2,14},{6,2},{... | collective-permute-start | bytes 12296 | tf_op jit(solution)/shard_map/ppermute | solution.py:655
  49.2 0.4 collective-permute-start.10
  49.5 0.7 collective-permute-start.9
  50.2 0.0 collective-permute-done.11.refs_7_
  50.2 2.9 %collective-permute-done.10.refs_6_ = f32[8,128]{1,0:T(8,128)S(1)} collective-permute-done((f32[8,128]{1,0:T(8,128)S(1)}, f32[8,128]{1,0:T(8,128)S(1)}, u32[]{:S(2)}, u32[]{:S(2)}) %collective-permute-start.10) | collective-permute-done | bytes 4128 | tf_op jit(solution)/shard_map/ppermute | solution.py:655
  53.1 0.1 collective-permute-done.9.refs_5_
  53.2 0.0 copy-start
  53.2 0.0 copy-start.2
  53.2 7.4 %backward.1 = (bf16[128,2048]{1,0:T(8,128)(2,1)}, f32[16,16,128]{2,1,0:T(8,128)S(1)}, f32[1,2048]{1,0:T(1,128)S(1)}, f32[8,128]{1,0:T(8,128)S(1)}) custom-call(bf16[128,2048]{1,0:T(8,128)(2,1)S(1)} %bitcast.20, f32[4864,128]{1,0:T(8,128)S(1)} %get-tuple-element.34.refs_10_.refs_1_, f32[8960,128]{1,0:T(8,128)S(1)} %get-tuple-element.43.refs_2_, ...), custom_call_target="tpu_custom_call" | custom-call | tf_op jit(solution)/shard_map/backward/pallas_call | solution.py:659
  60.6 15.6 %all_to_all.15.grads = f32[16,16,128]{2,1,0:T(8,128)S(1)} all-to-all(f32[16,16,128]{2,1,0:T(8,128)S(1)} %get-tuple-element.50), channel_id=1, replica_groups=mesh['z'=8,'core'=2,'grp'=4,'dp'=4] {'z','core'}, dimensions={0} | all-to-all | bytes 262144 | tf_op jit(solution)/shard_map/all_to_all | solution.py:682
  76.2 0.0 copy-done
  76.2 0.0 copy-done.2
  76.2 0.7 weights.1
  76.8 0.1 collective-permute-start.12
  76.9 1.5 %collective-permute-done.12 = f32[544,128]{1,0:T(8,128)S(1)} collective-permute-done((f32[544,128]{1,0:T(8,128)S(1)}, f32[544,128]{1,0:T(8,128)S(1)}, u32[]{:S(2)}, u32[]{:S(2)}) %collective-permute-start.12) | collective-permute-done | bytes 278560 | tf_op jit(solution)/shard_map/ppermute | solution.py:696
  78.5 16.6 %all_to_all.16 = f32[32,17,1,128]{3,2,1,0:T(1,128)S(1)} all-to-all(f32[32,17,1,128]{3,2,1,0:T(1,128)S(1)} %bitcast.23), channel_id=1, replica_groups=mesh['z'=8,'core'=2,'grp'=4,'dp'=4] {'z','dp'}, dimensions={0} | all-to-all | bytes 557056 | tf_op jit(solution)/shard_map/all_to_all | solution.py:698
  95.1 0.2 reduce_sum.9
  95.3 0.1 broadcast_in_dim.14
  95.5 15.0 %all_to_all.17 = f32[32,17,1,128]{3,2,1,0:T(1,128)S(1)} all-to-all(f32[32,17,1,128]{3,2,1,0:T(1,128)S(1)} %broadcast_in_dim.14), channel_id=1, replica_groups=mesh['z'=8,'core'=2,'grp'=4,'dp'=4] {'z','dp'}, dimensions={0} | all-to-all | bytes 557056 | tf_op jit(solution)/shard_map/all_to_all | solution.py:701
  110.5 3.5 %collective-permute-start.13 = (f32[544,128]{1,0:T(8,128)S(1)}, f32[544,128]{1,0:T(8,128)S(1)}, u32[]{:S(2)}, u32[]{:S(2)}) collective-permute-start(f32[544,128]{1,0:T(8,128)S(1)} %bitcast.21), channel_id=1, source_target_pairs={{0,16},{16,0},{1,17},{17,1},{2,18},{18,2},{3,19},{19,3},{4,20},{20... | collective-permute-start | bytes 835592 | tf_op jit(solution)/shard_map/ppermute | solution.py:703
  113.9 1.2 %collective-permute-done.13.other = f32[544,128]{1,0:T(8,128)S(1)} collective-permute-done((f32[544,128]{1,0:T(8,128)S(1)}, f32[544,128]{1,0:T(8,128)S(1)}, u32[]{:S(2)}, u32[]{:S(2)}) %collective-permute-start.13) | collective-permute-done | bytes 278560 | tf_op jit(solution)/shard_map/ppermute | solution.py:703
  115.1 0.8 finish.1
  (1 shorter events, 0.0 us)
Async XLA Ops:
  3.6 10.4 %collective-permute-start = (bf16[560,128]{1,0:T(8,128)(2,1)}, bf16[560,128]{1,0:T(8,128)(2,1)S(1)}, u32[]{:S(2)}, u32[]{:S(2)}) collective-permute-start(bf16[560,128]{1,0:T(8,128)(2,1)} %get-tuple-element.32.refs_1_), channel_id=1, source_target_pairs={{0,32},{32,64},{64,96},{96,128},{128,160},{160,192},{192,224},{224... | collective-permute-start | bytes 430088 | tf_op jit(solution)/shard_map/ppermute | solution.py:636
  6.1 14.8 %collective-permute-start.4 = (bf16[560,128]{1,0:T(8,128)(2,1)}, bf16[560,128]{1,0:T(8,128)(2,1)S(1)}, u32[]{:S(2)}, u32[]{:S(2)}) collective-permute-start(bf16[560,128]{1,0:T(8,128)(2,1)} %get-tuple-element.32.refs_1_), channel_id=1, source_target_pairs={{0,16},{16,0},{1,17},{17,1},{2,18},{18,2},{3,19},{19,3},{4,20},{20... | collective-permute-start | bytes 430088 | tf_op jit(solution)/shard_map/ppermute | solution.py:634
  7.0 1.0 copy-start.1
  8.1 0.9 copy-start.3
  9.0 0.7 copy-start.4
  14.0 6.9 %collective-permute-start.3 = (bf16[560,128]{1,0:T(8,128)(2,1)S(1)}, bf16[560,128]{1,0:T(8,128)(2,1)S(1)}, u32[]{:S(2)}, u32[]{:S(2)}) collective-permute-start(bf16[560,128]{1,0:T(8,128)(2,1)S(1)} %collective-permute-done.refs_3_), channel_id=1, source_target_pairs={{0,16},{16,0},{1,17},{17,1},{2,18},{18,2},{3,19},{19,3},{4,20},{20... | collective-permute-start | bytes 430088 | tf_op jit(solution)/shard_map/ppermute | solution.py:634
  14.9 9.5 %collective-permute-start.2 = (bf16[560,128]{1,0:T(8,128)(2,1)}, bf16[560,128]{1,0:T(8,128)(2,1)S(1)}, u32[]{:S(2)}, u32[]{:S(2)}) collective-permute-start(bf16[560,128]{1,0:T(8,128)(2,1)} %get-tuple-element.32.refs_1_), channel_id=1, source_target_pairs={{0,128},{32,160},{64,192},{96,224},{128,0},{160,32},{192,64},{224,... | collective-permute-start | bytes 430088 | tf_op jit(solution)/shard_map/ppermute | solution.py:637
  20.2 10.7 %collective-permute-start.1 = (bf16[560,128]{1,0:T(8,128)(2,1)S(1)}, bf16[560,128]{1,0:T(8,128)(2,1)S(1)}, u32[]{:S(2)}, u32[]{:S(2)}) collective-permute-start(bf16[560,128]{1,0:T(8,128)(2,1)S(1)} %collective-permute-done.refs_3_), channel_id=1, source_target_pairs={{0,32},{32,64},{64,96},{96,128},{128,160},{160,192},{192,224},{224... | collective-permute-start | bytes 430088 | tf_op jit(solution)/shard_map/ppermute | solution.py:641
  30.9 2.2 %collective-permute-start.6 = (bf16[560,128]{1,0:T(8,128)(2,1)S(1)}, bf16[560,128]{1,0:T(8,128)(2,1)S(1)}, u32[]{:S(2)}, u32[]{:S(2)}) collective-permute-start(bf16[560,128]{1,0:T(8,128)(2,1)S(1)} %collective-permute-done.1.refs_3_), channel_id=1, source_target_pairs={{0,16},{16,0},{1,17},{17,1},{2,18},{18,2},{3,19},{19,3},{4,20},{20... | collective-permute-start | bytes 430088 | tf_op jit(solution)/shard_map/ppermute | solution.py:634
  31.4 6.6 %collective-permute-start.5 = (bf16[560,128]{1,0:T(8,128)(2,1)S(1)}, bf16[560,128]{1,0:T(8,128)(2,1)S(1)}, u32[]{:S(2)}, u32[]{:S(2)}) collective-permute-start(bf16[560,128]{1,0:T(8,128)(2,1)S(1)} %collective-permute-done.1.refs_3_), channel_id=1, source_target_pairs={{0,32},{32,64},{64,96},{96,128},{128,160},{160,192},{192,224},{224... | collective-permute-start | bytes 430088 | tf_op jit(solution)/shard_map/ppermute | solution.py:645
  32.8 6.0 %collective-permute-start.8 = (bf16[560,128]{1,0:T(8,128)(2,1)S(1)}, bf16[560,128]{1,0:T(8,128)(2,1)S(1)}, u32[]{:S(2)}, u32[]{:S(2)}) collective-permute-start(bf16[560,128]{1,0:T(8,128)(2,1)S(1)} %collective-permute-done.2.refs_6_), channel_id=1, source_target_pairs={{0,16},{16,0},{1,17},{17,1},{2,18},{18,2},{3,19},{19,3},{4,20},{20... | collective-permute-start | bytes 430088 | tf_op jit(solution)/shard_map/ppermute | solution.py:634
  38.0 1.8 %collective-permute-start.7 = (bf16[560,128]{1,0:T(8,128)(2,1)S(1)}, bf16[560,128]{1,0:T(8,128)(2,1)S(1)}, u32[]{:S(2)}, u32[]{:S(2)}) collective-permute-start(bf16[560,128]{1,0:T(8,128)(2,1)S(1)} %collective-permute-done.5.refs_3_), channel_id=1, source_target_pairs={{0,16},{16,0},{1,17},{17,1},{2,18},{18,2},{3,19},{19,3},{4,20},{20... | collective-permute-start | bytes 430088 | tf_op jit(solution)/shard_map/ppermute | solution.py:634
  46.4 3.8 %collective-permute-start.11 = (f32[8,128]{1,0:T(8,128)S(1)}, f32[8,128]{1,0:T(8,128)S(1)}, u32[]{:S(2)}, u32[]{:S(2)}) collective-permute-start(f32[8,128]{1,0:T(8,128)S(1)} %get-tuple-element.45.refs_4_), channel_id=1, source_target_pairs={{0,12},{4,0},{8,4},{12,8},{1,13},{5,1},{9,5},{13,9},{2,14},{6,2},{... | collective-permute-start | bytes 12296 | tf_op jit(solution)/shard_map/ppermute | solution.py:655
  49.2 4.0 %collective-permute-start.10 = (f32[8,128]{1,0:T(8,128)S(1)}, f32[8,128]{1,0:T(8,128)S(1)}, u32[]{:S(2)}, u32[]{:S(2)}) collective-permute-start(f32[8,128]{1,0:T(8,128)S(1)} %get-tuple-element.45.refs_4_), channel_id=1, source_target_pairs={{0,8},{4,12},{8,0},{12,4},{1,9},{5,13},{9,1},{13,5},{2,10},{6,14},... | collective-permute-start | bytes 12296 | tf_op jit(solution)/shard_map/ppermute | solution.py:655
  49.5 3.7 %collective-permute-start.9 = (f32[8,128]{1,0:T(8,128)S(1)}, f32[8,128]{1,0:T(8,128)S(1)}, u32[]{:S(2)}, u32[]{:S(2)}) collective-permute-start(f32[8,128]{1,0:T(8,128)S(1)} %get-tuple-element.45.refs_4_), channel_id=1, source_target_pairs={{0,4},{4,8},{8,12},{12,0},{1,5},{5,9},{9,13},{13,1},{2,6},{6,10},{... | collective-permute-start | bytes 12296 | tf_op jit(solution)/shard_map/ppermute | solution.py:655
  53.2 23.0 %copy-start = (bf16[1,128,8192]{2,1,0:T(8,128)(2,1)S(1)}, bf16[1,128,8192]{2,1,0:T(8,128)(2,1)}, u32[]{:S(2)}) copy-start(bf16[1,128,8192]{2,1,0:T(8,128)(2,1)} %param.10) | copy-start | bytes 6291460
  53.2 23.0 %copy-start.2 = (f32[16,128]{1,0:T(8,128)S(1)}, f32[16,128]{1,0:T(8,128)}, u32[]{:S(2)}) copy-start(f32[16,128]{1,0:T(8,128)} %get-tuple-element.47.slope) | copy-start | bytes 24580
  76.8 1.6 %collective-permute-start.12 = (f32[544,128]{1,0:T(8,128)S(1)}, f32[544,128]{1,0:T(8,128)S(1)}, u32[]{:S(2)}, u32[]{:S(2)}) collective-permute-start(f32[544,128]{1,0:T(8,128)S(1)} %get-tuple-element.52), channel_id=1, source_target_pairs={{0,16},{16,0},{1,17},{17,1},{2,18},{18,2},{3,19},{19,3},{4,20},{20... | collective-permute-start | bytes 835592 | tf_op jit(solution)/shard_map/ppermute | solution.py:696
  110.5 4.6 %collective-permute-start.13 = (f32[544,128]{1,0:T(8,128)S(1)}, f32[544,128]{1,0:T(8,128)S(1)}, u32[]{:S(2)}, u32[]{:S(2)}) collective-permute-start(f32[544,128]{1,0:T(8,128)S(1)} %bitcast.21), channel_id=1, source_target_pairs={{0,16},{16,0},{1,17},{17,1},{2,18},{18,2},{3,19},{19,3},{4,20},{20... | collective-permute-start | bytes 835592 | tf_op jit(solution)/shard_map/ppermute | solution.py:703

commit v3 on v2

--- a/solution.py
+++ b/solution.py
@@ -71,13 +71,28 @@
 
 
 def prep_kernel(
-    kv, lengths, bias, decay, skip, gain, hidden, weight, keys, values, payload, slope, consts
+    kv,
+    lengths,
+    bias,
+    decay,
+    skip,
+    gain,
+    hidden,
+    weight,
+    keys,
+    values,
+    queries,
+    payload,
+    slope,
+    local,
+    consts,
 ):
+    heads = weight.shape[0]
     pre = (
         lax.dot_general(
-            weight[...], hidden[...], (((1,), (1,)), ((), ())), preferred_element_type=F32
-        )
-        + column_of(bias, weight.shape[0])
+            hidden[...], weight[...], (((1,), (1,)), ((), ())), preferred_element_type=F32
+        ).T
+        + column_of(bias, heads)
     )
     step = jnp.maximum(pre, 0.0) + jnp.log1p(jnp.exp(-jnp.abs(pre)))
     slope[...] = 1.0 / (1.0 + jnp.exp(-pre))
@@ -85,7 +100,6 @@
         cols = slice(g * HDIM, (g + 1) * HDIM)
         payload[g * HDIM : (g + 1) * HDIM, :] = keys[:, cols].astype(F32).T.astype(BF16)
         payload[(kv + g) * HDIM : (kv + g + 1) * HDIM, :] = values[:, cols]
-    heads = step.shape[0]
     consts[0:heads, :] = jnp.exp(column_of(decay, heads))
     consts[heads : 2 * heads, :] = column_of(skip, heads)
     for h in range(heads):
@@ -97,12 +111,22 @@
     marks = jnp.zeros((8, 128), jnp.int32)
     for i in range(3):
         marks = jnp.where(row == i, starts[i], marks)
-    consts[3 * heads :, :] = marks.astype(F32)
+    consts[3 * heads : 3 * heads + 8, :] = marks.astype(F32)
+    consts[3 * heads + 8 :, :] = jnp.zeros((consts.shape[0] - 3 * heads - 8, 128), F32)
     first = 2 * kv * HDIM
     for part in range(3):
         piece = step.astype(BF16)
         payload[first + part * heads : first + (part + 1) * heads, :] = piece
         step = step - piece.astype(F32)
+    at = local_rows(heads, kv)[0]
+    for h in range(heads):
+        local[at[0] + 128 * h : at[0] + 128 * h + 128, :] = queries[:, 128 * h : 128 * h + 128]
+    local[at[1] : at[1] + payload.shape[0], :] = payload[...]
+    rest = consts[...]
+    for part in range(3):
+        piece = rest.astype(BF16)
+        local[at[2 + part] : at[2 + part] + rest.shape[0], :] = piece
+        rest = rest - piece.astype(F32)
 
 
 def masks(info):
@@ -123,7 +147,7 @@
     return (segment_at(pos, info) == before) & (pos >= 0)
 
 
-PARTS = ((0,), (1, 2), (3, 4), (5, 6, 7, 8))
+PARTS = ((0,), (1, 2), (3, 4), (5, 6), (7, 8))
 
 
 def layout(*sizes):
@@ -138,9 +162,23 @@
     count = len(PARTS[part])
     wide = heads * 128
     if part == 0:
-        return layout(wide, wide, wide, 0, heads * 3, 3 * heads + 8, 0, 0)
+        return layout(wide, wide, wide, 0, heads * 3, const_rows(heads), 0, 0)
     turned = kv * count * 128
     return layout(wide, wide, wide, wide, heads * (2 + 2 * count), 0, turned, turned)
+
+
+def const_rows(heads):
+    return -(-(3 * heads + 8) // 16) * 16
+
+
+def local_rows(heads, kv):
+    size = const_rows(heads)
+    cargo = 2 * kv * HDIM + 3 * heads
+    starts, total = [], 0
+    for rows in (heads * 128, cargo, size, size, size):
+        starts.append(total)
+        total += rows
+    return starts, total
 
 
 def keep_rows(heads, kv):
@@ -150,7 +188,9 @@
 def real_rows(heads, kv):
     count = BACK + 1
     wide = heads * 128
-    return layout(wide, wide, wide, 3 * heads + 8, count * heads, BACK * heads, kv * count * 128)
+    return layout(
+        wide, wide, wide, const_rows(heads), count * heads, BACK * heads, kv * count * 128
+    )
 
 
 def half_rows(heads, kv):
@@ -171,12 +211,18 @@
 
     first, last = part == 0, part == len(PARTS) - 1
     blocks = PARTS[part]
-    queries = take(1)[0]
-    sources = [take(1 if d % 2 == 0 else 2) for d in blocks]
+    local = take(1)[0]
+    local_at = local_rows(heads, kv)[0]
     if first:
-        consts, carry, keep = take(3)
-        cum_ref, value_ref = refs[-2:]
+        sources = [[local]]
+        carry, keep = take(2)
+        cum_ref, value_ref, consts = refs[-3:]
+        total = jnp.zeros(consts.shape, F32)
+        for i in range(3):
+            total += local[local_at[2 + i] : local_at[2 + i] + consts.shape[0], :].astype(F32)
+        consts[...] = total
     else:
+        sources = [take(1 if d % 2 == 0 else 2) for d in blocks]
         origin = take(1)[0]
         carries = [origin] + take(part - 1)
         before_carry = carries[-1]
@@ -203,7 +249,7 @@
     cum_at = origin_at[4] + heads
     group = heads // kv
     size = 3 * heads + 8
-    info = place_of(constant[base + size - 8 : base + size, :], queries.shape[0])
+    info = place_of(constant[base + size - 8 : base + size, :], 128)
     even_core = info[4] == 0
     start, before, allowed, carried = masks(info)
 
@@ -218,6 +264,8 @@
         near = sources[i]
 
         def piece(low, high):
+            if first:
+                return near[0][local_at[1] + low : local_at[1] + high, :]
             if d % 2 == 0:
                 return near[0][low:high, :]
             return jnp.where(even_core, near[0][low:high, :], near[1][low:high, :])
@@ -296,7 +344,7 @@
 
     def one_head(h, unused):
         g = h // group
-        query = queries[:, slab(0, h)]
+        query = local[slab(local_at[0], h), :]
         scores = mm(query, kt[g])
         scaled = scores * (LOG2E / math.sqrt(HDIM)) + bias[...]
         top = jnp.broadcast_to(jnp.max(scaled, axis=1, keepdims=True), (128, 128))
@@ -387,7 +435,11 @@
         pltpu.VMEM((len(blocks), heads, 128), F32),
     ]
     if first:
-        scratch += [pltpu.VMEM((heads, 128), F32), pltpu.VMEM((kv, rows, HDIM), F32)]
+        scratch += [
+            pltpu.VMEM((heads, 128), F32),
+            pltpu.VMEM((kv, rows, HDIM), F32),
+            pltpu.VMEM((const_rows(heads), 128), F32),
+        ]
     else:
         scratch += [
             pltpu.VMEM((kv, HDIM, wide), F32),
@@ -407,12 +459,12 @@
             bytes_accessed=len(blocks) * 3 * 1024 * 1024,
             transcendentals=2 * heads * rows * wide,
         ),
-        name="forward_" + "abcd"[part],
+        name="forward_" + "abcde"[part],
     )(*operands)
 
 
 def backward_kernel(kv, heads, groups, features, row_total, *refs):
-    queries, keep, real, half, *refs = refs
+    local, keep, real, half, *refs = refs
     stats = refs[0][...]
     for other in refs[1:groups]:
         stats = stats + other[...]
@@ -424,7 +476,7 @@
     group = heads // kv
     size = 3 * heads + 8
     base = real_at[3]
-    info = place_of(real[base + size - 8 : base + size, :], queries.shape[0])
+    info = place_of(real[base + size - 8 : base + size, :], 128)
     place, count = info[5], grads.shape[0]
     grads[...] = jnp.zeros_like(grads)
     row_sums[...] = jnp.zeros_like(row_sums)
@@ -442,7 +494,7 @@
     def one_head(h, unused):
         g = h // group
         cols = slab(0, h)
-        query = queries[:, cols]
+        query = local[slab(0, h), :]
         raw, off = real[slab(real_at[0], h), :], real[slab(real_at[1], h), :]
         scale = real[pl.ds(base + 2 * heads + h, 1), :]
         inv = inv_col[...]
@@ -608,47 +660,48 @@
     gain = norm_gain[None, :]
     cargo = 2 * kv * HDIM + 3 * heads
 
-    payload, slope, consts = pl.pallas_call(
+    payload, slope, local = pl.pallas_call(
         functools.partial(prep_kernel, kv),
         out_shape=[
             shape((cargo, 128), BF16),
             shape((heads, 128)),
-            shape((3 * heads + 8, 128)),
+            shape((local_rows(heads, kv)[1], 128), BF16),
         ],
-        in_specs=smem(4) + vmem(5),
+        in_specs=smem(4) + vmem(6),
         out_specs=vmem(3),
+        scratch_shapes=[pltpu.VMEM((const_rows(heads), 128), F32)],
         compiler_params=LARGE,
         name="prep",
     )(
         doc_lengths, dt_bias, decay_log, skip_gain, gain, hidden, dt_weight.T,
-        teacher_keys[0], teacher_values[0],
+        teacher_keys[0], teacher_values[0], teacher_queries[0],
     )
 
     swap = [(0, 1), (1, 0)]
     hop = [(i, (i + 1) % chips) for i in range(chips)]
-    jump = [(i, (i + 4) % chips) for i in range(chips)]
-    queries = teacher_queries[0]
     run = functools.partial(forward, kv, heads, rows)
 
     def across(part):
         return lax.ppermute(part, "core", swap)
 
     hop1 = lax.ppermute(payload, "z", hop)
-    hop4 = lax.ppermute(payload, "z", jump)
     sib0 = across(payload)
-    origin, keep = run(0, [queries, payload, consts])
-    hop1, origin = lax.optimization_barrier((hop1, origin))
     hop2 = lax.ppermute(hop1, "z", hop)
     sib1 = across(hop1)
-    (carry1,) = run(1, [queries, sib1, sib0, hop1, origin])
-    hop2, hop4, carry1 = lax.optimization_barrier((hop2, hop4, carry1))
+    origin, keep = run(0, [local])
+    hop2, origin = lax.optimization_barrier((hop2, origin))
     hop3 = lax.ppermute(hop2, "z", hop)
-    sib2, sib4 = across(hop2), across(hop4)
-    (carry2,) = run(2, [queries, sib2, sib1, hop2, origin, carry1])
-    hop3, carry2 = lax.optimization_barrier((hop3, carry2))
+    sib2 = across(hop2)
+    (carry1,) = run(1, [local, sib1, sib0, hop1, origin])
+    hop3, carry1 = lax.optimization_barrier((hop3, carry1))
+    hop4 = lax.ppermute(hop3, "z", hop)
     sib3 = across(hop3)
+    (carry2,) = run(2, [local, sib2, sib1, hop2, origin, carry1])
+    hop4, carry2 = lax.optimization_barrier((hop4, carry2))
+    sib4 = across(hop4)
+    (carry3,) = run(3, [local, sib3, sib2, hop3, origin, carry1, carry2])
     real, half, stats = run(
-        3, [queries, sib3, sib2, hop3, sib4, sib3, hop4, origin, carry1, carry2, keep]
+        4, [local, sib4, sib3, hop4, origin, carry1, carry2, carry3, keep]
     )
     groups = lax.axis_size("grp")
     all_stats = [stats] + [
@@ -677,7 +730,7 @@
         ],
         compiler_params=SMALL,
         name="backward",
-    )(queries, keep, real, half, *all_stats)
+    )(local, keep, real, half, *all_stats)
 
     grads = lax.all_to_all(grads, ("z", "core"), 0, 0, tiled=True)
 

time: 116 us -> 113 us (0.974)
  starting transfers between devices: 20.7 us -> 16.1 us
  Pallas kernels: 28.3 us -> 30.3 us
  local copies, waits for them, and re-layouts: 2.85 us -> 1.26 us
    ppermute x1, waiting for transfers between devices: 0.01 us -> 7.63 us  [body(): hop1 = lax.ppermute(payload, 'z', hop)]
    ppermute x1, waiting for transfers between devices: 6.42 us -> 0.01 us  [body(): hop2 = lax.ppermute(hop1, 'z', hop)]
    ppermute x1, starting transfers between devices: 5.24 us -> 0.01 us  [body(): hop4 = lax.ppermute(hop3, 'z', hop)]
    ppermute x5, starting transfers between devices: 3.49 us -> 6.14 us  [across(): return lax.ppermute(part, 'core', swap)]
    unnamed x10 -> x6, local copies, waits for them, and re-layouts: 2.7 us -> 1.12 us
    pallas_call x4 -> x5, Pallas kernels: 16.4 us -> 17.9 us  [forward(): pl.pallas_call(functools.partial(forward_kernel, kv, heads, part), out_sh...]
    ppermute x1, starting transfers between devices: 1.38 us -> 0.08 us  [body(): hop3 = lax.ppermute(hop2, 'z', hop)]
  transfers between devices with their start and end apart: 14 -> 14, of which waited for: 8 -> 7; matrix products, arithmetic and copies ran while one was open for 0% -> 0% of each run, Pallas kernels for 8% -> 11%
where the time goes in v3:
time: 113 us
  blocking collectives  47.9 us (42%)
  Pallas kernels  30.3 us (27%)
  waiting for transfers between devices  16.7 us (15%)
  starting transfers between devices  16.1 us (14%)
  local copies, waits for them, and re-layouts  1.26 us (1%)
    pallas_call x5, Pallas kernels, forward(): pl.pallas_call(functools.partial(forward_kernel, kv, heads, part), out_sh...  17.9 us
    all_to_all x1, blocking collectives, body(): got = lax.all_to_all(half, axes, 0, 0, tiled=True)  16.6 us
    all_to_all x1, blocking collectives, body(): grads = lax.all_to_all(grads, ('z', 'core'), 0, 0, tiled=True)  16.2 us
    all_to_all x1, blocking collectives, body(): mine = lax.all_to_all(spread, axes, 0, 0, tiled=True)  15 us
    ppermute x1, waiting for transfers between devices, body(): hop1 = lax.ppermute(payload, 'z', hop)  7.63 us
    pallas_call x1, Pallas kernels, body(): pl.pallas_call(functools.partial(backward_kernel, kv, heads, groups, feat...  7.27 us
    ppermute x5, starting transfers between devices, across(): return lax.ppermute(part, 'core', swap)  6.14 us
    ppermute x3, starting transfers between devices, body(): lax.ppermute(stats, 'grp', [(i, (i + k) % groups) for i in range(groups)])  3.85 us
  transfers between devices with their start and end apart: 14, of which 7 were waited for; matrix products, arithmetic and copies ran while one was open for 0% of the time, Pallas kernels for 11%

profile of v3, /device:TPU:1, one launch (start us, length us, event | category | flops | bytes accessed | tf_op | source)
XLA Modules:
  0.0 113.2 jit_solution(12076111056515465642)
XLA Ops:
  0.6 3.6 %prep.1 = (bf16[560,128]{1,0:T(8,128)(2,1)}, f32[16,128]{1,0:T(8,128)}, bf16[2800,128]{1,0:T(8,128)(2,1)}) custom-call(s32[1,4]{1,0:T(1,128)} %lengths.1, f32[16]{0:T(128)} %bias.1, f32[16]{0:T(128)} %decay.1, f32[16]{0:T(128)} %skip.1, f32[1,2048]{1,0:T(1,128)} %bitcast.23, bf16[128,8192]{1,0:T(8,128)(2,1)} %bitcast.14, bf16[16,8192]{1,0:T(8,128)(2,1)} %bitcast.20, ...), custom_call_target="tpu_custom_call" | custom-call | tf_op jit(solution)/shard_map/prep/pallas_call | solution.py:663
  4.2 2.5 %collective-permute-start = (bf16[560,128]{1,0:T(8,128)(2,1)}, bf16[560,128]{1,0:T(8,128)(2,1)S(1)}, u32[]{:S(2)}, u32[]{:S(2)}) collective-permute-start(bf16[560,128]{1,0:T(8,128)(2,1)} %get-tuple-element.33), channel_id=1, source_target_pairs={{0,32},{32,64},{64,96},{96,128},{128,160},{160,192},{192,224},{224... | collective-permute-start | bytes 430088 | tf_op jit(solution)/shard_map/ppermute | solution.py:687
  6.7 7.6 %collective-permute-done.refs_3_ = bf16[560,128]{1,0:T(8,128)(2,1)S(1)} collective-permute-done((bf16[560,128]{1,0:T(8,128)(2,1)}, bf16[560,128]{1,0:T(8,128)(2,1)S(1)}, u32[]{:S(2)}, u32[]{:S(2)}) %collective-permute-start) | collective-permute-done | bytes 143392 | tf_op jit(solution)/shard_map/ppermute | solution.py:687
  14.3 0.0 collective-permute-start.1
  14.3 1.2 %collective-permute-start.4 = (bf16[560,128]{1,0:T(8,128)(2,1)}, bf16[560,128]{1,0:T(8,128)(2,1)S(1)}, u32[]{:S(2)}, u32[]{:S(2)}) collective-permute-start(bf16[560,128]{1,0:T(8,128)(2,1)} %get-tuple-element.33), channel_id=1, source_target_pairs={{0,16},{16,0},{1,17},{17,1},{2,18},{18,2},{3,19},{19,3},{4,20},{20... | collective-permute-start | bytes 430088 | tf_op jit(solution)/shard_map/ppermute | solution.py:685
  15.5 0.0 collective-permute-start.3
  15.5 0.0 copy-start
  15.5 1.1 copy-done
  16.6 4.2 %forward_a.1 = (f32[6400,128]{1,0:T(8,128)S(1)}, f32[4864,128]{1,0:T(8,128)S(1)}) custom-call(bf16[2800,128]{1,0:T(8,128)(2,1)S(1)} %copy-done), custom_call_target="tpu_custom_call" | custom-call | flops 402653184 | bytes 3145728 | tf_op jit(solution)/shard_map/forward_a/pallas_call | solution.py:450
  20.9 0.0 collective-permute-done.1.refs_3_
  20.9 0.1 collective-permute-start.2
  21.0 0.9 collective-permute-start.6
  21.8 0.0 collective-permute-done.4.refs_2_
  21.8 0.0 collective-permute-done.3.refs_1_.refs_2_
  21.8 2.8 %forward_b.1.refs_5_ = f32[9344,128]{1,0:T(8,128)S(1)} custom-call(bf16[2800,128]{1,0:T(8,128)(2,1)S(1)} %copy-done, bf16[560,128]{1,0:T(8,128)(2,1)S(1)} %collective-permute-done.3.refs_1_.refs_2_, bf16[560,128]{1,0:T(8,128)(2,1)S(1)} %collective-permute-done.4.refs_2_, bf16[560,128]{1,0:T(8,128)(2,1)S(1)} %collective-permute-done.refs_3_, ...), custom_call_target="tpu_custom_call" | custom-call | flops 805306368 | bytes 6291456 | tf_op jit(solution)/shard_map/forward_b/pallas_call | solution.py:450
  24.7 2.5 %collective-permute-done.2.refs_3_ = bf16[560,128]{1,0:T(8,128)(2,1)S(1)} collective-permute-done((bf16[560,128]{1,0:T(8,128)(2,1)S(1)}, bf16[560,128]{1,0:T(8,128)(2,1)S(1)}, u32[]{:S(2)}, u32[]{:S(2)}) %collective-permute-start.2) | collective-permute-done | bytes 143392 | tf_op jit(solution)/shard_map/ppermute | solution.py:693
  27.2 0.0 collective-permute-start.5
  27.2 1.4 %collective-permute-start.8 = (bf16[560,128]{1,0:T(8,128)(2,1)S(1)}, bf16[560,128]{1,0:T(8,128)(2,1)S(1)}, u32[]{:S(2)}, u32[]{:S(2)}) collective-permute-start(bf16[560,128]{1,0:T(8,128)(2,1)S(1)} %collective-permute-done.2.refs_3_), channel_id=1, source_target_pairs={{0,16},{16,0},{1,17},{17,1},{2,18},{18,2},{3,19},{19,3},{4,20},{20... | collective-permute-start | bytes 430088 | tf_op jit(solution)/shard_map/ppermute | solution.py:685
  28.6 0.0 collective-permute-done.6.refs_1_.refs_2_
  28.6 2.8 %forward_c.1.refs_6_ = f32[9344,128]{1,0:T(8,128)S(1)} custom-call(bf16[2800,128]{1,0:T(8,128)(2,1)S(1)} %copy-done, bf16[560,128]{1,0:T(8,128)(2,1)S(1)} %collective-permute-done.6.refs_1_.refs_2_, bf16[560,128]{1,0:T(8,128)(2,1)S(1)} %collective-permute-done.3.refs_1_.refs_2_, bf16[560,128]{1,0:T(8,128)(2,1)S(1)} %collective-permute-done.1.refs_3_, ...), custom_call_target="tpu_custom_call" | custom-call | flops 805306368 | bytes 6291456 | tf_op jit(solution)/shard_map/forward_c/pallas_call | solution.py:450
  31.5 0.9 collective-permute-done.5.refs_3_
  32.3 2.6 %collective-permute-start.7 = (bf16[560,128]{1,0:T(8,128)(2,1)S(1)}, bf16[560,128]{1,0:T(8,128)(2,1)S(1)}, u32[]{:S(2)}, u32[]{:S(2)}) collective-permute-start(bf16[560,128]{1,0:T(8,128)(2,1)S(1)} %collective-permute-done.5.refs_3_), channel_id=1, source_target_pairs={{0,16},{16,0},{1,17},{17,1},{2,18},{18,2},{3,19},{19,3},{4,20},{20... | collective-permute-start | bytes 430088 | tf_op jit(solution)/shard_map/ppermute | solution.py:685
  34.9 0.0 collective-permute-done.8.refs_1_.refs_2_
  34.9 2.8 %forward_d.1.refs_7_ = f32[9344,128]{1,0:T(8,128)S(1)} custom-call(bf16[2800,128]{1,0:T(8,128)(2,1)S(1)} %copy-done, bf16[560,128]{1,0:T(8,128)(2,1)S(1)} %collective-permute-done.8.refs_1_.refs_2_, bf16[560,128]{1,0:T(8,128)(2,1)S(1)} %collective-permute-done.6.refs_1_.refs_2_, bf16[560,128]{1,0:T(8,128)(2,1)S(1)} %collective-permute-done.2.refs_3_, ...), custom_call_target="tpu_custom_call" | custom-call | flops 805306368 | bytes 6291456 | tf_op jit(solution)/shard_map/forward_d/pallas_call | solution.py:450
  37.8 0.0 collective-permute-done.7.refs_1_
  37.8 5.2 %forward_e.1 = (f32[8960,128]{1,0:T(8,128)S(1)}, bf16[4352,128]{1,0:T(8,128)(2,1)S(1)}, f32[8,128]{1,0:T(8,128)S(1)}) custom-call(bf16[2800,128]{1,0:T(8,128)(2,1)S(1)} %copy-done, bf16[560,128]{1,0:T(8,128)(2,1)S(1)} %collective-permute-done.7.refs_1_, bf16[560,128]{1,0:T(8,128)(2,1)S(1)} %collective-permute-done.8.refs_1_.refs_2_, ...), custom_call_target="tpu_custom_call" | custom-call | flops 805306368 | bytes 6291456 | tf_op jit(solution)/shard_map/forward_e/pallas_call | solution.py:450
  43.0 2.8 %collective-permute-start.11 = (f32[8,128]{1,0:T(8,128)S(1)}, f32[8,128]{1,0:T(8,128)S(1)}, u32[]{:S(2)}, u32[]{:S(2)}) collective-permute-start(f32[8,128]{1,0:T(8,128)S(1)} %get-tuple-element.43.refs_4_), channel_id=1, source_target_pairs={{0,12},{4,0},{8,4},{12,8},{1,13},{5,1},{9,5},{13,9},{2,14},{6,2},{... | collective-permute-start | bytes 12296 | tf_op jit(solution)/shard_map/ppermute | solution.py:708
  45.8 0.3 collective-permute-start.10
  46.2 0.7 collective-permute-start.9
  46.9 0.0 collective-permute-done.11.refs_7_
  46.9 2.9 %collective-permute-done.10.refs_6_ = f32[8,128]{1,0:T(8,128)S(1)} collective-permute-done((f32[8,128]{1,0:T(8,128)S(1)}, f32[8,128]{1,0:T(8,128)S(1)}, u32[]{:S(2)}, u32[]{:S(2)}) %collective-permute-start.10) | collective-permute-done | bytes 4128 | tf_op jit(solution)/shard_map/ppermute | solution.py:708
  49.8 0.1 collective-permute-done.9.refs_5_
  49.8 0.0 copy-start.1
  49.8 0.0 copy-start.2
  49.8 7.3 %backward.1 = (bf16[128,2048]{1,0:T(8,128)(2,1)}, f32[16,16,128]{2,1,0:T(8,128)S(1)}, f32[1,2048]{1,0:T(1,128)S(1)}, f32[8,128]{1,0:T(8,128)S(1)}) custom-call(bf16[2800,128]{1,0:T(8,128)(2,1)S(1)} %copy-done, f32[4864,128]{1,0:T(8,128)S(1)} %get-tuple-element.32.refs_8_.refs_1_, f32[8960,128]{1,0:T(8,128)S(1)} %get-tuple-element.41.refs_2_, ...), custom_call_target="tpu_custom_call" | custom-call | tf_op jit(solution)/shard_map/backward/pallas_call | solution.py:712
  57.1 16.2 %all_to_all.15.grads = f32[16,16,128]{2,1,0:T(8,128)S(1)} all-to-all(f32[16,16,128]{2,1,0:T(8,128)S(1)} %get-tuple-element.48), channel_id=1, replica_groups=mesh['z'=8,'core'=2,'grp'=4,'dp'=4] {'z','core'}, dimensions={0} | all-to-all | bytes 262144 | tf_op jit(solution)/shard_map/all_to_all | solution.py:735
  73.3 0.0 copy-done.1
  73.3 0.0 copy-done.2
  73.4 0.7 weights.1
  74.0 0.1 collective-permute-start.12
  74.1 1.5 %collective-permute-done.12 = f32[544,128]{1,0:T(8,128)S(1)} collective-permute-done((f32[544,128]{1,0:T(8,128)S(1)}, f32[544,128]{1,0:T(8,128)S(1)}, u32[]{:S(2)}, u32[]{:S(2)}) %collective-permute-start.12) | collective-permute-done | bytes 278560 | tf_op jit(solution)/shard_map/ppermute | solution.py:749
  75.7 16.6 %all_to_all.16 = f32[32,17,1,128]{3,2,1,0:T(1,128)S(1)} all-to-all(f32[32,17,1,128]{3,2,1,0:T(1,128)S(1)} %bitcast.18), channel_id=1, replica_groups=mesh['z'=8,'core'=2,'grp'=4,'dp'=4] {'z','dp'}, dimensions={0} | all-to-all | bytes 557056 | tf_op jit(solution)/shard_map/all_to_all | solution.py:751
  92.3 0.2 reduce_sum.9
  92.5 0.1 broadcast_in_dim.14
  92.6 15.0 %all_to_all.17 = f32[32,17,1,128]{3,2,1,0:T(1,128)S(1)} all-to-all(f32[32,17,1,128]{3,2,1,0:T(1,128)S(1)} %broadcast_in_dim.14), channel_id=1, replica_groups=mesh['z'=8,'core'=2,'grp'=4,'dp'=4] {'z','dp'}, dimensions={0} | all-to-all | bytes 557056 | tf_op jit(solution)/shard_map/all_to_all | solution.py:754
  107.7 3.5 %collective-permute-start.13 = (f32[544,128]{1,0:T(8,128)S(1)}, f32[544,128]{1,0:T(8,128)S(1)}, u32[]{:S(2)}, u32[]{:S(2)}) collective-permute-start(f32[544,128]{1,0:T(8,128)S(1)} %bitcast.16), channel_id=1, source_target_pairs={{0,16},{16,0},{1,17},{17,1},{2,18},{18,2},{3,19},{19,3},{4,20},{20... | collective-permute-start | bytes 835592 | tf_op jit(solution)/shard_map/ppermute | solution.py:756
  111.1 1.2 %collective-permute-done.13.other = f32[544,128]{1,0:T(8,128)S(1)} collective-permute-done((f32[544,128]{1,0:T(8,128)S(1)}, f32[544,128]{1,0:T(8,128)S(1)}, u32[]{:S(2)}, u32[]{:S(2)}) %collective-permute-start.13) | collective-permute-done | bytes 278560 | tf_op jit(solution)/shard_map/ppermute | solution.py:756
  112.3 0.8 finish.1
  (1 shorter events, 0.0 us)
Async XLA Ops:
  4.2 10.1 %collective-permute-start = (bf16[560,128]{1,0:T(8,128)(2,1)}, bf16[560,128]{1,0:T(8,128)(2,1)S(1)}, u32[]{:S(2)}, u32[]{:S(2)}) collective-permute-start(bf16[560,128]{1,0:T(8,128)(2,1)} %get-tuple-element.33), channel_id=1, source_target_pairs={{0,32},{32,64},{64,96},{96,128},{128,160},{160,192},{192,224},{224... | collective-permute-start | bytes 430088 | tf_op jit(solution)/shard_map/ppermute | solution.py:687
  14.3 6.6 %collective-permute-start.1 = (bf16[560,128]{1,0:T(8,128)(2,1)S(1)}, bf16[560,128]{1,0:T(8,128)(2,1)S(1)}, u32[]{:S(2)}, u32[]{:S(2)}) collective-permute-start(bf16[560,128]{1,0:T(8,128)(2,1)S(1)} %collective-permute-done.refs_3_), channel_id=1, source_target_pairs={{0,32},{32,64},{64,96},{96,128},{128,160},{160,192},{192,224},{224... | collective-permute-start | bytes 430088 | tf_op jit(solution)/shard_map/ppermute | solution.py:689
  14.3 7.5 %collective-permute-start.4 = (bf16[560,128]{1,0:T(8,128)(2,1)}, bf16[560,128]{1,0:T(8,128)(2,1)S(1)}, u32[]{:S(2)}, u32[]{:S(2)}) collective-permute-start(bf16[560,128]{1,0:T(8,128)(2,1)} %get-tuple-element.33), channel_id=1, source_target_pairs={{0,16},{16,0},{1,17},{17,1},{2,18},{18,2},{3,19},{19,3},{4,20},{20... | collective-permute-start | bytes 430088 | tf_op jit(solution)/shard_map/ppermute | solution.py:685
  15.5 6.3 %collective-permute-start.3 = (bf16[560,128]{1,0:T(8,128)(2,1)S(1)}, bf16[560,128]{1,0:T(8,128)(2,1)S(1)}, u32[]{:S(2)}, u32[]{:S(2)}) collective-permute-start(bf16[560,128]{1,0:T(8,128)(2,1)S(1)} %collective-permute-done.refs_3_), channel_id=1, source_target_pairs={{0,16},{16,0},{1,17},{17,1},{2,18},{18,2},{3,19},{19,3},{4,20},{20... | collective-permute-start | bytes 430088 | tf_op jit(solution)/shard_map/ppermute | solution.py:685
  15.5 1.1 copy-start
  20.9 6.3 %collective-permute-start.2 = (bf16[560,128]{1,0:T(8,128)(2,1)S(1)}, bf16[560,128]{1,0:T(8,128)(2,1)S(1)}, u32[]{:S(2)}, u32[]{:S(2)}) collective-permute-start(bf16[560,128]{1,0:T(8,128)(2,1)S(1)} %collective-permute-done.1.refs_3_), channel_id=1, source_target_pairs={{0,32},{32,64},{64,96},{96,128},{128,160},{160,192},{192,224},{224... | collective-permute-start | bytes 430088 | tf_op jit(solution)/shard_map/ppermute | solution.py:693
  21.0 7.7 %collective-permute-start.6 = (bf16[560,128]{1,0:T(8,128)(2,1)S(1)}, bf16[560,128]{1,0:T(8,128)(2,1)S(1)}, u32[]{:S(2)}, u32[]{:S(2)}) collective-permute-start(bf16[560,128]{1,0:T(8,128)(2,1)S(1)} %collective-permute-done.1.refs_3_), channel_id=1, source_target_pairs={{0,16},{16,0},{1,17},{17,1},{2,18},{18,2},{3,19},{19,3},{4,20},{20... | collective-permute-start | bytes 430088 | tf_op jit(solution)/shard_map/ppermute | solution.py:685
  27.2 5.2 %collective-permute-start.5 = (bf16[560,128]{1,0:T(8,128)(2,1)S(1)}, bf16[560,128]{1,0:T(8,128)(2,1)S(1)}, u32[]{:S(2)}, u32[]{:S(2)}) collective-permute-start(bf16[560,128]{1,0:T(8,128)(2,1)S(1)} %collective-permute-done.2.refs_3_), channel_id=1, source_target_pairs={{0,32},{32,64},{64,96},{96,128},{128,160},{160,192},{192,224},{224... | collective-permute-start | bytes 430088 | tf_op jit(solution)/shard_map/ppermute | solution.py:697
  27.2 7.8 %collective-permute-start.8 = (bf16[560,128]{1,0:T(8,128)(2,1)S(1)}, bf16[560,128]{1,0:T(8,128)(2,1)S(1)}, u32[]{:S(2)}, u32[]{:S(2)}) collective-permute-start(bf16[560,128]{1,0:T(8,128)(2,1)S(1)} %collective-permute-done.2.refs_3_), channel_id=1, source_target_pairs={{0,16},{16,0},{1,17},{17,1},{2,18},{18,2},{3,19},{19,3},{4,20},{20... | collective-permute-start | bytes 430088 | tf_op jit(solution)/shard_map/ppermute | solution.py:685
  32.3 5.4 %collective-permute-start.7 = (bf16[560,128]{1,0:T(8,128)(2,1)S(1)}, bf16[560,128]{1,0:T(8,128)(2,1)S(1)}, u32[]{:S(2)}, u32[]{:S(2)}) collective-permute-start(bf16[560,128]{1,0:T(8,128)(2,1)S(1)} %collective-permute-done.5.refs_3_), channel_id=1, source_target_pairs={{0,16},{16,0},{1,17},{17,1},{2,18},{18,2},{3,19},{19,3},{4,20},{20... | collective-permute-start | bytes 430088 | tf_op jit(solution)/shard_map/ppermute | solution.py:685
  43.0 3.9 %collective-permute-start.11 = (f32[8,128]{1,0:T(8,128)S(1)}, f32[8,128]{1,0:T(8,128)S(1)}, u32[]{:S(2)}, u32[]{:S(2)}) collective-permute-start(f32[8,128]{1,0:T(8,128)S(1)} %get-tuple-element.43.refs_4_), channel_id=1, source_target_pairs={{0,12},{4,0},{8,4},{12,8},{1,13},{5,1},{9,5},{13,9},{2,14},{6,2},{... | collective-permute-start | bytes 12296 | tf_op jit(solution)/shard_map/ppermute | solution.py:708
  45.8 4.0 %collective-permute-start.10 = (f32[8,128]{1,0:T(8,128)S(1)}, f32[8,128]{1,0:T(8,128)S(1)}, u32[]{:S(2)}, u32[]{:S(2)}) collective-permute-start(f32[8,128]{1,0:T(8,128)S(1)} %get-tuple-element.43.refs_4_), channel_id=1, source_target_pairs={{0,8},{4,12},{8,0},{12,4},{1,9},{5,13},{9,1},{13,5},{2,10},{6,14},... | collective-permute-start | bytes 12296 | tf_op jit(solution)/shard_map/ppermute | solution.py:708
  46.2 3.7 %collective-permute-start.9 = (f32[8,128]{1,0:T(8,128)S(1)}, f32[8,128]{1,0:T(8,128)S(1)}, u32[]{:S(2)}, u32[]{:S(2)}) collective-permute-start(f32[8,128]{1,0:T(8,128)S(1)} %get-tuple-element.43.refs_4_), channel_id=1, source_target_pairs={{0,4},{4,8},{8,12},{12,0},{1,5},{5,9},{9,13},{13,1},{2,6},{6,10},{... | collective-permute-start | bytes 12296 | tf_op jit(solution)/shard_map/ppermute | solution.py:708
  49.8 23.5 %copy-start.1 = (bf16[1,128,8192]{2,1,0:T(8,128)(2,1)S(1)}, bf16[1,128,8192]{2,1,0:T(8,128)(2,1)}, u32[]{:S(2)}) copy-start(bf16[1,128,8192]{2,1,0:T(8,128)(2,1)} %param.10) | copy-start | bytes 6291460
  49.8 23.5 %copy-start.2 = (f32[16,128]{1,0:T(8,128)S(1)}, f32[16,128]{1,0:T(8,128)}, u32[]{:S(2)}) copy-start(f32[16,128]{1,0:T(8,128)} %get-tuple-element.45.slope) | copy-start | bytes 24580
  74.0 1.6 %collective-permute-start.12 = (f32[544,128]{1,0:T(8,128)S(1)}, f32[544,128]{1,0:T(8,128)S(1)}, u32[]{:S(2)}, u32[]{:S(2)}) collective-permute-start(f32[544,128]{1,0:T(8,128)S(1)} %get-tuple-element.50), channel_id=1, source_target_pairs={{0,16},{16,0},{1,17},{17,1},{2,18},{18,2},{3,19},{19,3},{4,20},{20... | collective-permute-start | bytes 835592 | tf_op jit(solution)/shard_map/ppermute | solution.py:749
  107.7 4.6 %collective-permute-start.13 = (f32[544,128]{1,0:T(8,128)S(1)}, f32[544,128]{1,0:T(8,128)S(1)}, u32[]{:S(2)}, u32[]{:S(2)}) collective-permute-start(f32[544,128]{1,0:T(8,128)S(1)} %bitcast.16), channel_id=1, source_target_pairs={{0,16},{16,0},{1,17},{17,1},{2,18},{18,2},{3,19},{19,3},{4,20},{20... | collective-permute-start | bytes 835592 | tf_op jit(solution)/shard_map/ppermute | solution.py:756

commit v4 on v3

--- a/solution.py
+++ b/solution.py
@@ -27,6 +27,12 @@
 
 
 def mm_two(a, b):
+    rows = a.shape[0]
+    both = mm(jnp.concatenate(two_parts(a), axis=0), b)
+    return both[:rows] + both[rows:]
+
+
+def mm_apart(a, b):
     high, low = two_parts(a)
     return mm(high, b) + mm(low, b)
 
@@ -77,23 +83,46 @@
     decay,
     skip,
     gain,
-    hidden,
+    hidden_far,
+    queries,
     weight,
     keys,
     values,
-    queries,
     payload,
     slope,
     local,
+    sent,
     consts,
+    hidden,
+    asked,
+    stage,
+    fetched,
+    moved,
 ):
     heads = weight.shape[0]
-    pre = (
-        lax.dot_general(
-            hidden[...], weight[...], (((1,), (1,)), ((), ())), preferred_element_type=F32
-        ).T
-        + column_of(bias, heads)
-    )
+    side = sent.shape[1]
+    at = local_rows(heads, kv)[0]
+    chunks = fetched.shape[0]
+    width = hidden.shape[1] // chunks
+    fetches = []
+    for i in range(chunks):
+        part = slice(width * i, width * (i + 1))
+        fetch = pltpu.make_async_copy(hidden_far.at[:, part], hidden.at[:, part], fetched.at[i])
+        fetch.start()
+        fetches.append(fetch)
+    ask = pltpu.make_async_copy(queries, asked, moved.at[0])
+    ask.start()
+    pre = jnp.zeros((hidden.shape[0], heads), F32)
+    for i in range(chunks):
+        part = slice(width * i, width * (i + 1))
+        fetches[i].wait()
+        pre = pre + lax.dot_general(
+            hidden[:, part], weight[:, part], (((1,), (1,)), ((), ())), preferred_element_type=F32
+        )
+    other = pl.multiple_of((1 - lax.axis_index("core")) * side, side)
+    give = pltpu.make_async_copy(hidden.at[:, pl.ds(other, side)], sent, moved.at[1])
+    give.start()
+    pre = pre.T + column_of(bias, heads)
     step = jnp.maximum(pre, 0.0) + jnp.log1p(jnp.exp(-jnp.abs(pre)))
     slope[...] = 1.0 / (1.0 + jnp.exp(-pre))
     for g in range(kv):
@@ -118,15 +147,19 @@
         piece = step.astype(BF16)
         payload[first + part * heads : first + (part + 1) * heads, :] = piece
         step = step - piece.astype(F32)
-    at = local_rows(heads, kv)[0]
-    for h in range(heads):
-        local[at[0] + 128 * h : at[0] + 128 * h + 128, :] = queries[:, 128 * h : 128 * h + 128]
-    local[at[1] : at[1] + payload.shape[0], :] = payload[...]
+    stage[at[1] : at[1] + payload.shape[0], :] = payload[...]
     rest = consts[...]
     for part in range(3):
         piece = rest.astype(BF16)
-        local[at[2 + part] : at[2 + part] + rest.shape[0], :] = piece
+        stage[at[2 + part] : at[2 + part] + rest.shape[0], :] = piece
         rest = rest - piece.astype(F32)
+    ask.wait()
+    for h in range(heads):
+        stage[at[0] + 128 * h : at[0] + 128 * h + 128, :] = asked[:, 128 * h : 128 * h + 128]
+    put = pltpu.make_async_copy(stage, local, moved.at[2])
+    put.start()
+    give.wait()
+    put.wait()
 
 
 def masks(info):
@@ -164,7 +197,9 @@
     if part == 0:
         return layout(wide, wide, wide, 0, heads * 3, const_rows(heads), 0, 0)
     turned = kv * count * 128
-    return layout(wide, wide, wide, wide, heads * (2 + 2 * count), 0, turned, turned)
+    return layout(
+        wide, wide, wide, wide, heads * (2 + 2 * count), 0, turned, turned, wide if part == 2 else 0
+    )
 
 
 def const_rows(heads):
@@ -189,7 +224,7 @@
     count = BACK + 1
     wide = heads * 128
     return layout(
-        wide, wide, wide, const_rows(heads), count * heads, BACK * heads, kv * count * 128
+        wide, wide, 0, const_rows(heads), count * heads, BACK * heads, kv * count * 128
     )
 
 
@@ -247,6 +282,7 @@
     else:
         constant, base = origin, origin_at[5]
     cum_at = origin_at[4] + heads
+    enter_at = carry_rows(heads, kv, 2)[0][8]
     group = heads // kv
     size = 3 * heads + 8
     info = place_of(constant[base + size - 8 : base + size, :], 128)
@@ -342,6 +378,9 @@
         if not first:
             small[fade_at + heads * i : fade_at + heads * (i + 1), :] = fade_ref[i]
 
+    def rate_of(h):
+        return constant[pl.ds(base + h, 1), :]
+
     def one_head(h, unused):
         g = h // group
         query = local[slab(local_at[0], h), :]
@@ -358,7 +397,7 @@
         for other in weights[1:]:
             total = total + other
         total = jnp.broadcast_to(jnp.sum(total, axis=1, keepdims=True), (128, 128))
-        mixed = mm(jnp.concatenate([w.astype(BF16) for w in weights], axis=1), vv[g])
+        weights = jnp.concatenate([w.astype(BF16) for w in weights], axis=1)
         if not first:
             weight_row = jnp.concatenate(
                 [
@@ -367,47 +406,52 @@
                 ],
                 axis=1,
             )
-            state = mm_two(key32[g] * weight_row, vv[g])
+            mixed = mm(weights, vv[g])
+            state = mm_apart(key32[g] * weight_row, vv[g])
             scale = jnp.exp2(old - top)
             total = total + before_carry[slab(before_at[1], h), :] * scale
             mixed = mixed + before_carry[slab(before_at[2], h), :] * scale
             if part > 1:
                 state = state + before_carry[slab(before_at[3], h), :]
+        else:
+            decay_row = rate_of(h)
+            cum_row = jnp.broadcast_to(cum_ref[pl.ds(h, 1), :], (128, 128))
+            cum_col = cum_row.T
+            decay = jnp.where(
+                allowed, jnp.exp(-decay_row * jnp.maximum(cum_col - cum_row, 0.0)), 0.0
+            )
+            decayed = scores[:, :128] * decay
+            keep[slab(keep_at[1], h), :] = decayed
+            skipped = constant[pl.ds(base + heads + h, 1), :] * value_ref[g]
+            high, low = two_parts(decayed * step_ref[0, pl.ds(h, 1), :])
+            joined = mm(jnp.concatenate([weights, high, low], axis=0), vv[g])
+            mixed = joined[:128]
+            keep[slab(keep_at[0], h), :] = joined[128:256] + joined[256:] + skipped
         if not last:
             carry[slab(carry_at[0], h), :] = top
             carry[slab(carry_at[1], h), :] = total
             carry[slab(carry_at[2], h), :] = mixed
             if not first:
                 carry[slab(carry_at[3], h), :] = state
-        rate_h = constant[pl.ds(base + h, 1), :]
-        if first:
-            cum_row = jnp.broadcast_to(cum_ref[pl.ds(h, 1), :], (128, 128))
-            cum_col = cum_row.T
-            decay = jnp.where(
-                allowed, jnp.exp(-rate_h * jnp.maximum(cum_col - cum_row, 0.0)), 0.0
+        if part == 2:
+            cum_col = jnp.broadcast_to(origin[pl.ds(cum_at + h, 1), :], (128, 128)).T
+            carry[slab(enter_at, h), :] = jnp.where(
+                carried, jnp.exp(-rate_of(h) * cum_col), 0.0
             )
-            decayed = scores[:, :128] * decay
-            keep[slab(keep_at[1], h), :] = decayed
-            skipped = constant[pl.ds(base + heads + h, 1), :] * value_ref[g]
-            mixing = decayed * step_ref[0, pl.ds(h, 1), :]
-            keep[slab(keep_at[0], h), :] = mm_two(mixing, vv[g, :128, :]) + skipped
         if last:
             teach = (mixed / total).astype(BF16)
             half[slab(half_at[0], h), :] = teach
-            cum_col = jnp.broadcast_to(origin[pl.ds(cum_at + h, 1), :], (128, 128)).T
-            entering = jnp.where(carried, jnp.exp(-rate_h * cum_col), 0.0)
-            off = mm_right(query, state) * entering
+            off = mm_right(query, state) * carries[2][slab(enter_at, h), :]
             raw = keep[slab(keep_at[0], h), :] + off
             real[slab(real_at[0], h), :] = raw
             real[slab(real_at[1], h), :] = off
-            real[slab(real_at[2], h), :] = entering
             gained = raw * constant[pl.ds(base + 2 * heads + h, 1), :]
             acc[0] += raw * raw
             acc[1] += gained * gained
             acc[2] += gained * teach.astype(F32)
         return unused
 
-    lax.fori_loop(0, heads, one_head, 0, unroll=4)
+    lax.fori_loop(0, heads, one_head, 0, unroll=(8, 4, 4, 8, 16)[part])
     if last:
         stats[...] = jnp.concatenate(
             [to_row(acc[0]), to_row(acc[1]), to_row(acc[2]), jnp.zeros((5, 128), F32)], axis=0
@@ -464,7 +508,7 @@
 
 
 def backward_kernel(kv, heads, groups, features, row_total, *refs):
-    local, keep, real, half, *refs = refs
+    local, keep, enter, real, half, *refs = refs
     stats = refs[0][...]
     for other in refs[1:groups]:
         stats = stats + other[...]
@@ -474,6 +518,7 @@
     real_at = real_rows(heads, kv)[0]
     half_at = half_rows(heads, kv)[0]
     group = heads // kv
+    enter_at = carry_rows(heads, kv, 2)[0][8]
     size = 3 * heads + 8
     base = real_at[3]
     info = place_of(real[base + size - 8 : base + size, :], 128)
@@ -505,7 +550,7 @@
         grad = inv * grad_normed * scale - raw * coef_col[...]
         value = keep[slab(keep_at[2], g), :]
         skip_rows[pl.ds(h, 1), :] = jnp.sum(grad * value, axis=0, keepdims=True)
-        entering = real[slab(real_at[2], h), :]
+        entering = enter[slab(enter_at, h), :]
         grad_state = mm_two((grad * entering).T, query)
         turned = [slab(g * ((BACK + 1) * 128), d) for d in range(BACK + 1)]
         keys = jnp.concatenate(
@@ -530,7 +575,7 @@
         row_sums[...] += jnp.where(col_i == h, jnp.broadcast_to(sums, (128, 128)), 0.0)
         return unused
 
-    lax.fori_loop(0, heads, one_head, 0, unroll=4)
+    lax.fori_loop(0, heads, one_head, 0, unroll=16)
 
     def summed(x, triangle):
         high, low = two_parts(x)
@@ -556,38 +601,59 @@
     )
 
 
-def weight_kernel(slope, hidden, gain, small, grads, keep, send):
+def fold_kernel(grads, gain, small, out):
     total = jnp.sum(grads[...], axis=0)
-    grad_pre = total * slope[...]
-    low = grad_pre.astype(BF16)
-    heads = low.shape[0]
-    count = keep.shape[0] // (heads + 1)
+    rows = total.shape[0]
     tiles = gain.shape[1] // 128
+    out[0:rows, :] = total
+    for i in range(tiles):
+        out[rows + i : rows + i + 1, :] = gain[:, 128 * i : 128 * i + 128]
+    out[rows + tiles : rows + tiles + 8, :] = small[...]
+
+
+def weight_kernel(own, other, slope, slope_other, hidden, far, out, wide):
+    heads = slope.shape[0]
+    total = own[...] + other[...]
     core = lax.axis_index("core")
-
-    def fill(out, half):
-        for j in range(count):
-            i = half * count + j
-            start = j * (heads + 1)
-            out[start : start + heads, :] = mm(low, hidden[:, 128 * i : 128 * i + 128])
-            at = slice(start + heads, start + heads + 1)
-            if i < tiles:
-                out[at, :] = gain[:, 128 * i : 128 * i + 128]
-            elif i == tiles:
-                out[at, :] = to_row(grad_pre)
-            elif i == tiles + 1:
-                out[at, :] = small[1:2, :]
-            elif i == tiles + 2:
-                out[at, :] = small[0:1, :]
-            else:
-                out[at, :] = jnp.zeros((1, 128), F32)
-
-    for mine in range(2):
-
-        @pl.when(core == mine)
-        def _():
-            fill(keep, mine)
-            fill(send, 1 - mine)
+    low_core = core == 0
+    near_slope, far_slope = slope[...], slope_other[...]
+    top, bottom = total[0:heads], total[heads : 2 * heads]
+    near_pre = jnp.where(low_core, top, bottom) * near_slope
+    far_pre = jnp.where(low_core, bottom, top) * far_slope
+    near_low, far_low = near_pre.astype(BF16), far_pre.astype(BF16)
+    side = far.shape[1]
+    count = side // 128
+    tiles = total.shape[0] - 2 * heads - 8
+    lines = [total[2 * heads + i : 2 * heads + i + 1] for i in range(tiles)]
+    lines.append(to_row(near_pre + far_pre))
+    base = 2 * heads + tiles
+    lines += [total[base + 1 : base + 2], total[base : base + 1]]
+    for j in range(count):
+        start = j * (heads + 2)
+        near = hidden[:, pl.ds(pl.multiple_of(core * side + 128 * j, 128), 128)]
+        wide[start : start + heads, :] = mm(near_low, near) + mm(
+            far_low, far[:, 128 * j : 128 * j + 128]
+        )
+        line = jnp.zeros((1, 128), F32)
+        if j < len(lines):
+            line = jnp.where(low_core, lines[j], line)
+        high = line.astype(BF16).astype(F32)
+        wide[start + heads : start + heads + 1, :] = high
+        wide[start + heads + 1 : start + heads + 2, :] = line - high
+    out[...] = wide[...].astype(BF16)
+
+
+def spread_kernel(count, got, out, wide):
+    wide[...] = got[...].astype(F32)
+    each = wide.shape[0] // count
+    total = wide[0:each, :]
+    for j in range(1, count):
+        total = total + wide[each * j : each * (j + 1), :]
+    small = total[each - 2 : each - 1, :] + total[each - 1 : each, :]
+    for j in range(count):
+        start = (each - 1) * j
+        out[start : start + each - 2, :] = total[: each - 2, :]
+        out[start + each - 2 : start + each - 1, :] = small
 
 
 def finish_kernel(mine, other, weight, bias, decay, skip, gain):
@@ -625,6 +691,10 @@
 
 def smem(count):
     return [pl.BlockSpec(memory_space=pltpu.SMEM)] * count
+
+
+def anywhere(count):
+    return [pl.BlockSpec(memory_space=pl.ANY)] * count
 
 
 def shape(dims, kind=F32):
@@ -660,21 +730,29 @@
     gain = norm_gain[None, :]
     cargo = 2 * kv * HDIM + 3 * heads
 
-    payload, slope, local = pl.pallas_call(
+    payload, slope, local, sent = pl.pallas_call(
         functools.partial(prep_kernel, kv),
         out_shape=[
             shape((cargo, 128), BF16),
             shape((heads, 128)),
             shape((local_rows(heads, kv)[1], 128), BF16),
+            shape((rows, depth // 2), BF16),
         ],
-        in_specs=smem(4) + vmem(6),
-        out_specs=vmem(3),
-        scratch_shapes=[pltpu.VMEM((const_rows(heads), 128), F32)],
+        in_specs=smem(4) + vmem(1) + anywhere(2) + vmem(3),
+        out_specs=vmem(2) + anywhere(2),
+        scratch_shapes=[
+            pltpu.VMEM((const_rows(heads), 128), F32),
+            pltpu.VMEM((rows, depth), BF16),
+            pltpu.VMEM((rows, width), BF16),
+            pltpu.VMEM((local_rows(heads, kv)[1], 128), BF16),
+            pltpu.SemaphoreType.DMA((4,)),
+            pltpu.SemaphoreType.DMA((3,)),
+        ],
         compiler_params=LARGE,
         name="prep",
     )(
-        doc_lengths, dt_bias, decay_log, skip_gain, gain, hidden, dt_weight.T,
-        teacher_keys[0], teacher_values[0], teacher_queries[0],
+        doc_lengths, dt_bias, decay_log, skip_gain, gain, hidden, teacher_queries[0],
+        dt_weight.T, teacher_keys[0], teacher_values[0],
     )
 
     swap = [(0, 1), (1, 0)]
@@ -688,12 +766,14 @@
     sib0 = across(payload)
     hop2 = lax.ppermute(hop1, "z", hop)
     sib1 = across(hop1)
+    far = across(sent)
+    slope_other = across(slope)
     origin, keep = run(0, [local])
     hop2, origin = lax.optimization_barrier((hop2, origin))
     hop3 = lax.ppermute(hop2, "z", hop)
     sib2 = across(hop2)
     (carry1,) = run(1, [local, sib1, sib0, hop1, origin])
-    hop3, carry1 = lax.optimization_barrier((hop3, carry1))
+    hop3, carry1, far, slope_other = lax.optimization_barrier((hop3, carry1, far, slope_other))
     hop4 = lax.ppermute(hop3, "z", hop)
     sib3 = across(hop3)
     (carry2,) = run(2, [local, sib2, sib1, hop2, origin, carry1])
@@ -710,14 +790,14 @@
     ]
 
     student, grads, grad_gain, small = pl.pallas_call(
-        functools.partial(backward_kernel, kv, heads, groups, features, row_total),
+        functools.partial(backward_kernel, kv, heads, len(all_stats), features, row_total),
         out_shape=[
             shape((rows, width), BF16),
             shape((blocks, heads, 128)),
             shape((1, width)),
             shape((8, 128)),
         ],
-        in_specs=vmem(4 + groups),
+        in_specs=vmem(5 + len(all_stats)),
         out_specs=vmem(4),
         scratch_shapes=[
             pltpu.VMEM((rows, 128), F32),
@@ -730,27 +810,41 @@
         ],
         compiler_params=SMALL,
         name="backward",
-    )(local, keep, real, half, *all_stats)
-
-    grads = lax.all_to_all(grads, ("z", "core"), 0, 0, tiled=True)
+    )(local, keep, carry2, real, half, *all_stats)
+
+    grads = lax.all_to_all(grads.reshape(chips, 2 * heads, 128), "z", 0, 0, tiled=True)
+    folded = pl.pallas_call(
+        fold_kernel,
+        out_shape=shape((3 * heads + 8, 128)),
+        in_specs=vmem(3),
+        out_specs=pl.BlockSpec(memory_space=pltpu.VMEM),
+        compiler_params=SMALL,
+        name="fold",
+    )(grads, grad_gain, small)
 
     axes = ("z", "dp")
     count = chips * lax.axis_size("dp")
-    part = shape((count * (heads + 1), 128))
-    keep, send = pl.pallas_call(
+    half = pl.pallas_call(
         weight_kernel,
-        out_shape=[part, part],
-        in_specs=vmem(5),
-        out_specs=vmem(2),
+        out_shape=shape((count * (heads + 2), 128), BF16),
+        in_specs=vmem(6),
+        out_specs=pl.BlockSpec(memory_space=pltpu.VMEM),
+        scratch_shapes=[pltpu.VMEM((count * (heads + 2), 128), F32)],
         compiler_params=SMALL,
         name="weights",
-    )(slope, hidden, grad_gain, small, grads)
-
-    half = keep + lax.ppermute(send, "core", swap)
-    half = half.reshape(count, heads + 1, 1, 128)
+    )(folded, across(folded), slope, slope_other, hidden, far)
+    half = half.reshape(count, (heads + 2) // 2, 2, 128)
     got = lax.all_to_all(half, axes, 0, 0, tiled=True)
-    summed = jnp.sum(got, axis=0)
-    spread = jnp.broadcast_to(summed[None], got.shape)
+    spread = pl.pallas_call(
+        functools.partial(spread_kernel, count),
+        out_shape=shape((count * (heads + 1), 128)),
+        in_specs=vmem(1),
+        out_specs=pl.BlockSpec(memory_space=pltpu.VMEM),
+        scratch_shapes=[pltpu.VMEM((count * (heads + 2), 128), F32)],
+        compiler_params=SMALL,
+        name="spread",
+    )(got.reshape(count * (heads + 2), 128))
+    spread = spread.reshape(count, heads + 1, 1, 128)
     mine = lax.all_to_all(spread, axes, 0, 0, tiled=True)
     mine = mine.reshape(count * (heads + 1), 128)
     other = lax.ppermute(mine, "core", swap)

time: 113 us -> 110 us (0.973)
  blocking collectives: 47.9 us -> 41.3 us
  starting transfers between devices: 16.1 us -> 22.2 us
  waiting for transfers between devices: 16.7 us -> 15 us
  Pallas kernels: 30.3 us -> 29.1 us
    ppermute x5 -> x8, starting transfers between devices: 6.14 us -> 14.8 us  [across(): return lax.ppermute(part, 'core', swap)]
    all_to_all x1, blocking collectives: 16.2 us -> 12.9 us  [body(): lax.all_to_all(grads.reshape(chips, 2 * heads, 128), 'z', 0, 0, tiled=True)]
    all_to_all x1, blocking collectives: 16.6 us -> 13.8 us  [body(): got = lax.all_to_all(half, axes, 0, 0, tiled=True)]
    ppermute x1, starting transfers between devices: 2.46 us -> 0.01 us  [body(): hop1 = lax.ppermute(payload, 'z', hop)]
    pallas_call x5, Pallas kernels: 17.9 us -> 15.6 us  [forward(): pl.pallas_call(functools.partial(forward_kernel, kv, heads, part), out_sh...]
    pallas_call x1, Pallas kernels: 3.56 us -> 5.47 us  [body(): pl.pallas_call(functools.partial(prep_kernel, kv), out_shape=[shape((carg...]
    ppermute x1, waiting for transfers between devices: 2.51 us -> 0.76 us  [body(): hop3 = lax.ppermute(hop2, 'z', hop)]
    ppermute x1 -> x0, waiting for transfers between devices: 1.55 us -> none  [body(): half = keep + lax.ppermute(send, 'core', swap)]
  transfers between devices with their start and end apart: 14 -> 16, of which waited for: 7 -> 7; matrix products, arithmetic and copies ran while one was open for 0% -> 0% of each run, Pallas kernels for 11% -> 10%
where the time goes in v4:
time: 110 us; the launch traced here: 109 us
  blocking collectives  41.3 us (38%)
  Pallas kernels  29.1 us (26%)
  starting transfers between devices  22.2 us (20%)
  waiting for transfers between devices  15 us (14%)
  local copies, waits for them, and re-layouts  1.12 us (1%)
    pallas_call x5, Pallas kernels, forward(): pl.pallas_call(functools.partial(forward_kernel, kv, heads, part), out_sh...  15.6 us
    ppermute x8, starting transfers between devices, across(): return lax.ppermute(part, 'core', swap)  14.8 us
    all_to_all x1, blocking collectives, body(): mine = lax.all_to_all(spread, axes, 0, 0, tiled=True)  14.7 us
    all_to_all x1, blocking collectives, body(): got = lax.all_to_all(half, axes, 0, 0, tiled=True)  13.8 us
    all_to_all x1, blocking collectives, body(): lax.all_to_all(grads.reshape(chips, 2 * heads, 128), 'z', 0, 0, tiled=True)  12.9 us
    ppermute x1, waiting for transfers between devices, body(): hop1 = lax.ppermute(payload, 'z', hop)  8.09 us
    pallas_call x1, Pallas kernels, body(): pl.pallas_call(functools.partial(backward_kernel, kv, heads, len(all_stat...  6.49 us
    pallas_call x1, Pallas kernels, body(): pl.pallas_call(functools.partial(prep_kernel, kv), out_shape=[shape((carg...  5.47 us
  transfers between devices with their start and end apart: 16, of which 7 were waited for; matrix products, arithmetic and copies ran while one was open for 0% of the time, Pallas kernels for 10%

profile of v4, /device:TPU:1, one launch (start us, length us, event | category | flops | bytes accessed | tf_op | source)
XLA Modules:
  0.0 109.5 jit_solution(5790434702070694722)
XLA Ops:
  0.6 5.5 %prep.1 = (bf16[560,128]{1,0:T(8,128)(2,1)}, f32[16,128]{1,0:T(8,128)}, bf16[2800,128]{1,0:T(8,128)(2,1)}, bf16[128,4096]{1,0:T(8,128)(2,1)}) custom-call(s32[1,4]{1,0:T(1,128)} %lengths.1, f32[16]{0:T(128)} %bias.1, f32[16]{0:T(128)} %decay.1, f32[16]{0:T(128)} %skip.1, f32[1,2048]{1,0:T(1,128)} %bitcast.29, bf16[128,8192]{1,0:T(8,128)(2,1)} %bitcast.17, ...), custom_call_target="tpu_custom_call" | custom-call | tf_op jit(solution)/shard_map/prep/pallas_call | solution.py:733
  6.1 3.3 %collective-permute-start.5 = (bf16[128,4096]{1,0:T(8,128)(2,1)}, bf16[128,4096]{1,0:T(8,128)(2,1)S(1)}, u32[]{:S(2)}, u32[]{:S(2)}) collective-permute-start(bf16[128,4096]{1,0:T(8,128)(2,1)} %get-tuple-element.38), channel_id=1, source_target_pairs={{0,16},{16,0},{1,17},{17,1},{2,18},{18,2},{3,19},{19,3},{4,20},{20... | collective-permute-start | bytes 3145736 | tf_op jit(solution)/shard_map/ppermute | solution.py:763
  9.4 0.0 collective-permute-start
  9.4 8.1 %collective-permute-done.refs_3_ = bf16[560,128]{1,0:T(8,128)(2,1)S(1)} collective-permute-done((bf16[560,128]{1,0:T(8,128)(2,1)}, bf16[560,128]{1,0:T(8,128)(2,1)S(1)}, u32[]{:S(2)}, u32[]{:S(2)}) %collective-permute-start) | collective-permute-done | bytes 143392 | tf_op jit(solution)/shard_map/ppermute | solution.py:765
  17.5 0.0 collective-permute-start.1
  17.5 0.7 collective-permute-start.4
  18.2 0.0 collective-permute-start.3
  18.2 0.0 copy-start
  18.2 1.1 %copy-done = bf16[2800,128]{1,0:T(8,128)(2,1)S(1)} copy-done((bf16[2800,128]{1,0:T(8,128)(2,1)S(1)}, bf16[2800,128]{1,0:T(8,128)(2,1)}, u32[]{:S(2)}) %copy-start) | copy-done | bytes 716824
  19.3 2.9 %forward_a.1 = (f32[6400,128]{1,0:T(8,128)S(1)}, f32[4864,128]{1,0:T(8,128)S(1)}) custom-call(bf16[2800,128]{1,0:T(8,128)(2,1)S(1)} %copy-done), custom_call_target="tpu_custom_call" | custom-call | flops 402653184 | bytes 3145728 | tf_op jit(solution)/shard_map/forward_a/pallas_call | solution.py:494
  22.3 1.1 %collective-permute-done.1.refs_3_ = bf16[560,128]{1,0:T(8,128)(2,1)S(1)} collective-permute-done((bf16[560,128]{1,0:T(8,128)(2,1)S(1)}, bf16[560,128]{1,0:T(8,128)(2,1)S(1)}, u32[]{:S(2)}, u32[]{:S(2)}) %collective-permute-start.1) | collective-permute-done | bytes 143392 | tf_op jit(solution)/shard_map/ppermute | solution.py:767
  23.4 0.0 collective-permute-start.2
  23.4 1.5 %collective-permute-start.6 = (f32[16,128]{1,0:T(8,128)}, f32[16,128]{1,0:T(8,128)S(1)}, u32[]{:S(2)}, u32[]{:S(2)}) collective-permute-start(f32[16,128]{1,0:T(8,128)} %get-tuple-element.39.slope), channel_id=1, source_target_pairs={{0,16},{16,0},{1,17},{17,1},{2,18},{18,2},{3,19},{19,3},{4,20},{20... | collective-permute-start | bytes 24584 | tf_op jit(solution)/shard_map/ppermute | solution.py:763
  24.9 0.0 collective-permute-done.4.refs_2_
  24.9 0.1 collective-permute-start.8
  25.0 0.0 collective-permute-done.3.refs_1_.refs_2_
  25.0 2.7 %forward_b.1.refs_5_ = f32[9344,128]{1,0:T(8,128)S(1)} custom-call(bf16[2800,128]{1,0:T(8,128)(2,1)S(1)} %copy-done, bf16[560,128]{1,0:T(8,128)(2,1)S(1)} %collective-permute-done.3.refs_1_.refs_2_, bf16[560,128]{1,0:T(8,128)(2,1)S(1)} %collective-permute-done.4.refs_2_, bf16[560,128]{1,0:T(8,128)(2,1)S(1)} %collective-permute-done.refs_3_, ...), custom_call_target="tpu_custom_call" | custom-call | flops 805306368 | bytes 6291456 | tf_op jit(solution)/shard_map/forward_b/pallas_call | solution.py:494
  27.8 0.0 collective-permute-done.6.slope_other
  27.8 0.8 collective-permute-done.2.refs_3_
  28.5 0.0 collective-permute-done.5.far
  28.5 0.0 collective-permute-start.7
  28.5 2.7 %collective-permute-start.10 = (bf16[560,128]{1,0:T(8,128)(2,1)S(1)}, bf16[560,128]{1,0:T(8,128)(2,1)S(1)}, u32[]{:S(2)}, u32[]{:S(2)}) collective-permute-start(bf16[560,128]{1,0:T(8,128)(2,1)S(1)} %collective-permute-done.2.refs_3_), channel_id=1, source_target_pairs={{0,16},{16,0},{1,17},{17,1},{2,18},{18,2},{3,19},{19,3},{4,20},{20... | collective-permute-start | bytes 430088 | tf_op jit(solution)/shard_map/ppermute | solution.py:763
  31.2 0.0 collective-permute-done.8.refs_1_.refs_2_
  31.2 2.9 %forward_c.1.refs_6_.refs_2_ = f32[11392,128]{1,0:T(8,128)S(1)} custom-call(bf16[2800,128]{1,0:T(8,128)(2,1)S(1)} %copy-done, bf16[560,128]{1,0:T(8,128)(2,1)S(1)} %collective-permute-done.8.refs_1_.refs_2_, bf16[560,128]{1,0:T(8,128)(2,1)S(1)} %collective-permute-done.3.refs_1_.refs_2_, bf16[560,128]{1,0:T(8,128)(2,1)S(1)} %collective-permute-done.1.refs_3_, ...), custom_call_target="tpu_custom_call" | custom-call | flops 805306368 | bytes 6291456 | tf_op jit(solution)/shard_map/forward_c/pallas_call | solution.py:494
  34.2 0.0 collective-permute-done.7.refs_3_
  34.2 3.3 %collective-permute-start.9 = (bf16[560,128]{1,0:T(8,128)(2,1)S(1)}, bf16[560,128]{1,0:T(8,128)(2,1)S(1)}, u32[]{:S(2)}, u32[]{:S(2)}) collective-permute-start(bf16[560,128]{1,0:T(8,128)(2,1)S(1)} %collective-permute-done.7.refs_3_), channel_id=1, source_target_pairs={{0,16},{16,0},{1,17},{17,1},{2,18},{18,2},{3,19},{19,3},{4,20},{20... | collective-permute-start | bytes 430088 | tf_op jit(solution)/shard_map/ppermute | solution.py:763
  37.5 0.0 collective-permute-done.10.refs_1_.refs_2_
  37.5 2.3 %forward_d.1.refs_7_ = f32[9344,128]{1,0:T(8,128)S(1)} custom-call(bf16[2800,128]{1,0:T(8,128)(2,1)S(1)} %copy-done, bf16[560,128]{1,0:T(8,128)(2,1)S(1)} %collective-permute-done.10.refs_1_.refs_2_, bf16[560,128]{1,0:T(8,128)(2,1)S(1)} %collective-permute-done.8.refs_1_.refs_2_, bf16[560,128]{1,0:T(8,128)(2,1)S(1)} %collective-permute-done.2.refs_3_, ...), custom_call_target="tpu_custom_call" | custom-call | flops 805306368 | bytes 6291456 | tf_op jit(solution)/shard_map/forward_d/pallas_call | solution.py:494
  39.9 0.0 collective-permute-done.9.refs_1_
  39.9 4.6 %forward_e.1 = (f32[6912,128]{1,0:T(8,128)S(1)}, bf16[4352,128]{1,0:T(8,128)(2,1)S(1)}, f32[8,128]{1,0:T(8,128)S(1)}) custom-call(bf16[2800,128]{1,0:T(8,128)(2,1)S(1)} %copy-done, bf16[560,128]{1,0:T(8,128)(2,1)S(1)} %collective-permute-done.9.refs_1_, bf16[560,128]{1,0:T(8,128)(2,1)S(1)} %collective-permute-done.10.refs_1_.refs_2_, ...), custom_call_target="tpu_custom_call" | custom-call | flops 805306368 | bytes 6291456 | tf_op jit(solution)/shard_map/forward_e/pallas_call | solution.py:494
  44.5 2.8 %collective-permute-start.13 = (f32[8,128]{1,0:T(8,128)S(1)}, f32[8,128]{1,0:T(8,128)S(1)}, u32[]{:S(2)}, u32[]{:S(2)}) collective-permute-start(f32[8,128]{1,0:T(8,128)S(1)} %get-tuple-element.46.refs_5_), channel_id=1, source_target_pairs={{0,12},{4,0},{8,4},{12,8},{1,13},{5,1},{9,5},{13,9},{2,14},{6,2},{... | collective-permute-start | bytes 12296 | tf_op jit(solution)/shard_map/ppermute | solution.py:788
  47.3 0.3 collective-permute-start.12
  47.7 0.7 collective-permute-start.11
  48.4 0.0 collective-permute-done.13.refs_8_
  48.4 2.9 %collective-permute-done.12.refs_7_ = f32[8,128]{1,0:T(8,128)S(1)} collective-permute-done((f32[8,128]{1,0:T(8,128)S(1)}, f32[8,128]{1,0:T(8,128)S(1)}, u32[]{:S(2)}, u32[]{:S(2)}) %collective-permute-start.12) | collective-permute-done | bytes 4128 | tf_op jit(solution)/shard_map/ppermute | solution.py:788
  51.3 0.1 collective-permute-done.11.refs_6_
  51.3 0.0 copy-start.1
  51.3 0.0 copy-start.2
  51.3 6.5 %backward.1 = (bf16[128,2048]{1,0:T(8,128)(2,1)}, f32[16,16,128]{2,1,0:T(8,128)S(1)}, f32[1,2048]{1,0:T(1,128)S(1)}, f32[8,128]{1,0:T(8,128)S(1)}) custom-call(bf16[2800,128]{1,0:T(8,128)(2,1)S(1)} %copy-done, f32[4864,128]{1,0:T(8,128)S(1)} %get-tuple-element.33.refs_8_.refs_1_, f32[11392,128]{1,0:T(8,128)S(1)} %forward_c.1.refs_6_.refs_2_, ...), custom_call_target="tpu_custom_call" | custom-call | tf_op jit(solution)/shard_map/backward/pallas_call | solution.py:792
  57.8 12.9 %all_to_all.15.grads = f32[8,32,128]{2,1,0:T(8,128)S(1)} all-to-all(f32[8,32,128]{2,1,0:T(8,128)S(1)} %bitcast.24), channel_id=1, replica_groups=mesh['z'=8,'core'=2,'grp'=4,'dp'=4] {'z'}, dimensions={0} | all-to-all | bytes 262144 | tf_op jit(solution)/shard_map/all_to_all | solution.py:815
  70.8 3.1 %collective-permute-start.14 = (f32[56,128]{1,0:T(8,128)S(1)}, f32[56,128]{1,0:T(8,128)S(1)}, u32[]{:S(2)}, u32[]{:S(2)}) collective-permute-start(f32[56,128]{1,0:T(8,128)S(1)} %fold.1.own), channel_id=1, source_target_pairs={{0,16},{16,0},{1,17},{17,1},{2,18},{18,2},{3,19},{19,3},{4,20},{20... | collective-permute-start | bytes 86024 | tf_op jit(solution)/shard_map/ppermute | solution.py:763
  73.9 0.9 collective-permute-done.14.other
  74.7 0.0 copy-done.1
  74.7 0.0 copy-done.2
  74.8 0.7 weights.1
  75.4 13.8 %all_to_all.16 = bf16[32,9,2,128]{3,2,1,0:T(2,128)(2,1)S(1)} all-to-all(bf16[32,9,2,128]{3,2,1,0:T(2,128)(2,1)S(1)} %bitcast.22), channel_id=1, replica_groups=mesh['z'=8,'core'=2,'grp'=4,'dp'=4] {'z','dp'}, dimensions={0} | all-to-all | bytes 294912 | tf_op jit(solution)/shard_map/all_to_all | solution.py:837
  89.2 0.1 spread.1
  89.3 14.7 %all_to_all.17 = f32[32,17,1,128]{3,2,1,0:T(1,128)S(1)} all-to-all(f32[32,17,1,128]{3,2,1,0:T(1,128)S(1)} %bitcast.21), channel_id=1, replica_groups=mesh['z'=8,'core'=2,'grp'=4,'dp'=4] {'z','dp'}, dimensions={0} | all-to-all | bytes 557056 | tf_op jit(solution)/shard_map/all_to_all | solution.py:848
  103.9 3.5 %collective-permute-start.15 = (f32[544,128]{1,0:T(8,128)S(1)}, f32[544,128]{1,0:T(8,128)S(1)}, u32[]{:S(2)}, u32[]{:S(2)}) collective-permute-start(f32[544,128]{1,0:T(8,128)S(1)} %bitcast.19), channel_id=1, source_target_pairs={{0,16},{16,0},{1,17},{17,1},{2,18},{18,2},{3,19},{19,3},{4,20},{20... | collective-permute-start | bytes 835592 | tf_op jit(solution)/shard_map/ppermute | solution.py:850
  107.4 1.2 %collective-permute-done.15.other = f32[544,128]{1,0:T(8,128)S(1)} collective-permute-done((f32[544,128]{1,0:T(8,128)S(1)}, f32[544,128]{1,0:T(8,128)S(1)}, u32[]{:S(2)}, u32[]{:S(2)}) %collective-permute-start.15) | collective-permute-done | bytes 278560 | tf_op jit(solution)/shard_map/ppermute | solution.py:850
  108.6 0.8 finish.1
  (1 shorter events, 0.0 us)
Async XLA Ops:
  6.1 22.4 %collective-permute-start.5 = (bf16[128,4096]{1,0:T(8,128)(2,1)}, bf16[128,4096]{1,0:T(8,128)(2,1)S(1)}, u32[]{:S(2)}, u32[]{:S(2)}) collective-permute-start(bf16[128,4096]{1,0:T(8,128)(2,1)} %get-tuple-element.38), channel_id=1, source_target_pairs={{0,16},{16,0},{1,17},{17,1},{2,18},{18,2},{3,19},{19,3},{4,20},{20... | collective-permute-start | bytes 3145736 | tf_op jit(solution)/shard_map/ppermute | solution.py:763
  9.4 8.1 %collective-permute-start = (bf16[560,128]{1,0:T(8,128)(2,1)}, bf16[560,128]{1,0:T(8,128)(2,1)S(1)}, u32[]{:S(2)}, u32[]{:S(2)}) collective-permute-start(bf16[560,128]{1,0:T(8,128)(2,1)} %get-tuple-element.34), channel_id=1, source_target_pairs={{0,32},{32,64},{64,96},{96,128},{128,160},{160,192},{192,224},{224... | collective-permute-start | bytes 430088 | tf_op jit(solution)/shard_map/ppermute | solution.py:765
  17.5 5.8 %collective-permute-start.1 = (bf16[560,128]{1,0:T(8,128)(2,1)S(1)}, bf16[560,128]{1,0:T(8,128)(2,1)S(1)}, u32[]{:S(2)}, u32[]{:S(2)}) collective-permute-start(bf16[560,128]{1,0:T(8,128)(2,1)S(1)} %collective-permute-done.refs_3_), channel_id=1, source_target_pairs={{0,32},{32,64},{64,96},{96,128},{128,160},{160,192},{192,224},{224... | collective-permute-start | bytes 430088 | tf_op jit(solution)/shard_map/ppermute | solution.py:767
  17.5 7.4 %collective-permute-start.4 = (bf16[560,128]{1,0:T(8,128)(2,1)}, bf16[560,128]{1,0:T(8,128)(2,1)S(1)}, u32[]{:S(2)}, u32[]{:S(2)}) collective-permute-start(bf16[560,128]{1,0:T(8,128)(2,1)} %get-tuple-element.34), channel_id=1, source_target_pairs={{0,16},{16,0},{1,17},{17,1},{2,18},{18,2},{3,19},{19,3},{4,20},{20... | collective-permute-start | bytes 430088 | tf_op jit(solution)/shard_map/ppermute | solution.py:763
  18.2 6.8 %collective-permute-start.3 = (bf16[560,128]{1,0:T(8,128)(2,1)S(1)}, bf16[560,128]{1,0:T(8,128)(2,1)S(1)}, u32[]{:S(2)}, u32[]{:S(2)}) collective-permute-start(bf16[560,128]{1,0:T(8,128)(2,1)S(1)} %collective-permute-done.refs_3_), channel_id=1, source_target_pairs={{0,16},{16,0},{1,17},{17,1},{2,18},{18,2},{3,19},{19,3},{4,20},{20... | collective-permute-start | bytes 430088 | tf_op jit(solution)/shard_map/ppermute | solution.py:763
  18.2 1.1 %copy-start = (bf16[2800,128]{1,0:T(8,128)(2,1)S(1)}, bf16[2800,128]{1,0:T(8,128)(2,1)}, u32[]{:S(2)}) copy-start(bf16[2800,128]{1,0:T(8,128)(2,1)} %get-tuple-element.32.refs_0_) | copy-start | bytes 2150404
  23.4 5.2 %collective-permute-start.2 = (bf16[560,128]{1,0:T(8,128)(2,1)S(1)}, bf16[560,128]{1,0:T(8,128)(2,1)S(1)}, u32[]{:S(2)}, u32[]{:S(2)}) collective-permute-start(bf16[560,128]{1,0:T(8,128)(2,1)S(1)} %collective-permute-done.1.refs_3_), channel_id=1, source_target_pairs={{0,32},{32,64},{64,96},{96,128},{128,160},{160,192},{192,224},{224... | collective-permute-start | bytes 430088 | tf_op jit(solution)/shard_map/ppermute | solution.py:773
  23.4 4.4 %collective-permute-start.6 = (f32[16,128]{1,0:T(8,128)}, f32[16,128]{1,0:T(8,128)S(1)}, u32[]{:S(2)}, u32[]{:S(2)}) collective-permute-start(f32[16,128]{1,0:T(8,128)} %get-tuple-element.39.slope), channel_id=1, source_target_pairs={{0,16},{16,0},{1,17},{17,1},{2,18},{18,2},{3,19},{19,3},{4,20},{20... | collective-permute-start | bytes 24584 | tf_op jit(solution)/shard_map/ppermute | solution.py:763
  24.9 6.3 %collective-permute-start.8 = (bf16[560,128]{1,0:T(8,128)(2,1)S(1)}, bf16[560,128]{1,0:T(8,128)(2,1)S(1)}, u32[]{:S(2)}, u32[]{:S(2)}) collective-permute-start(bf16[560,128]{1,0:T(8,128)(2,1)S(1)} %collective-permute-done.1.refs_3_), channel_id=1, source_target_pairs={{0,16},{16,0},{1,17},{17,1},{2,18},{18,2},{3,19},{19,3},{4,20},{20... | collective-permute-start | bytes 430088 | tf_op jit(solution)/shard_map/ppermute | solution.py:763
  28.5 5.7 %collective-permute-start.7 = (bf16[560,128]{1,0:T(8,128)(2,1)S(1)}, bf16[560,128]{1,0:T(8,128)(2,1)S(1)}, u32[]{:S(2)}, u32[]{:S(2)}) collective-permute-start(bf16[560,128]{1,0:T(8,128)(2,1)S(1)} %collective-permute-done.2.refs_3_), channel_id=1, source_target_pairs={{0,32},{32,64},{64,96},{96,128},{128,160},{160,192},{192,224},{224... | collective-permute-start | bytes 430088 | tf_op jit(solution)/shard_map/ppermute | solution.py:777
  28.5 9.0 %collective-permute-start.10 = (bf16[560,128]{1,0:T(8,128)(2,1)S(1)}, bf16[560,128]{1,0:T(8,128)(2,1)S(1)}, u32[]{:S(2)}, u32[]{:S(2)}) collective-permute-start(bf16[560,128]{1,0:T(8,128)(2,1)S(1)} %collective-permute-done.2.refs_3_), channel_id=1, source_target_pairs={{0,16},{16,0},{1,17},{17,1},{2,18},{18,2},{3,19},{19,3},{4,20},{20... | collective-permute-start | bytes 430088 | tf_op jit(solution)/shard_map/ppermute | solution.py:763
  34.2 5.7 %collective-permute-start.9 = (bf16[560,128]{1,0:T(8,128)(2,1)S(1)}, bf16[560,128]{1,0:T(8,128)(2,1)S(1)}, u32[]{:S(2)}, u32[]{:S(2)}) collective-permute-start(bf16[560,128]{1,0:T(8,128)(2,1)S(1)} %collective-permute-done.7.refs_3_), channel_id=1, source_target_pairs={{0,16},{16,0},{1,17},{17,1},{2,18},{18,2},{3,19},{19,3},{4,20},{20... | collective-permute-start | bytes 430088 | tf_op jit(solution)/shard_map/ppermute | solution.py:763
  44.5 3.9 %collective-permute-start.13 = (f32[8,128]{1,0:T(8,128)S(1)}, f32[8,128]{1,0:T(8,128)S(1)}, u32[]{:S(2)}, u32[]{:S(2)}) collective-permute-start(f32[8,128]{1,0:T(8,128)S(1)} %get-tuple-element.46.refs_5_), channel_id=1, source_target_pairs={{0,12},{4,0},{8,4},{12,8},{1,13},{5,1},{9,5},{13,9},{2,14},{6,2},{... | collective-permute-start | bytes 12296 | tf_op jit(solution)/shard_map/ppermute | solution.py:788
  47.3 4.0 %collective-permute-start.12 = (f32[8,128]{1,0:T(8,128)S(1)}, f32[8,128]{1,0:T(8,128)S(1)}, u32[]{:S(2)}, u32[]{:S(2)}) collective-permute-start(f32[8,128]{1,0:T(8,128)S(1)} %get-tuple-element.46.refs_5_), channel_id=1, source_target_pairs={{0,8},{4,12},{8,0},{12,4},{1,9},{5,13},{9,1},{13,5},{2,10},{6,14},... | collective-permute-start | bytes 12296 | tf_op jit(solution)/shard_map/ppermute | solution.py:788
  47.7 3.7 %collective-permute-start.11 = (f32[8,128]{1,0:T(8,128)S(1)}, f32[8,128]{1,0:T(8,128)S(1)}, u32[]{:S(2)}, u32[]{:S(2)}) collective-permute-start(f32[8,128]{1,0:T(8,128)S(1)} %get-tuple-element.46.refs_5_), channel_id=1, source_target_pairs={{0,4},{4,8},{8,12},{12,0},{1,5},{5,9},{9,13},{13,1},{2,6},{6,10},{... | collective-permute-start | bytes 12296 | tf_op jit(solution)/shard_map/ppermute | solution.py:788
  51.3 23.4 %copy-start.1 = (bf16[1,128,8192]{2,1,0:T(8,128)(2,1)S(1)}, bf16[1,128,8192]{2,1,0:T(8,128)(2,1)}, u32[]{:S(2)}) copy-start(bf16[1,128,8192]{2,1,0:T(8,128)(2,1)} %param.10) | copy-start | bytes 6291460
  51.3 23.4 %copy-start.2 = (f32[16,128]{1,0:T(8,128)S(1)}, f32[16,128]{1,0:T(8,128)}, u32[]{:S(2)}) copy-start(f32[16,128]{1,0:T(8,128)} %get-tuple-element.39.slope) | copy-start | bytes 24580
  70.8 4.0 %collective-permute-start.14 = (f32[56,128]{1,0:T(8,128)S(1)}, f32[56,128]{1,0:T(8,128)S(1)}, u32[]{:S(2)}, u32[]{:S(2)}) collective-permute-start(f32[56,128]{1,0:T(8,128)S(1)} %fold.1.own), channel_id=1, source_target_pairs={{0,16},{16,0},{1,17},{17,1},{2,18},{18,2},{3,19},{19,3},{4,20},{20... | collective-permute-start | bytes 86024 | tf_op jit(solution)/shard_map/ppermute | solution.py:763
  103.9 4.7 %collective-permute-start.15 = (f32[544,128]{1,0:T(8,128)S(1)}, f32[544,128]{1,0:T(8,128)S(1)}, u32[]{:S(2)}, u32[]{:S(2)}) collective-permute-start(f32[544,128]{1,0:T(8,128)S(1)} %bitcast.19), channel_id=1, source_target_pairs={{0,16},{16,0},{1,17},{17,1},{2,18},{18,2},{3,19},{19,3},{4,20},{20... | collective-permute-start | bytes 835592 | tf_op jit(solution)/shard_map/ppermute | solution.py:850

commit v5 on v4

--- a/solution.py
+++ b/solution.py
@@ -83,46 +83,23 @@
     decay,
     skip,
     gain,
-    hidden_far,
-    queries,
+    hidden,
     weight,
     keys,
     values,
+    queries,
     payload,
     slope,
     local,
-    sent,
     consts,
-    hidden,
-    asked,
-    stage,
-    fetched,
-    moved,
 ):
     heads = weight.shape[0]
-    side = sent.shape[1]
-    at = local_rows(heads, kv)[0]
-    chunks = fetched.shape[0]
-    width = hidden.shape[1] // chunks
-    fetches = []
-    for i in range(chunks):
-        part = slice(width * i, width * (i + 1))
-        fetch = pltpu.make_async_copy(hidden_far.at[:, part], hidden.at[:, part], fetched.at[i])
-        fetch.start()
-        fetches.append(fetch)
-    ask = pltpu.make_async_copy(queries, asked, moved.at[0])
-    ask.start()
-    pre = jnp.zeros((hidden.shape[0], heads), F32)
-    for i in range(chunks):
-        part = slice(width * i, width * (i + 1))
-        fetches[i].wait()
-        pre = pre + lax.dot_general(
-            hidden[:, part], weight[:, part], (((1,), (1,)), ((), ())), preferred_element_type=F32
-        )
-    other = pl.multiple_of((1 - lax.axis_index("core")) * side, side)
-    give = pltpu.make_async_copy(hidden.at[:, pl.ds(other, side)], sent, moved.at[1])
-    give.start()
-    pre = pre.T + column_of(bias, heads)
+    pre = (
+        lax.dot_general(
+            hidden[...], weight[...], (((1,), (1,)), ((), ())), preferred_element_type=F32
+        ).T
+        + column_of(bias, heads)
+    )
     step = jnp.maximum(pre, 0.0) + jnp.log1p(jnp.exp(-jnp.abs(pre)))
     slope[...] = 1.0 / (1.0 + jnp.exp(-pre))
     for g in range(kv):
@@ -147,19 +124,15 @@
         piece = step.astype(BF16)
         payload[first + part * heads : first + (part + 1) * heads, :] = piece
         step = step - piece.astype(F32)
-    stage[at[1] : at[1] + payload.shape[0], :] = payload[...]
+    at = local_rows(heads, kv)[0]
+    for h in range(heads):
+        local[at[0] + 128 * h : at[0] + 128 * h + 128, :] = queries[:, 128 * h : 128 * h + 128]
+    local[at[1] : at[1] + payload.shape[0], :] = payload[...]
     rest = consts[...]
     for part in range(3):
         piece = rest.astype(BF16)
-        stage[at[2 + part] : at[2 + part] + rest.shape[0], :] = piece
+        local[at[2 + part] : at[2 + part] + rest.shape[0], :] = piece
         rest = rest - piece.astype(F32)
-    ask.wait()
-    for h in range(heads):
-        stage[at[0] + 128 * h : at[0] + 128 * h + 128, :] = asked[:, 128 * h : 128 * h + 128]
-    put = pltpu.make_async_copy(stage, local, moved.at[2])
-    put.start()
-    give.wait()
-    put.wait()
 
 
 def masks(info):
@@ -451,7 +424,7 @@
             acc[2] += gained * teach.astype(F32)
         return unused
 
-    lax.fori_loop(0, heads, one_head, 0, unroll=(8, 4, 4, 8, 16)[part])
+    lax.fori_loop(0, heads, one_head, 0, unroll=(16, 8, 8, 16, 16)[part])
     if last:
         stats[...] = jnp.concatenate(
             [to_row(acc[0]), to_row(acc[1]), to_row(acc[2]), jnp.zeros((5, 128), F32)], axis=0
@@ -621,7 +594,7 @@
     near_pre = jnp.where(low_core, top, bottom) * near_slope
     far_pre = jnp.where(low_core, bottom, top) * far_slope
     near_low, far_low = near_pre.astype(BF16), far_pre.astype(BF16)
-    side = far.shape[1]
+    side = far.shape[1] // 2
     count = side // 128
     tiles = total.shape[0] - 2 * heads - 8
     lines = [total[2 * heads + i : 2 * heads + i + 1] for i in range(tiles)]
@@ -630,9 +603,9 @@
     lines += [total[base + 1 : base + 2], total[base : base + 1]]
     for j in range(count):
         start = j * (heads + 2)
-        near = hidden[:, pl.ds(pl.multiple_of(core * side + 128 * j, 128), 128)]
-        wide[start : start + heads, :] = mm(near_low, near) + mm(
-            far_low, far[:, 128 * j : 128 * j + 128]
+        cols = pl.ds(pl.multiple_of(core * side + 128 * j, 128), 128)
+        wide[start : start + heads, :] = mm(near_low, hidden[:, cols]) + mm(
+            far_low, far[:, cols]
         )
         line = jnp.zeros((1, 128), F32)
         if j < len(lines):
@@ -691,10 +664,6 @@
 
 def smem(count):
     return [pl.BlockSpec(memory_space=pltpu.SMEM)] * count
-
-
-def anywhere(count):
-    return [pl.BlockSpec(memory_space=pl.ANY)] * count
 
 
 def shape(dims, kind=F32):
@@ -730,29 +699,21 @@
     gain = norm_gain[None, :]
     cargo = 2 * kv * HDIM + 3 * heads
 
-    payload, slope, local, sent = pl.pallas_call(
+    payload, slope, local = pl.pallas_call(
         functools.partial(prep_kernel, kv),
         out_shape=[
             shape((cargo, 128), BF16),
             shape((heads, 128)),
             shape((local_rows(heads, kv)[1], 128), BF16),
-            shape((rows, depth // 2), BF16),
         ],
-        in_specs=smem(4) + vmem(1) + anywhere(2) + vmem(3),
-        out_specs=vmem(2) + anywhere(2),
-        scratch_shapes=[
-            pltpu.VMEM((const_rows(heads), 128), F32),
-            pltpu.VMEM((rows, depth), BF16),
-            pltpu.VMEM((rows, width), BF16),
-            pltpu.VMEM((local_rows(heads, kv)[1], 128), BF16),
-            pltpu.SemaphoreType.DMA((4,)),
-            pltpu.SemaphoreType.DMA((3,)),
-        ],
+        in_specs=smem(4) + vmem(6),
+        out_specs=vmem(3),
+        scratch_shapes=[pltpu.VMEM((const_rows(heads), 128), F32)],
         compiler_params=LARGE,
         name="prep",
     )(
-        doc_lengths, dt_bias, decay_log, skip_gain, gain, hidden, teacher_queries[0],
-        dt_weight.T, teacher_keys[0], teacher_values[0],
+        doc_lengths, dt_bias, decay_log, skip_gain, gain, hidden, dt_weight.T,
+        teacher_keys[0], teacher_values[0], teacher_queries[0],
     )
 
     swap = [(0, 1), (1, 0)]
@@ -766,7 +727,7 @@
     sib0 = across(payload)
     hop2 = lax.ppermute(hop1, "z", hop)
     sib1 = across(hop1)
-    far = across(sent)
+    far = across(hidden)
     slope_other = across(slope)
     origin, keep = run(0, [local])
     hop2, origin = lax.optimization_barrier((hop2, origin))

time: 110 us -> 108 us (0.982)
  Pallas kernels: 29.1 us -> 25.8 us
  waiting for transfers between devices: 15 us -> 16.1 us
    pallas_call x1, Pallas kernels: 5.47 us -> 3.53 us  [body(): pl.pallas_call(functools.partial(prep_kernel, kv), out_shape=[shape((carg...]
    pallas_call x5, Pallas kernels: 15.6 us -> 14.2 us  [forward(): pl.pallas_call(functools.partial(forward_kernel, kv, heads, part), out_sh...]
  transfers between devices with their start and end apart: 16 -> 16, of which waited for: 7 -> 7; matrix products, arithmetic and copies ran while one was open for 0% -> 0% of each run, Pallas kernels for 10% -> 12%
where the time goes in v5:
time: 108 us
  blocking collectives  41.4 us (38%)
  Pallas kernels  25.8 us (24%)
  starting transfers between devices  22.5 us (21%)
  waiting for transfers between devices  16.1 us (15%)
  local copies, waits for them, and re-layouts  1.12 us (1%)
    ppermute x8, starting transfers between devices, across(): return lax.ppermute(part, 'core', swap)  15.2 us
    all_to_all x1, blocking collectives, body(): mine = lax.all_to_all(spread, axes, 0, 0, tiled=True)  14.7 us
    pallas_call x5, Pallas kernels, forward(): pl.pallas_call(functools.partial(forward_kernel, kv, heads, part), out_sh...  14.2 us
    all_to_all x1, blocking collectives, body(): got = lax.all_to_all(half, axes, 0, 0, tiled=True)  13.8 us
    all_to_all x1, blocking collectives, body(): lax.all_to_all(grads.reshape(chips, 2 * heads, 128), 'z', 0, 0, tiled=True)  12.9 us
    ppermute x1, waiting for transfers between devices, body(): hop1 = lax.ppermute(payload, 'z', hop)  8.17 us
    pallas_call x1, Pallas kernels, body(): pl.pallas_call(functools.partial(backward_kernel, kv, heads, len(all_stat...  6.48 us
    ppermute x3, starting transfers between devices, body(): lax.ppermute(stats, 'grp', [(i, (i + k) % groups) for i in range(groups)])  3.85 us
  transfers between devices with their start and end apart: 16, of which 7 were waited for; matrix products, arithmetic and copies ran while one was open for 0% of the time, Pallas kernels for 12%

profile of v5, /device:TPU:1, one launch (start us, length us, event | category | flops | bytes accessed | tf_op | source)
XLA Modules:
  0.0 107.7 jit_solution(12868964735555822786)
XLA Ops:
  0.6 3.3 %collective-permute-start.5 = (bf16[128,8192]{1,0:T(8,128)(2,1)}, bf16[128,8192]{1,0:T(8,128)(2,1)S(1)}, u32[]{:S(2)}, u32[]{:S(2)}) collective-permute-start(bf16[128,8192]{1,0:T(8,128)(2,1)} %bitcast.17), channel_id=1, source_target_pairs={{0,16},{16,0},{1,17},{17,1},{2,18},{18,2},{3,19},{19,3},{4,20},{20... | collective-permute-start | bytes 6291464 | tf_op jit(solution)/shard_map/ppermute | solution.py:724
  4.0 3.5 %prep.1 = (bf16[560,128]{1,0:T(8,128)(2,1)}, f32[16,128]{1,0:T(8,128)}, bf16[2800,128]{1,0:T(8,128)(2,1)}) custom-call(s32[1,4]{1,0:T(1,128)} %lengths.1, f32[16]{0:T(128)} %bias.1, f32[16]{0:T(128)} %decay.1, f32[16]{0:T(128)} %skip.1, f32[1,2048]{1,0:T(1,128)} %bitcast.30, bf16[128,8192]{1,0:T(8,128)(2,1)} %bitcast.18, bf16[16,8192]{1,0:T(8,128)(2,1)} %bitcast.27, ...), custom_call_target="tpu_custom_call" | custom-call | tf_op jit(solution)/shard_map/prep/pallas_call | solution.py:702
  7.5 0.0 collective-permute-start
  7.5 8.2 %collective-permute-done.refs_3_ = bf16[560,128]{1,0:T(8,128)(2,1)S(1)} collective-permute-done((bf16[560,128]{1,0:T(8,128)(2,1)}, bf16[560,128]{1,0:T(8,128)(2,1)S(1)}, u32[]{:S(2)}, u32[]{:S(2)}) %collective-permute-start) | collective-permute-done | bytes 143392 | tf_op jit(solution)/shard_map/ppermute | solution.py:726
  15.7 0.0 collective-permute-start.1
  15.7 0.6 collective-permute-start.4
  16.3 0.0 collective-permute-start.3
  16.3 0.0 copy-start
  16.3 1.1 %copy-done = bf16[2800,128]{1,0:T(8,128)(2,1)S(1)} copy-done((bf16[2800,128]{1,0:T(8,128)(2,1)S(1)}, bf16[2800,128]{1,0:T(8,128)(2,1)}, u32[]{:S(2)}) %copy-start) | copy-done | bytes 716824
  17.4 2.8 %forward_a.1 = (f32[6400,128]{1,0:T(8,128)S(1)}, f32[4864,128]{1,0:T(8,128)S(1)}) custom-call(bf16[2800,128]{1,0:T(8,128)(2,1)S(1)} %copy-done), custom_call_target="tpu_custom_call" | custom-call | flops 402653184 | bytes 3145728 | tf_op jit(solution)/shard_map/forward_a/pallas_call | solution.py:467
  20.2 1.4 %collective-permute-done.1.refs_3_ = bf16[560,128]{1,0:T(8,128)(2,1)S(1)} collective-permute-done((bf16[560,128]{1,0:T(8,128)(2,1)S(1)}, bf16[560,128]{1,0:T(8,128)(2,1)S(1)}, u32[]{:S(2)}, u32[]{:S(2)}) %collective-permute-start.1) | collective-permute-done | bytes 143392 | tf_op jit(solution)/shard_map/ppermute | solution.py:728
  21.6 0.0 collective-permute-start.2
  21.6 1.5 %collective-permute-start.6 = (f32[16,128]{1,0:T(8,128)}, f32[16,128]{1,0:T(8,128)S(1)}, u32[]{:S(2)}, u32[]{:S(2)}) collective-permute-start(f32[16,128]{1,0:T(8,128)} %get-tuple-element.37.slope), channel_id=1, source_target_pairs={{0,16},{16,0},{1,17},{17,1},{2,18},{18,2},{3,19},{19,3},{4,20},{20... | collective-permute-start | bytes 24584 | tf_op jit(solution)/shard_map/ppermute | solution.py:724
  23.1 0.0 collective-permute-done.4.refs_2_
  23.1 0.1 collective-permute-start.8
  23.2 0.0 collective-permute-done.3.refs_1_.refs_2_
  23.2 2.1 %forward_b.1.refs_5_ = f32[9344,128]{1,0:T(8,128)S(1)} custom-call(bf16[2800,128]{1,0:T(8,128)(2,1)S(1)} %copy-done, bf16[560,128]{1,0:T(8,128)(2,1)S(1)} %collective-permute-done.3.refs_1_.refs_2_, bf16[560,128]{1,0:T(8,128)(2,1)S(1)} %collective-permute-done.4.refs_2_, bf16[560,128]{1,0:T(8,128)(2,1)S(1)} %collective-permute-done.refs_3_, ...), custom_call_target="tpu_custom_call" | custom-call | flops 805306368 | bytes 6291456 | tf_op jit(solution)/shard_map/forward_b/pallas_call | solution.py:467
  25.3 0.0 collective-permute-done.6.slope_other
  25.3 1.4 %collective-permute-done.2.refs_3_ = bf16[560,128]{1,0:T(8,128)(2,1)S(1)} collective-permute-done((bf16[560,128]{1,0:T(8,128)(2,1)S(1)}, bf16[560,128]{1,0:T(8,128)(2,1)S(1)}, u32[]{:S(2)}, u32[]{:S(2)}) %collective-permute-start.2) | collective-permute-done | bytes 143392 | tf_op jit(solution)/shard_map/ppermute | solution.py:734
  26.8 0.0 collective-permute-done.5.far
  26.8 0.0 collective-permute-start.7
  26.8 2.6 %collective-permute-start.10 = (bf16[560,128]{1,0:T(8,128)(2,1)S(1)}, bf16[560,128]{1,0:T(8,128)(2,1)S(1)}, u32[]{:S(2)}, u32[]{:S(2)}) collective-permute-start(bf16[560,128]{1,0:T(8,128)(2,1)S(1)} %collective-permute-done.2.refs_3_), channel_id=1, source_target_pairs={{0,16},{16,0},{1,17},{17,1},{2,18},{18,2},{3,19},{19,3},{4,20},{20... | collective-permute-start | bytes 430088 | tf_op jit(solution)/shard_map/ppermute | solution.py:724
  29.4 0.0 collective-permute-done.8.refs_1_.refs_2_
  29.4 2.4 %forward_c.1.refs_6_.refs_2_ = f32[11392,128]{1,0:T(8,128)S(1)} custom-call(bf16[2800,128]{1,0:T(8,128)(2,1)S(1)} %copy-done, bf16[560,128]{1,0:T(8,128)(2,1)S(1)} %collective-permute-done.8.refs_1_.refs_2_, bf16[560,128]{1,0:T(8,128)(2,1)S(1)} %collective-permute-done.3.refs_1_.refs_2_, bf16[560,128]{1,0:T(8,128)(2,1)S(1)} %collective-permute-done.1.refs_3_, ...), custom_call_target="tpu_custom_call" | custom-call | flops 805306368 | bytes 6291456 | tf_op jit(solution)/shard_map/forward_c/pallas_call | solution.py:467
  31.8 0.1 collective-permute-done.7.refs_3_
  31.9 3.8 %collective-permute-start.9 = (bf16[560,128]{1,0:T(8,128)(2,1)S(1)}, bf16[560,128]{1,0:T(8,128)(2,1)S(1)}, u32[]{:S(2)}, u32[]{:S(2)}) collective-permute-start(bf16[560,128]{1,0:T(8,128)(2,1)S(1)} %collective-permute-done.7.refs_3_), channel_id=1, source_target_pairs={{0,16},{16,0},{1,17},{17,1},{2,18},{18,2},{3,19},{19,3},{4,20},{20... | collective-permute-start | bytes 430088 | tf_op jit(solution)/shard_map/ppermute | solution.py:724
  35.7 0.0 collective-permute-done.10.refs_1_.refs_2_
  35.7 2.2 %forward_d.1.refs_7_ = f32[9344,128]{1,0:T(8,128)S(1)} custom-call(bf16[2800,128]{1,0:T(8,128)(2,1)S(1)} %copy-done, bf16[560,128]{1,0:T(8,128)(2,1)S(1)} %collective-permute-done.10.refs_1_.refs_2_, bf16[560,128]{1,0:T(8,128)(2,1)S(1)} %collective-permute-done.8.refs_1_.refs_2_, bf16[560,128]{1,0:T(8,128)(2,1)S(1)} %collective-permute-done.2.refs_3_, ...), custom_call_target="tpu_custom_call" | custom-call | flops 805306368 | bytes 6291456 | tf_op jit(solution)/shard_map/forward_d/pallas_call | solution.py:467
  37.9 0.0 collective-permute-done.9.refs_1_
  37.9 4.6 %forward_e.1 = (f32[6912,128]{1,0:T(8,128)S(1)}, bf16[4352,128]{1,0:T(8,128)(2,1)S(1)}, f32[8,128]{1,0:T(8,128)S(1)}) custom-call(bf16[2800,128]{1,0:T(8,128)(2,1)S(1)} %copy-done, bf16[560,128]{1,0:T(8,128)(2,1)S(1)} %collective-permute-done.9.refs_1_, bf16[560,128]{1,0:T(8,128)(2,1)S(1)} %collective-permute-done.10.refs_1_.refs_2_, ...), custom_call_target="tpu_custom_call" | custom-call | flops 805306368 | bytes 6291456 | tf_op jit(solution)/shard_map/forward_e/pallas_call | solution.py:467
  42.5 2.8 %collective-permute-start.13 = (f32[8,128]{1,0:T(8,128)S(1)}, f32[8,128]{1,0:T(8,128)S(1)}, u32[]{:S(2)}, u32[]{:S(2)}) collective-permute-start(f32[8,128]{1,0:T(8,128)S(1)} %get-tuple-element.44.refs_5_), channel_id=1, source_target_pairs={{0,12},{4,0},{8,4},{12,8},{1,13},{5,1},{9,5},{13,9},{2,14},{6,2},{... | collective-permute-start | bytes 12296 | tf_op jit(solution)/shard_map/ppermute | solution.py:749
  45.3 0.3 collective-permute-start.12
  45.7 0.7 collective-permute-start.11
  46.4 0.0 collective-permute-done.13.refs_8_
  46.4 2.9 %collective-permute-done.12.refs_7_ = f32[8,128]{1,0:T(8,128)S(1)} collective-permute-done((f32[8,128]{1,0:T(8,128)S(1)}, f32[8,128]{1,0:T(8,128)S(1)}, u32[]{:S(2)}, u32[]{:S(2)}) %collective-permute-start.12) | collective-permute-done | bytes 4128 | tf_op jit(solution)/shard_map/ppermute | solution.py:749
  49.3 0.0 collective-permute-done.11.refs_6_
  49.3 0.0 copy-start.1
  49.3 0.0 copy-start.2
  49.3 6.5 %backward.1 = (bf16[128,2048]{1,0:T(8,128)(2,1)}, f32[16,16,128]{2,1,0:T(8,128)S(1)}, f32[1,2048]{1,0:T(1,128)S(1)}, f32[8,128]{1,0:T(8,128)S(1)}) custom-call(bf16[2800,128]{1,0:T(8,128)(2,1)S(1)} %copy-done, f32[4864,128]{1,0:T(8,128)S(1)} %get-tuple-element.32.refs_8_.refs_1_, f32[11392,128]{1,0:T(8,128)S(1)} %forward_c.1.refs_6_.refs_2_, ...), custom_call_target="tpu_custom_call" | custom-call | tf_op jit(solution)/shard_map/backward/pallas_call | solution.py:753
  55.8 12.9 %all_to_all.15.grads = f32[8,32,128]{2,1,0:T(8,128)S(1)} all-to-all(f32[8,32,128]{2,1,0:T(8,128)S(1)} %bitcast.25), channel_id=1, replica_groups=mesh['z'=8,'core'=2,'grp'=4,'dp'=4] {'z'}, dimensions={0} | all-to-all | bytes 262144 | tf_op jit(solution)/shard_map/all_to_all | solution.py:776
  68.7 3.3 %collective-permute-start.14 = (f32[56,128]{1,0:T(8,128)S(1)}, f32[56,128]{1,0:T(8,128)S(1)}, u32[]{:S(2)}, u32[]{:S(2)}) collective-permute-start(f32[56,128]{1,0:T(8,128)S(1)} %fold.1.own), channel_id=1, source_target_pairs={{0,16},{16,0},{1,17},{17,1},{2,18},{18,2},{3,19},{19,3},{4,20},{20... | collective-permute-start | bytes 86024 | tf_op jit(solution)/shard_map/ppermute | solution.py:724
  72.1 0.9 collective-permute-done.14.other
  73.0 0.0 copy-done.1
  73.0 0.0 copy-done.2
  73.0 0.7 weights.1
  73.7 13.8 %all_to_all.16 = bf16[32,9,2,128]{3,2,1,0:T(2,128)(2,1)S(1)} all-to-all(bf16[32,9,2,128]{3,2,1,0:T(2,128)(2,1)S(1)} %bitcast.23), channel_id=1, replica_groups=mesh['z'=8,'core'=2,'grp'=4,'dp'=4] {'z','dp'}, dimensions={0} | all-to-all | bytes 294912 | tf_op jit(solution)/shard_map/all_to_all | solution.py:798
  87.4 0.1 spread.1
  87.5 14.7 %all_to_all.17 = f32[32,17,1,128]{3,2,1,0:T(1,128)S(1)} all-to-all(f32[32,17,1,128]{3,2,1,0:T(1,128)S(1)} %bitcast.22), channel_id=1, replica_groups=mesh['z'=8,'core'=2,'grp'=4,'dp'=4] {'z','dp'}, dimensions={0} | all-to-all | bytes 557056 | tf_op jit(solution)/shard_map/all_to_all | solution.py:809
  102.2 3.5 %collective-permute-start.15 = (f32[544,128]{1,0:T(8,128)S(1)}, f32[544,128]{1,0:T(8,128)S(1)}, u32[]{:S(2)}, u32[]{:S(2)}) collective-permute-start(f32[544,128]{1,0:T(8,128)S(1)} %bitcast.20), channel_id=1, source_target_pairs={{0,16},{16,0},{1,17},{17,1},{2,18},{18,2},{3,19},{19,3},{4,20},{20... | collective-permute-start | bytes 835592 | tf_op jit(solution)/shard_map/ppermute | solution.py:811
  105.7 1.2 %collective-permute-done.15.other = f32[544,128]{1,0:T(8,128)S(1)} collective-permute-done((f32[544,128]{1,0:T(8,128)S(1)}, f32[544,128]{1,0:T(8,128)S(1)}, u32[]{:S(2)}, u32[]{:S(2)}) %collective-permute-start.15) | collective-permute-done | bytes 278560 | tf_op jit(solution)/shard_map/ppermute | solution.py:811
  106.8 0.8 finish.1
  (1 shorter events, 0.0 us)
Async XLA Ops:
  0.6 26.1 %collective-permute-start.5 = (bf16[128,8192]{1,0:T(8,128)(2,1)}, bf16[128,8192]{1,0:T(8,128)(2,1)S(1)}, u32[]{:S(2)}, u32[]{:S(2)}) collective-permute-start(bf16[128,8192]{1,0:T(8,128)(2,1)} %bitcast.17), channel_id=1, source_target_pairs={{0,16},{16,0},{1,17},{17,1},{2,18},{18,2},{3,19},{19,3},{4,20},{20... | collective-permute-start | bytes 6291464 | tf_op jit(solution)/shard_map/ppermute | solution.py:724
  7.5 8.2 %collective-permute-start = (bf16[560,128]{1,0:T(8,128)(2,1)}, bf16[560,128]{1,0:T(8,128)(2,1)S(1)}, u32[]{:S(2)}, u32[]{:S(2)}) collective-permute-start(bf16[560,128]{1,0:T(8,128)(2,1)} %get-tuple-element.33), channel_id=1, source_target_pairs={{0,32},{32,64},{64,96},{96,128},{128,160},{160,192},{192,224},{224... | collective-permute-start | bytes 430088 | tf_op jit(solution)/shard_map/ppermute | solution.py:726
  15.7 5.9 %collective-permute-start.1 = (bf16[560,128]{1,0:T(8,128)(2,1)S(1)}, bf16[560,128]{1,0:T(8,128)(2,1)S(1)}, u32[]{:S(2)}, u32[]{:S(2)}) collective-permute-start(bf16[560,128]{1,0:T(8,128)(2,1)S(1)} %collective-permute-done.refs_3_), channel_id=1, source_target_pairs={{0,32},{32,64},{64,96},{96,128},{128,160},{160,192},{192,224},{224... | collective-permute-start | bytes 430088 | tf_op jit(solution)/shard_map/ppermute | solution.py:728
  15.7 7.4 %collective-permute-start.4 = (bf16[560,128]{1,0:T(8,128)(2,1)}, bf16[560,128]{1,0:T(8,128)(2,1)S(1)}, u32[]{:S(2)}, u32[]{:S(2)}) collective-permute-start(bf16[560,128]{1,0:T(8,128)(2,1)} %get-tuple-element.33), channel_id=1, source_target_pairs={{0,16},{16,0},{1,17},{17,1},{2,18},{18,2},{3,19},{19,3},{4,20},{20... | collective-permute-start | bytes 430088 | tf_op jit(solution)/shard_map/ppermute | solution.py:724
  16.3 6.9 %collective-permute-start.3 = (bf16[560,128]{1,0:T(8,128)(2,1)S(1)}, bf16[560,128]{1,0:T(8,128)(2,1)S(1)}, u32[]{:S(2)}, u32[]{:S(2)}) collective-permute-start(bf16[560,128]{1,0:T(8,128)(2,1)S(1)} %collective-permute-done.refs_3_), channel_id=1, source_target_pairs={{0,16},{16,0},{1,17},{17,1},{2,18},{18,2},{3,19},{19,3},{4,20},{20... | collective-permute-start | bytes 430088 | tf_op jit(solution)/shard_map/ppermute | solution.py:724
  16.3 1.1 %copy-start = (bf16[2800,128]{1,0:T(8,128)(2,1)S(1)}, bf16[2800,128]{1,0:T(8,128)(2,1)}, u32[]{:S(2)}) copy-start(bf16[2800,128]{1,0:T(8,128)(2,1)} %get-tuple-element.31.refs_0_) | copy-start | bytes 2150404
  21.6 5.2 %collective-permute-start.2 = (bf16[560,128]{1,0:T(8,128)(2,1)S(1)}, bf16[560,128]{1,0:T(8,128)(2,1)S(1)}, u32[]{:S(2)}, u32[]{:S(2)}) collective-permute-start(bf16[560,128]{1,0:T(8,128)(2,1)S(1)} %collective-permute-done.1.refs_3_), channel_id=1, source_target_pairs={{0,32},{32,64},{64,96},{96,128},{128,160},{160,192},{192,224},{224... | collective-permute-start | bytes 430088 | tf_op jit(solution)/shard_map/ppermute | solution.py:734
  21.6 3.7 %collective-permute-start.6 = (f32[16,128]{1,0:T(8,128)}, f32[16,128]{1,0:T(8,128)S(1)}, u32[]{:S(2)}, u32[]{:S(2)}) collective-permute-start(f32[16,128]{1,0:T(8,128)} %get-tuple-element.37.slope), channel_id=1, source_target_pairs={{0,16},{16,0},{1,17},{17,1},{2,18},{18,2},{3,19},{19,3},{4,20},{20... | collective-permute-start | bytes 24584 | tf_op jit(solution)/shard_map/ppermute | solution.py:724
  23.1 6.3 %collective-permute-start.8 = (bf16[560,128]{1,0:T(8,128)(2,1)S(1)}, bf16[560,128]{1,0:T(8,128)(2,1)S(1)}, u32[]{:S(2)}, u32[]{:S(2)}) collective-permute-start(bf16[560,128]{1,0:T(8,128)(2,1)S(1)} %collective-permute-done.1.refs_3_), channel_id=1, source_target_pairs={{0,16},{16,0},{1,17},{17,1},{2,18},{18,2},{3,19},{19,3},{4,20},{20... | collective-permute-start | bytes 430088 | tf_op jit(solution)/shard_map/ppermute | solution.py:724
  26.8 5.2 %collective-permute-start.7 = (bf16[560,128]{1,0:T(8,128)(2,1)S(1)}, bf16[560,128]{1,0:T(8,128)(2,1)S(1)}, u32[]{:S(2)}, u32[]{:S(2)}) collective-permute-start(bf16[560,128]{1,0:T(8,128)(2,1)S(1)} %collective-permute-done.2.refs_3_), channel_id=1, source_target_pairs={{0,32},{32,64},{64,96},{96,128},{128,160},{160,192},{192,224},{224... | collective-permute-start | bytes 430088 | tf_op jit(solution)/shard_map/ppermute | solution.py:738
  26.8 8.9 %collective-permute-start.10 = (bf16[560,128]{1,0:T(8,128)(2,1)S(1)}, bf16[560,128]{1,0:T(8,128)(2,1)S(1)}, u32[]{:S(2)}, u32[]{:S(2)}) collective-permute-start(bf16[560,128]{1,0:T(8,128)(2,1)S(1)} %collective-permute-done.2.refs_3_), channel_id=1, source_target_pairs={{0,16},{16,0},{1,17},{17,1},{2,18},{18,2},{3,19},{19,3},{4,20},{20... | collective-permute-start | bytes 430088 | tf_op jit(solution)/shard_map/ppermute | solution.py:724
  31.9 5.9 %collective-permute-start.9 = (bf16[560,128]{1,0:T(8,128)(2,1)S(1)}, bf16[560,128]{1,0:T(8,128)(2,1)S(1)}, u32[]{:S(2)}, u32[]{:S(2)}) collective-permute-start(bf16[560,128]{1,0:T(8,128)(2,1)S(1)} %collective-permute-done.7.refs_3_), channel_id=1, source_target_pairs={{0,16},{16,0},{1,17},{17,1},{2,18},{18,2},{3,19},{19,3},{4,20},{20... | collective-permute-start | bytes 430088 | tf_op jit(solution)/shard_map/ppermute | solution.py:724
  42.5 3.9 %collective-permute-start.13 = (f32[8,128]{1,0:T(8,128)S(1)}, f32[8,128]{1,0:T(8,128)S(1)}, u32[]{:S(2)}, u32[]{:S(2)}) collective-permute-start(f32[8,128]{1,0:T(8,128)S(1)} %get-tuple-element.44.refs_5_), channel_id=1, source_target_pairs={{0,12},{4,0},{8,4},{12,8},{1,13},{5,1},{9,5},{13,9},{2,14},{6,2},{... | collective-permute-start | bytes 12296 | tf_op jit(solution)/shard_map/ppermute | solution.py:749
  45.3 4.0 %collective-permute-start.12 = (f32[8,128]{1,0:T(8,128)S(1)}, f32[8,128]{1,0:T(8,128)S(1)}, u32[]{:S(2)}, u32[]{:S(2)}) collective-permute-start(f32[8,128]{1,0:T(8,128)S(1)} %get-tuple-element.44.refs_5_), channel_id=1, source_target_pairs={{0,8},{4,12},{8,0},{12,4},{1,9},{5,13},{9,1},{13,5},{2,10},{6,14},... | collective-permute-start | bytes 12296 | tf_op jit(solution)/shard_map/ppermute | solution.py:749
  45.7 3.7 %collective-permute-start.11 = (f32[8,128]{1,0:T(8,128)S(1)}, f32[8,128]{1,0:T(8,128)S(1)}, u32[]{:S(2)}, u32[]{:S(2)}) collective-permute-start(f32[8,128]{1,0:T(8,128)S(1)} %get-tuple-element.44.refs_5_), channel_id=1, source_target_pairs={{0,4},{4,8},{8,12},{12,0},{1,5},{5,9},{9,13},{13,1},{2,6},{6,10},{... | collective-permute-start | bytes 12296 | tf_op jit(solution)/shard_map/ppermute | solution.py:749
  49.3 23.6 %copy-start.1 = (bf16[1,128,8192]{2,1,0:T(8,128)(2,1)S(1)}, bf16[1,128,8192]{2,1,0:T(8,128)(2,1)}, u32[]{:S(2)}) copy-start(bf16[1,128,8192]{2,1,0:T(8,128)(2,1)} %param.10) | copy-start | bytes 6291460
  49.3 23.6 %copy-start.2 = (f32[16,128]{1,0:T(8,128)S(1)}, f32[16,128]{1,0:T(8,128)}, u32[]{:S(2)}) copy-start(f32[16,128]{1,0:T(8,128)} %get-tuple-element.37.slope) | copy-start | bytes 24580
  68.7 4.2 %collective-permute-start.14 = (f32[56,128]{1,0:T(8,128)S(1)}, f32[56,128]{1,0:T(8,128)S(1)}, u32[]{:S(2)}, u32[]{:S(2)}) collective-permute-start(f32[56,128]{1,0:T(8,128)S(1)} %fold.1.own), channel_id=1, source_target_pairs={{0,16},{16,0},{1,17},{17,1},{2,18},{18,2},{3,19},{19,3},{4,20},{20... | collective-permute-start | bytes 86024 | tf_op jit(solution)/shard_map/ppermute | solution.py:724
  102.2 4.7 %collective-permute-start.15 = (f32[544,128]{1,0:T(8,128)S(1)}, f32[544,128]{1,0:T(8,128)S(1)}, u32[]{:S(2)}, u32[]{:S(2)}) collective-permute-start(f32[544,128]{1,0:T(8,128)S(1)} %bitcast.20), channel_id=1, source_target_pairs={{0,16},{16,0},{1,17},{17,1},{2,18},{18,2},{3,19},{19,3},{4,20},{20... | collective-permute-start | bytes 835592 | tf_op jit(solution)/shard_map/ppermute | solution.py:811

commit v6 on v5

--- a/solution.py
+++ b/solution.py
@@ -87,10 +87,8 @@
     weight,
     keys,
     values,
-    queries,
     payload,
     slope,
-    local,
     consts,
 ):
     heads = weight.shape[0]
@@ -124,6 +122,10 @@
         piece = step.astype(BF16)
         payload[first + part * heads : first + (part + 1) * heads, :] = piece
         step = step - piece.astype(F32)
+
+
+def pack_kernel(kv, queries, payload, consts, local):
+    heads = queries.shape[1] // 128
     at = local_rows(heads, kv)[0]
     for h in range(heads):
         local[at[0] + 128 * h : at[0] + 128 * h + 128, :] = queries[:, 128 * h : 128 * h + 128]
@@ -699,21 +701,20 @@
     gain = norm_gain[None, :]
     cargo = 2 * kv * HDIM + 3 * heads
 
-    payload, slope, local = pl.pallas_call(
+    payload, slope, consts = pl.pallas_call(
         functools.partial(prep_kernel, kv),
         out_shape=[
             shape((cargo, 128), BF16),
             shape((heads, 128)),
-            shape((local_rows(heads, kv)[1], 128), BF16),
+            shape((const_rows(heads), 128)),
         ],
-        in_specs=smem(4) + vmem(6),
+        in_specs=smem(4) + vmem(5),
         out_specs=vmem(3),
-        scratch_shapes=[pltpu.VMEM((const_rows(heads), 128), F32)],
         compiler_params=LARGE,
         name="prep",
     )(
         doc_lengths, dt_bias, decay_log, skip_gain, gain, hidden, dt_weight.T,
-        teacher_keys[0], teacher_values[0], teacher_queries[0],
+        teacher_keys[0], teacher_values[0],
     )
 
     swap = [(0, 1), (1, 0)]
@@ -725,16 +726,24 @@
 
     hop1 = lax.ppermute(payload, "z", hop)
     sib0 = across(payload)
+    local = pl.pallas_call(
+        functools.partial(pack_kernel, kv),
+        out_shape=shape((local_rows(heads, kv)[1], 128), BF16),
+        in_specs=vmem(3),
+        out_specs=pl.BlockSpec(memory_space=pltpu.VMEM),
+        compiler_params=SMALL,
+        name="pack",
+    )(teacher_queries[0], payload, consts)
+    hop1, local = lax.optimization_barrier((hop1, local))
     hop2 = lax.ppermute(hop1, "z", hop)
     sib1 = across(hop1)
-    far = across(hidden)
     slope_other = across(slope)
     origin, keep = run(0, [local])
     hop2, origin = lax.optimization_barrier((hop2, origin))
     hop3 = lax.ppermute(hop2, "z", hop)
     sib2 = across(hop2)
     (carry1,) = run(1, [local, sib1, sib0, hop1, origin])
-    hop3, carry1, far, slope_other = lax.optimization_barrier((hop3, carry1, far, slope_other))
+    hop3, carry1, slope_other = lax.optimization_barrier((hop3, carry1, slope_other))
     hop4 = lax.ppermute(hop3, "z", hop)
     sib3 = across(hop3)
     (carry2,) = run(2, [local, sib2, sib1, hop2, origin, carry1])
@@ -744,6 +753,8 @@
     real, half, stats = run(
         4, [local, sib4, sib3, hop4, origin, carry1, carry2, carry3, keep]
     )
+    hidden_late, stats = lax.optimization_barrier((hidden, stats))
+    far = across(hidden_late)
     groups = lax.axis_size("grp")
     all_stats = [stats] + [
         lax.ppermute(stats, "grp", [(i, (i + k) % groups) for i in range(groups)])

time: 108 us -> 107 us (level)
  waiting for transfers between devices: 16.1 us -> 11.5 us
  starting transfers between devices: 22.5 us -> 24.5 us
  local copies, waits for them, and re-layouts: 1.12 us -> 2.72 us
    ppermute x1, waiting for transfers between devices: 8.17 us -> 4.81 us  [body(): hop1 = lax.ppermute(payload, 'z', hop)]
    ppermute x1, starting transfers between devices: 0.01 us -> 2.47 us  [body(): hop1 = lax.ppermute(payload, 'z', hop)]
    unnamed x6 -> x10, local copies, waits for them, and re-layouts: 1.12 us -> 2.72 us
  transfers between devices with their start and end apart: 16 -> 16, of which waited for: 7 -> 7; matrix products, arithmetic and copies ran while one was open for 0% -> 0% of each run, Pallas kernels for 12% -> 15%
where the time goes in v6:
time: 107 us; the launch traced here: 106 us
  blocking collectives  41.5 us (39%)
  Pallas kernels  25.4 us (24%)
  starting transfers between devices  24.5 us (23%)
  waiting for transfers between devices  11.5 us (11%)
  local copies, waits for them, and re-layouts  2.72 us (3%)
    all_to_all x1, blocking collectives, body(): mine = lax.all_to_all(spread, axes, 0, 0, tiled=True)  14.7 us
    ppermute x8, starting transfers between devices, across(): return lax.ppermute(part, 'core', swap)  14.7 us
    pallas_call x5, Pallas kernels, forward(): pl.pallas_call(functools.partial(forward_kernel, kv, heads, part), out_sh...  14.2 us
    all_to_all x1, blocking collectives, body(): got = lax.all_to_all(half, axes, 0, 0, tiled=True)  13.8 us
    all_to_all x1, blocking collectives, body(): lax.all_to_all(grads.reshape(chips, 2 * heads, 128), 'z', 0, 0, tiled=True)  13.1 us
    pallas_call x1, Pallas kernels, body(): pl.pallas_call(functools.partial(backward_kernel, kv, heads, len(all_stat...  6.44 us
    ppermute x1, waiting for transfers between devices, body(): hop1 = lax.ppermute(payload, 'z', hop)  4.81 us
    ppermute x3, starting transfers between devices, body(): lax.ppermute(stats, 'grp', [(i, (i + k) % groups) for i in range(groups)])  3.85 us
  transfers between devices with their start and end apart: 16, of which 7 were waited for; matrix products, arithmetic and copies ran while one was open for 0% of the time, Pallas kernels for 15%

profile of v6, /device:TPU:1, one launch (start us, length us, event | category | flops | bytes accessed | tf_op | source)
XLA Modules:
  0.0 106.4 jit_solution(4611158638397137580)
XLA Ops:
  0.6 3.0 %prep.1 = (bf16[560,128]{1,0:T(8,128)(2,1)}, f32[16,128]{1,0:T(8,128)}, f32[64,128]{1,0:T(8,128)}) custom-call(s32[1,4]{1,0:T(1,128)} %lengths.1, f32[16]{0:T(128)} %bias.1, f32[16]{0:T(128)} %decay.1, f32[16]{0:T(128)} %skip.1, f32[1,2048]{1,0:T(1,128)} %bitcast.30, bf16[128,8192]{1,0:T(8,128)(2,1)} %bitcast.17, bf16[16,8192]{1,0:T(8,128)(2,1)} %bitcast.27, ...), custom_call_target="tpu_custom_call" | custom-call | tf_op jit(solution)/shard_map/prep/pallas_call | solution.py:704
  3.7 2.5 %collective-permute-start = (bf16[560,128]{1,0:T(8,128)(2,1)}, bf16[560,128]{1,0:T(8,128)(2,1)S(1)}, u32[]{:S(2)}, u32[]{:S(2)}) collective-permute-start(bf16[560,128]{1,0:T(8,128)(2,1)} %get-tuple-element.34.payload), channel_id=1, source_target_pairs={{0,32},{32,64},{64,96},{96,128},{128,160},{160,192},{192,224},{224... | collective-permute-start | bytes 430088 | tf_op jit(solution)/shard_map/ppermute | solution.py:727
  6.1 0.0 copy-start.1
  6.1 1.0 copy-done.1
  7.2 0.0 copy-start.2
  7.2 0.9 copy-done.2
  8.1 0.0 copy-start.3
  8.1 0.8 copy-done.3
  8.9 0.1 pack.1.refs_0_
  9.0 4.8 %collective-permute-done.refs_3_ = bf16[560,128]{1,0:T(8,128)(2,1)S(1)} collective-permute-done((bf16[560,128]{1,0:T(8,128)(2,1)}, bf16[560,128]{1,0:T(8,128)(2,1)S(1)}, u32[]{:S(2)}, u32[]{:S(2)}) %collective-permute-start) | collective-permute-done | bytes 143392 | tf_op jit(solution)/shard_map/ppermute | solution.py:727
  13.8 0.0 collective-permute-start.1
  13.8 1.2 %collective-permute-start.4 = (bf16[560,128]{1,0:T(8,128)(2,1)S(1)}, bf16[560,128]{1,0:T(8,128)(2,1)S(1)}, u32[]{:S(2)}, u32[]{:S(2)}) collective-permute-start(bf16[560,128]{1,0:T(8,128)(2,1)S(1)} %copy-done.2), channel_id=1, source_target_pairs={{0,16},{16,0},{1,17},{17,1},{2,18},{18,2},{3,19},{19,3},{4,20},{20... | collective-permute-start | bytes 430088 | tf_op jit(solution)/shard_map/ppermute | solution.py:725
  15.0 0.0 collective-permute-start.3
  15.0 2.8 %forward_a.1 = (f32[6400,128]{1,0:T(8,128)S(1)}, f32[4864,128]{1,0:T(8,128)S(1)}) custom-call(bf16[2800,128]{1,0:T(8,128)(2,1)S(1)} %pack.1.refs_0_), custom_call_target="tpu_custom_call" | custom-call | flops 402653184 | bytes 3145728 | tf_op jit(solution)/shard_map/forward_a/pallas_call | solution.py:469
  17.9 1.1 %collective-permute-done.1.refs_3_ = bf16[560,128]{1,0:T(8,128)(2,1)S(1)} collective-permute-done((bf16[560,128]{1,0:T(8,128)(2,1)S(1)}, bf16[560,128]{1,0:T(8,128)(2,1)S(1)}, u32[]{:S(2)}, u32[]{:S(2)}) %collective-permute-start.1) | collective-permute-done | bytes 143392 | tf_op jit(solution)/shard_map/ppermute | solution.py:738
  18.9 0.0 collective-permute-start.2
  18.9 2.4 %collective-permute-start.5 = (f32[16,128]{1,0:T(8,128)}, f32[16,128]{1,0:T(8,128)S(1)}, u32[]{:S(2)}, u32[]{:S(2)}) collective-permute-start(f32[16,128]{1,0:T(8,128)} %get-tuple-element.42.slope), channel_id=1, source_target_pairs={{0,16},{16,0},{1,17},{17,1},{2,18},{18,2},{3,19},{19,3},{4,20},{20... | collective-permute-start | bytes 24584 | tf_op jit(solution)/shard_map/ppermute | solution.py:725
  21.3 0.0 collective-permute-start.7
  21.3 0.0 collective-permute-done.4.refs_2_
  21.3 0.0 collective-permute-done.3.refs_1_.refs_2_
  21.3 2.1 %forward_b.1.refs_5_ = f32[9344,128]{1,0:T(8,128)S(1)} custom-call(bf16[2800,128]{1,0:T(8,128)(2,1)S(1)} %pack.1.refs_0_, bf16[560,128]{1,0:T(8,128)(2,1)S(1)} %collective-permute-done.3.refs_1_.refs_2_, bf16[560,128]{1,0:T(8,128)(2,1)S(1)} %collective-permute-done.4.refs_2_, bf16[560,128]{1,0:T(8,128)(2,1)S(1)} %collective-permute-done.refs_3_, ...), custom_call_target="tpu_custom_call" | custom-call | flops 805306368 | bytes 6291456 | tf_op jit(solution)/shard_map/forward_b/pallas_call | solution.py:469
  23.5 0.0 collective-permute-done.5.slope_other
  23.5 0.6 collective-permute-done.2.refs_3_
  24.1 0.0 collective-permute-start.6
  24.1 3.5 %collective-permute-start.9 = (bf16[560,128]{1,0:T(8,128)(2,1)S(1)}, bf16[560,128]{1,0:T(8,128)(2,1)S(1)}, u32[]{:S(2)}, u32[]{:S(2)}) collective-permute-start(bf16[560,128]{1,0:T(8,128)(2,1)S(1)} %collective-permute-done.2.refs_3_), channel_id=1, source_target_pairs={{0,16},{16,0},{1,17},{17,1},{2,18},{18,2},{3,19},{19,3},{4,20},{20... | collective-permute-start | bytes 430088 | tf_op jit(solution)/shard_map/ppermute | solution.py:725
  27.6 0.0 collective-permute-done.7.refs_1_.refs_2_
  27.6 2.4 %forward_c.1.refs_6_.refs_2_ = f32[11392,128]{1,0:T(8,128)S(1)} custom-call(bf16[2800,128]{1,0:T(8,128)(2,1)S(1)} %pack.1.refs_0_, bf16[560,128]{1,0:T(8,128)(2,1)S(1)} %collective-permute-done.7.refs_1_.refs_2_, bf16[560,128]{1,0:T(8,128)(2,1)S(1)} %collective-permute-done.3.refs_1_.refs_2_, bf16[560,128]{1,0:T(8,128)(2,1)S(1)} %collective-permute-done.1.refs_3_, ...), custom_call_target="tpu_custom_call" | custom-call | flops 805306368 | bytes 6291456 | tf_op jit(solution)/shard_map/forward_c/pallas_call | solution.py:469
  30.1 0.0 collective-permute-done.6.refs_3_
  30.1 3.9 %collective-permute-start.8 = (bf16[560,128]{1,0:T(8,128)(2,1)S(1)}, bf16[560,128]{1,0:T(8,128)(2,1)S(1)}, u32[]{:S(2)}, u32[]{:S(2)}) collective-permute-start(bf16[560,128]{1,0:T(8,128)(2,1)S(1)} %collective-permute-done.6.refs_3_), channel_id=1, source_target_pairs={{0,16},{16,0},{1,17},{17,1},{2,18},{18,2},{3,19},{19,3},{4,20},{20... | collective-permute-start | bytes 430088 | tf_op jit(solution)/shard_map/ppermute | solution.py:725
  33.9 0.0 collective-permute-done.9.refs_1_.refs_2_
  33.9 2.2 %forward_d.1.refs_7_ = f32[9344,128]{1,0:T(8,128)S(1)} custom-call(bf16[2800,128]{1,0:T(8,128)(2,1)S(1)} %pack.1.refs_0_, bf16[560,128]{1,0:T(8,128)(2,1)S(1)} %collective-permute-done.9.refs_1_.refs_2_, bf16[560,128]{1,0:T(8,128)(2,1)S(1)} %collective-permute-done.7.refs_1_.refs_2_, bf16[560,128]{1,0:T(8,128)(2,1)S(1)} %collective-permute-done.2.refs_3_, ...), custom_call_target="tpu_custom_call" | custom-call | flops 805306368 | bytes 6291456 | tf_op jit(solution)/shard_map/forward_d/pallas_call | solution.py:469
  36.1 0.0 collective-permute-done.8.refs_1_
  36.1 0.0 copy-start
  36.2 4.6 %forward_e.1 = (f32[6912,128]{1,0:T(8,128)S(1)}, bf16[4352,128]{1,0:T(8,128)(2,1)S(1)}, f32[8,128]{1,0:T(8,128)S(1)}) custom-call(bf16[2800,128]{1,0:T(8,128)(2,1)S(1)} %pack.1.refs_0_, bf16[560,128]{1,0:T(8,128)(2,1)S(1)} %collective-permute-done.8.refs_1_, bf16[560,128]{1,0:T(8,128)(2,1)S(1)} %collective-permute-done.9.refs_1_.refs_2_, ...), custom_call_target="tpu_custom_call" | custom-call | flops 805306368 | bytes 6291456 | tf_op jit(solution)/shard_map/forward_e/pallas_call | solution.py:469
  40.8 0.0 copy-done
  40.8 0.1 collective-permute-start.14
  40.9 2.8 %collective-permute-start.12 = (f32[8,128]{1,0:T(8,128)S(1)}, f32[8,128]{1,0:T(8,128)S(1)}, u32[]{:S(2)}, u32[]{:S(2)}) collective-permute-start(f32[8,128]{1,0:T(8,128)S(1)} %get-tuple-element.50.refs_5_), channel_id=1, source_target_pairs={{0,12},{4,0},{8,4},{12,8},{1,13},{5,1},{9,5},{13,9},{2,14},{6,2},{... | collective-permute-start | bytes 12296 | tf_op jit(solution)/shard_map/ppermute | solution.py:760
  43.7 0.4 collective-permute-start.11
  44.1 0.7 collective-permute-start.10
  44.7 0.0 collective-permute-done.12.refs_8_
  44.7 2.9 %collective-permute-done.11.refs_7_ = f32[8,128]{1,0:T(8,128)S(1)} collective-permute-done((f32[8,128]{1,0:T(8,128)S(1)}, f32[8,128]{1,0:T(8,128)S(1)}, u32[]{:S(2)}, u32[]{:S(2)}) %collective-permute-start.11) | collective-permute-done | bytes 4128 | tf_op jit(solution)/shard_map/ppermute | solution.py:760
  47.7 0.1 collective-permute-done.10.refs_6_
  47.7 0.0 copy-start.4
  47.7 6.4 %backward.1 = (bf16[128,2048]{1,0:T(8,128)(2,1)}, f32[16,16,128]{2,1,0:T(8,128)S(1)}, f32[1,2048]{1,0:T(1,128)S(1)}, f32[8,128]{1,0:T(8,128)S(1)}) custom-call(bf16[2800,128]{1,0:T(8,128)(2,1)S(1)} %pack.1.refs_0_, f32[4864,128]{1,0:T(8,128)S(1)} %get-tuple-element.37.refs_8_.refs_1_, f32[11392,128]{1,0:T(8,128)S(1)} %forward_c.1.refs_6_.refs_2_, ...), custom_call_target="tpu_custom_call" | custom-call | tf_op jit(solution)/shard_map/backward/pallas_call | solution.py:764
  54.2 13.1 %all_to_all.15.grads = f32[8,32,128]{2,1,0:T(8,128)S(1)} all-to-all(f32[8,32,128]{2,1,0:T(8,128)S(1)} %bitcast.26), channel_id=1, replica_groups=mesh['z'=8,'core'=2,'grp'=4,'dp'=4] {'z'}, dimensions={0} | all-to-all | bytes 262144 | tf_op jit(solution)/shard_map/all_to_all | solution.py:787
  67.3 3.5 %collective-permute-start.13 = (f32[56,128]{1,0:T(8,128)S(1)}, f32[56,128]{1,0:T(8,128)S(1)}, u32[]{:S(2)}, u32[]{:S(2)}) collective-permute-start(f32[56,128]{1,0:T(8,128)S(1)} %fold.1.own), channel_id=1, source_target_pairs={{0,16},{16,0},{1,17},{17,1},{2,18},{18,2},{3,19},{19,3},{4,20},{20... | collective-permute-start | bytes 86024 | tf_op jit(solution)/shard_map/ppermute | solution.py:725
  70.8 0.9 collective-permute-done.13.other
  71.7 0.0 collective-permute-done.14.far
  71.7 0.0 copy-done.4
  71.7 0.7 weights.1
  72.4 13.8 %all_to_all.16 = bf16[32,9,2,128]{3,2,1,0:T(2,128)(2,1)S(1)} all-to-all(bf16[32,9,2,128]{3,2,1,0:T(2,128)(2,1)S(1)} %bitcast.23), channel_id=1, replica_groups=mesh['z'=8,'core'=2,'grp'=4,'dp'=4] {'z','dp'}, dimensions={0} | all-to-all | bytes 294912 | tf_op jit(solution)/shard_map/all_to_all | solution.py:809
  86.2 0.1 spread.1
  86.2 14.7 %all_to_all.17 = f32[32,17,1,128]{3,2,1,0:T(1,128)S(1)} all-to-all(f32[32,17,1,128]{3,2,1,0:T(1,128)S(1)} %bitcast.22), channel_id=1, replica_groups=mesh['z'=8,'core'=2,'grp'=4,'dp'=4] {'z','dp'}, dimensions={0} | all-to-all | bytes 557056 | tf_op jit(solution)/shard_map/all_to_all | solution.py:820
  100.9 3.5 %collective-permute-start.15 = (f32[544,128]{1,0:T(8,128)S(1)}, f32[544,128]{1,0:T(8,128)S(1)}, u32[]{:S(2)}, u32[]{:S(2)}) collective-permute-start(f32[544,128]{1,0:T(8,128)S(1)} %bitcast.20), channel_id=1, source_target_pairs={{0,16},{16,0},{1,17},{17,1},{2,18},{18,2},{3,19},{19,3},{4,20},{20... | collective-permute-start | bytes 835592 | tf_op jit(solution)/shard_map/ppermute | solution.py:822
  104.4 1.2 %collective-permute-done.15.other = f32[544,128]{1,0:T(8,128)S(1)} collective-permute-done((f32[544,128]{1,0:T(8,128)S(1)}, f32[544,128]{1,0:T(8,128)S(1)}, u32[]{:S(2)}, u32[]{:S(2)}) %collective-permute-start.15) | collective-permute-done | bytes 278560 | tf_op jit(solution)/shard_map/ppermute | solution.py:822
  105.6 0.8 finish.1
  (1 shorter events, 0.0 us)
Async XLA Ops:
  3.7 10.1 %collective-permute-start = (bf16[560,128]{1,0:T(8,128)(2,1)}, bf16[560,128]{1,0:T(8,128)(2,1)S(1)}, u32[]{:S(2)}, u32[]{:S(2)}) collective-permute-start(bf16[560,128]{1,0:T(8,128)(2,1)} %get-tuple-element.34.payload), channel_id=1, source_target_pairs={{0,32},{32,64},{64,96},{96,128},{128,160},{160,192},{192,224},{224... | collective-permute-start | bytes 430088 | tf_op jit(solution)/shard_map/ppermute | solution.py:727
  6.1 1.0 copy-start.1
  7.2 0.9 copy-start.2
  8.1 0.8 copy-start.3
  13.8 5.2 %collective-permute-start.1 = (bf16[560,128]{1,0:T(8,128)(2,1)S(1)}, bf16[560,128]{1,0:T(8,128)(2,1)S(1)}, u32[]{:S(2)}, u32[]{:S(2)}) collective-permute-start(bf16[560,128]{1,0:T(8,128)(2,1)S(1)} %collective-permute-done.refs_3_), channel_id=1, source_target_pairs={{0,32},{32,64},{64,96},{96,128},{128,160},{160,192},{192,224},{224... | collective-permute-start | bytes 430088 | tf_op jit(solution)/shard_map/ppermute | solution.py:738
  13.8 7.5 %collective-permute-start.4 = (bf16[560,128]{1,0:T(8,128)(2,1)S(1)}, bf16[560,128]{1,0:T(8,128)(2,1)S(1)}, u32[]{:S(2)}, u32[]{:S(2)}) collective-permute-start(bf16[560,128]{1,0:T(8,128)(2,1)S(1)} %copy-done.2), channel_id=1, source_target_pairs={{0,16},{16,0},{1,17},{17,1},{2,18},{18,2},{3,19},{19,3},{4,20},{20... | collective-permute-start | bytes 430088 | tf_op jit(solution)/shard_map/ppermute | solution.py:725
  15.0 6.3 %collective-permute-start.3 = (bf16[560,128]{1,0:T(8,128)(2,1)S(1)}, bf16[560,128]{1,0:T(8,128)(2,1)S(1)}, u32[]{:S(2)}, u32[]{:S(2)}) collective-permute-start(bf16[560,128]{1,0:T(8,128)(2,1)S(1)} %collective-permute-done.refs_3_), channel_id=1, source_target_pairs={{0,16},{16,0},{1,17},{17,1},{2,18},{18,2},{3,19},{19,3},{4,20},{20... | collective-permute-start | bytes 430088 | tf_op jit(solution)/shard_map/ppermute | solution.py:725
  18.9 5.2 %collective-permute-start.2 = (bf16[560,128]{1,0:T(8,128)(2,1)S(1)}, bf16[560,128]{1,0:T(8,128)(2,1)S(1)}, u32[]{:S(2)}, u32[]{:S(2)}) collective-permute-start(bf16[560,128]{1,0:T(8,128)(2,1)S(1)} %collective-permute-done.1.refs_3_), channel_id=1, source_target_pairs={{0,32},{32,64},{64,96},{96,128},{128,160},{160,192},{192,224},{224... | collective-permute-start | bytes 430088 | tf_op jit(solution)/shard_map/ppermute | solution.py:743
  18.9 4.5 %collective-permute-start.5 = (f32[16,128]{1,0:T(8,128)}, f32[16,128]{1,0:T(8,128)S(1)}, u32[]{:S(2)}, u32[]{:S(2)}) collective-permute-start(f32[16,128]{1,0:T(8,128)} %get-tuple-element.42.slope), channel_id=1, source_target_pairs={{0,16},{16,0},{1,17},{17,1},{2,18},{18,2},{3,19},{19,3},{4,20},{20... | collective-permute-start | bytes 24584 | tf_op jit(solution)/shard_map/ppermute | solution.py:725
  21.3 6.3 %collective-permute-start.7 = (bf16[560,128]{1,0:T(8,128)(2,1)S(1)}, bf16[560,128]{1,0:T(8,128)(2,1)S(1)}, u32[]{:S(2)}, u32[]{:S(2)}) collective-permute-start(bf16[560,128]{1,0:T(8,128)(2,1)S(1)} %collective-permute-done.1.refs_3_), channel_id=1, source_target_pairs={{0,16},{16,0},{1,17},{17,1},{2,18},{18,2},{3,19},{19,3},{4,20},{20... | collective-permute-start | bytes 430088 | tf_op jit(solution)/shard_map/ppermute | solution.py:725
  24.1 6.0 %collective-permute-start.6 = (bf16[560,128]{1,0:T(8,128)(2,1)S(1)}, bf16[560,128]{1,0:T(8,128)(2,1)S(1)}, u32[]{:S(2)}, u32[]{:S(2)}) collective-permute-start(bf16[560,128]{1,0:T(8,128)(2,1)S(1)} %collective-permute-done.2.refs_3_), channel_id=1, source_target_pairs={{0,32},{32,64},{64,96},{96,128},{128,160},{160,192},{192,224},{224... | collective-permute-start | bytes 430088 | tf_op jit(solution)/shard_map/ppermute | solution.py:747
  24.1 9.8 %collective-permute-start.9 = (bf16[560,128]{1,0:T(8,128)(2,1)S(1)}, bf16[560,128]{1,0:T(8,128)(2,1)S(1)}, u32[]{:S(2)}, u32[]{:S(2)}) collective-permute-start(bf16[560,128]{1,0:T(8,128)(2,1)S(1)} %collective-permute-done.2.refs_3_), channel_id=1, source_target_pairs={{0,16},{16,0},{1,17},{17,1},{2,18},{18,2},{3,19},{19,3},{4,20},{20... | collective-permute-start | bytes 430088 | tf_op jit(solution)/shard_map/ppermute | solution.py:725
  30.1 6.1 %collective-permute-start.8 = (bf16[560,128]{1,0:T(8,128)(2,1)S(1)}, bf16[560,128]{1,0:T(8,128)(2,1)S(1)}, u32[]{:S(2)}, u32[]{:S(2)}) collective-permute-start(bf16[560,128]{1,0:T(8,128)(2,1)S(1)} %collective-permute-done.6.refs_3_), channel_id=1, source_target_pairs={{0,16},{16,0},{1,17},{17,1},{2,18},{18,2},{3,19},{19,3},{4,20},{20... | collective-permute-start | bytes 430088 | tf_op jit(solution)/shard_map/ppermute | solution.py:725
  36.1 4.6 %copy-start = (bf16[1,128,8192]{2,1,0:T(8,128)(2,1)S(1)}, bf16[1,128,8192]{2,1,0:T(8,128)(2,1)}, u32[]{:S(2)}) copy-start(bf16[1,128,8192]{2,1,0:T(8,128)(2,1)} %param.10) | copy-start | bytes 6291460
  40.8 30.9 %collective-permute-start.14 = (bf16[128,8192]{1,0:T(8,128)(2,1)S(1)}, bf16[128,8192]{1,0:T(8,128)(2,1)S(1)}, u32[]{:S(2)}, u32[]{:S(2)}) collective-permute-start(bf16[128,8192]{1,0:T(8,128)(2,1)S(1)} %bitcast.18), channel_id=1, source_target_pairs={{0,16},{16,0},{1,17},{17,1},{2,18},{18,2},{3,19},{19,3},{4,20},{20... | collective-permute-start | bytes 6291464 | tf_op jit(solution)/shard_map/ppermute | solution.py:725
  40.9 3.9 %collective-permute-start.12 = (f32[8,128]{1,0:T(8,128)S(1)}, f32[8,128]{1,0:T(8,128)S(1)}, u32[]{:S(2)}, u32[]{:S(2)}) collective-permute-start(f32[8,128]{1,0:T(8,128)S(1)} %get-tuple-element.50.refs_5_), channel_id=1, source_target_pairs={{0,12},{4,0},{8,4},{12,8},{1,13},{5,1},{9,5},{13,9},{2,14},{6,2},{... | collective-permute-start | bytes 12296 | tf_op jit(solution)/shard_map/ppermute | solution.py:760
  43.7 4.0 %collective-permute-start.11 = (f32[8,128]{1,0:T(8,128)S(1)}, f32[8,128]{1,0:T(8,128)S(1)}, u32[]{:S(2)}, u32[]{:S(2)}) collective-permute-start(f32[8,128]{1,0:T(8,128)S(1)} %get-tuple-element.50.refs_5_), channel_id=1, source_target_pairs={{0,8},{4,12},{8,0},{12,4},{1,9},{5,13},{9,1},{13,5},{2,10},{6,14},... | collective-permute-start | bytes 12296 | tf_op jit(solution)/shard_map/ppermute | solution.py:760
  44.1 3.7 %collective-permute-start.10 = (f32[8,128]{1,0:T(8,128)S(1)}, f32[8,128]{1,0:T(8,128)S(1)}, u32[]{:S(2)}, u32[]{:S(2)}) collective-permute-start(f32[8,128]{1,0:T(8,128)S(1)} %get-tuple-element.50.refs_5_), channel_id=1, source_target_pairs={{0,4},{4,8},{8,12},{12,0},{1,5},{5,9},{9,13},{13,1},{2,6},{6,10},{... | collective-permute-start | bytes 12296 | tf_op jit(solution)/shard_map/ppermute | solution.py:760
  47.7 24.0 %copy-start.4 = (f32[16,128]{1,0:T(8,128)S(1)}, f32[16,128]{1,0:T(8,128)}, u32[]{:S(2)}) copy-start(f32[16,128]{1,0:T(8,128)} %get-tuple-element.42.slope) | copy-start | bytes 24580
  67.3 4.4 %collective-permute-start.13 = (f32[56,128]{1,0:T(8,128)S(1)}, f32[56,128]{1,0:T(8,128)S(1)}, u32[]{:S(2)}, u32[]{:S(2)}) collective-permute-start(f32[56,128]{1,0:T(8,128)S(1)} %fold.1.own), channel_id=1, source_target_pairs={{0,16},{16,0},{1,17},{17,1},{2,18},{18,2},{3,19},{19,3},{4,20},{20... | collective-permute-start | bytes 86024 | tf_op jit(solution)/shard_map/ppermute | solution.py:725
  100.9 4.7 %collective-permute-start.15 = (f32[544,128]{1,0:T(8,128)S(1)}, f32[544,128]{1,0:T(8,128)S(1)}, u32[]{:S(2)}, u32[]{:S(2)}) collective-permute-start(f32[544,128]{1,0:T(8,128)S(1)} %bitcast.20), channel_id=1, source_target_pairs={{0,16},{16,0},{1,17},{17,1},{2,18},{18,2},{3,19},{19,3},{4,20},{20... | collective-permute-start | bytes 835592 | tf_op jit(solution)/shard_map/ppermute | solution.py:822

commit v7 on v6

--- a/solution.py
+++ b/solution.py
@@ -239,8 +239,6 @@
         before_at = carry_rows(heads, kv, part - 1)[0]
     if last:
         keep, real, half, stats = take(4)
-        acc = refs[-1]
-        acc[...] = jnp.zeros_like(acc)
     elif not first:
         carry = take(1)[0]
     kt, vv, bias, step_ref = take(4)
@@ -356,7 +354,7 @@
     def rate_of(h):
         return constant[pl.ds(base + h, 1), :]
 
-    def one_head(h, unused):
+    def one_head(h, sums):
         g = h // group
         query = local[slab(local_at[0], h), :]
         scores = mm(query, kt[g])
@@ -421,15 +419,18 @@
             real[slab(real_at[0], h), :] = raw
             real[slab(real_at[1], h), :] = off
             gained = raw * constant[pl.ds(base + 2 * heads + h, 1), :]
-            acc[0] += raw * raw
-            acc[1] += gained * gained
-            acc[2] += gained * teach.astype(F32)
-        return unused
-
-    lax.fori_loop(0, heads, one_head, 0, unroll=(16, 8, 8, 16, 16)[part])
+            sums = (
+                sums[0] + raw * raw,
+                sums[1] + gained * gained,
+                sums[2] + gained * teach.astype(F32),
+            )
+        return sums
+
+    nothing = tuple(jnp.zeros((128, 128), F32) for _ in range(3 if last else 0))
+    sums = lax.fori_loop(0, heads, one_head, nothing, unroll=(16, 8, 8, 16, 16)[part])
     if last:
         stats[...] = jnp.concatenate(
-            [to_row(acc[0]), to_row(acc[1]), to_row(acc[2]), jnp.zeros((5, 128), F32)], axis=0
+            [to_row(sums[0]), to_row(sums[1]), to_row(sums[2]), jnp.zeros((5, 128), F32)], axis=0
         )
 
 
@@ -464,8 +465,6 @@
             pltpu.VMEM((kv, HDIM, wide), F32),
             pltpu.VMEM((len(blocks), heads, 128), F32),
         ]
-    if last:
-        scratch.append(pltpu.VMEM((3, rows, HDIM), F32))
     return pl.pallas_call(
         functools.partial(forward_kernel, kv, heads, part),
         out_shape=outs,
@@ -488,7 +487,7 @@
     for other in refs[1:groups]:
         stats = stats + other[...]
     student_out, grads, gain_out, small_out, *refs = refs[groups:]
-    inv_col, coef_col, late, skip_rows, direct_rows, minus_rows, row_sums = refs
+    inv_col, coef_col, late, skip_rows, direct_rows, minus_rows = refs
     keep_at = keep_rows(heads, kv)[0]
     real_at = real_rows(heads, kv)[0]
     half_at = half_rows(heads, kv)[0]
@@ -499,7 +498,6 @@
     info = place_of(real[base + size - 8 : base + size, :], 128)
     place, count = info[5], grads.shape[0]
     grads[...] = jnp.zeros_like(grads)
-    row_sums[...] = jnp.zeros_like(row_sums)
     share = 2.0 / row_total
     squares, gained_squares, crossed = stats[0:1, :], stats[1:2, :], stats[2:3, :]
     inverse = lax.rsqrt(squares / features + EPSILON)
@@ -511,7 +509,7 @@
     later = (row_i >= col_i).astype(BF16)
     strict = (row_i < col_i).astype(BF16)
 
-    def one_head(h, unused):
+    def one_head(h, row_sums):
         g = h // group
         cols = slab(0, h)
         query = local[slab(0, h), :]
@@ -547,10 +545,9 @@
         )
         minus_rows[pl.ds(h, 1), :] = jnp.sum(pairs, axis=0, keepdims=True)
         sums = jnp.sum(pairs + grad * off, axis=1, keepdims=True)
-        row_sums[...] += jnp.where(col_i == h, jnp.broadcast_to(sums, (128, 128)), 0.0)
-        return unused
-
-    lax.fori_loop(0, heads, one_head, 0, unroll=16)
+        return jnp.where(col_i == h, jnp.broadcast_to(sums, (128, 128)), row_sums)
+
+    row_sums = lax.fori_loop(0, heads, one_head, jnp.zeros((128, 128), F32), unroll=16)
 
     def summed(x, triangle):
         high, low = two_parts(x)
@@ -558,7 +555,7 @@
         return mm(high, triangle) + mm(low, triangle) + mm(rest, triangle)
 
     rate = real[base : base + heads, :]
-    spanned = summed(row_sums[...].T[:heads, :] - minus_rows[...], later)
+    spanned = summed(row_sums.T[:heads, :] - minus_rows[...], later)
     grads[place] = direct_rows[...] - rate * spanned
     rate_rows = spanned * real[real_at[4] : real_at[4] + heads, :]
     earlier = jnp.zeros((heads, 128), F32)
@@ -737,13 +734,12 @@
     hop1, local = lax.optimization_barrier((hop1, local))
     hop2 = lax.ppermute(hop1, "z", hop)
     sib1 = across(hop1)
-    slope_other = across(slope)
     origin, keep = run(0, [local])
     hop2, origin = lax.optimization_barrier((hop2, origin))
     hop3 = lax.ppermute(hop2, "z", hop)
     sib2 = across(hop2)
     (carry1,) = run(1, [local, sib1, sib0, hop1, origin])
-    hop3, carry1, slope_other = lax.optimization_barrier((hop3, carry1, slope_other))
+    hop3, carry1 = lax.optimization_barrier((hop3, carry1))
     hop4 = lax.ppermute(hop3, "z", hop)
     sib3 = across(hop3)
     (carry2,) = run(2, [local, sib2, sib1, hop2, origin, carry1])
@@ -753,13 +749,14 @@
     real, half, stats = run(
         4, [local, sib4, sib3, hop4, origin, carry1, carry2, carry3, keep]
     )
-    hidden_late, stats = lax.optimization_barrier((hidden, stats))
-    far = across(hidden_late)
+    hidden_late, slope_late, stats = lax.optimization_barrier((hidden, slope, stats))
+    far, slope_other = across(hidden_late), across(slope_late)
     groups = lax.axis_size("grp")
     all_stats = [stats] + [
         lax.ppermute(stats, "grp", [(i, (i + k) % groups) for i in range(groups)])
         for k in range(1, groups)
     ]
+    all_stats[1], slope_other = lax.optimization_barrier((all_stats[1], slope_other))
 
     student, grads, grad_gain, small = pl.pallas_call(
         functools.partial(backward_kernel, kv, heads, len(all_stats), features, row_total),
@@ -778,7 +775,6 @@
             pltpu.VMEM((heads, 128), F32),
             pltpu.VMEM((heads, 128), F32),
             pltpu.VMEM((heads, 128), F32),
-            pltpu.VMEM((128, 128), F32),
         ],
         compiler_params=SMALL,
         name="backward",

time: 107 us -> 107 us (level)
  transfers between devices with their start and end apart: 16 -> 16, of which waited for: 7 -> 6; matrix products, arithmetic and copies ran while one was open for 0% -> 0% of each run, Pallas kernels for 15% -> 15%
where the time goes in v7:
time: 107 us; the launch traced here: 106 us
  blocking collectives  41.5 us (39%)
  Pallas kernels  25.4 us (24%)
  starting transfers between devices  25.1 us (23%)
  waiting for transfers between devices  10.9 us (10%)
  local copies, waits for them, and re-layouts  2.72 us (3%)
    ppermute x8, starting transfers between devices, across(): return lax.ppermute(part, 'core', swap)  14.8 us
    all_to_all x1, blocking collectives, body(): mine = lax.all_to_all(spread, axes, 0, 0, tiled=True)  14.7 us
    pallas_call x5, Pallas kernels, forward(): pl.pallas_call(functools.partial(forward_kernel, kv, heads, part), out_sh...  14.2 us
    all_to_all x1, blocking collectives, body(): got = lax.all_to_all(half, axes, 0, 0, tiled=True)  13.8 us
    all_to_all x1, blocking collectives, body(): lax.all_to_all(grads.reshape(chips, 2 * heads, 128), 'z', 0, 0, tiled=True)  13.1 us
    pallas_call x1, Pallas kernels, body(): pl.pallas_call(functools.partial(backward_kernel, kv, heads, len(all_stat...  6.45 us
    ppermute x1, waiting for transfers between devices, body(): hop1 = lax.ppermute(payload, 'z', hop)  4.81 us
    ppermute x3, starting transfers between devices, body(): lax.ppermute(stats, 'grp', [(i, (i + k) % groups) for i in range(groups)])  4.4 us
  transfers between devices with their start and end apart: 16, of which 6 were waited for; matrix products, arithmetic and copies ran while one was open for 0% of the time, Pallas kernels for 15%

profile of v7, /device:TPU:1, one launch (start us, length us, event | category | flops | bytes accessed | tf_op | source)
XLA Modules:
  0.0 106.4 jit_solution(11254100234705083188)
XLA Ops:
  0.6 3.0 %prep.1 = (bf16[560,128]{1,0:T(8,128)(2,1)}, f32[16,128]{1,0:T(8,128)}, f32[64,128]{1,0:T(8,128)}) custom-call(s32[1,4]{1,0:T(1,128)} %lengths.1, f32[16]{0:T(128)} %bias.1, f32[16]{0:T(128)} %decay.1, f32[16]{0:T(128)} %skip.1, f32[1,2048]{1,0:T(1,128)} %bitcast.30, bf16[128,8192]{1,0:T(8,128)(2,1)} %bitcast.17, bf16[16,8192]{1,0:T(8,128)(2,1)} %bitcast.27, ...), custom_call_target="tpu_custom_call" | custom-call | tf_op jit(solution)/shard_map/prep/pallas_call | solution.py:701
  3.7 2.5 %collective-permute-start = (bf16[560,128]{1,0:T(8,128)(2,1)}, bf16[560,128]{1,0:T(8,128)(2,1)S(1)}, u32[]{:S(2)}, u32[]{:S(2)}) collective-permute-start(bf16[560,128]{1,0:T(8,128)(2,1)} %get-tuple-element.36.payload), channel_id=1, source_target_pairs={{0,32},{32,64},{64,96},{96,128},{128,160},{160,192},{192,224},{224... | collective-permute-start | bytes 430088 | tf_op jit(solution)/shard_map/ppermute | solution.py:724
  6.1 0.0 copy-start.1
  6.1 1.0 copy-done.1
  7.2 0.0 copy-start.2
  7.2 0.9 copy-done.2
  8.1 0.0 copy-start.3
  8.1 0.8 copy-done.3
  8.9 0.1 pack.1.refs_0_
  9.0 4.8 %collective-permute-done.refs_3_ = bf16[560,128]{1,0:T(8,128)(2,1)S(1)} collective-permute-done((bf16[560,128]{1,0:T(8,128)(2,1)}, bf16[560,128]{1,0:T(8,128)(2,1)S(1)}, u32[]{:S(2)}, u32[]{:S(2)}) %collective-permute-start) | collective-permute-done | bytes 143392 | tf_op jit(solution)/shard_map/ppermute | solution.py:724
  13.8 0.0 collective-permute-start.1
  13.8 1.2 %collective-permute-start.4 = (bf16[560,128]{1,0:T(8,128)(2,1)S(1)}, bf16[560,128]{1,0:T(8,128)(2,1)S(1)}, u32[]{:S(2)}, u32[]{:S(2)}) collective-permute-start(bf16[560,128]{1,0:T(8,128)(2,1)S(1)} %copy-done.2), channel_id=1, source_target_pairs={{0,16},{16,0},{1,17},{17,1},{2,18},{18,2},{3,19},{19,3},{4,20},{20... | collective-permute-start | bytes 430088 | tf_op jit(solution)/shard_map/ppermute | solution.py:722
  15.0 0.0 collective-permute-start.3
  15.0 2.8 %forward_a.1 = (f32[6400,128]{1,0:T(8,128)S(1)}, f32[4864,128]{1,0:T(8,128)S(1)}) custom-call(bf16[2800,128]{1,0:T(8,128)(2,1)S(1)} %pack.1.refs_0_), custom_call_target="tpu_custom_call" | custom-call | flops 402653184 | bytes 3145728 | tf_op jit(solution)/shard_map/forward_a/pallas_call | solution.py:468
  17.9 1.1 %collective-permute-done.1.refs_3_ = bf16[560,128]{1,0:T(8,128)(2,1)S(1)} collective-permute-done((bf16[560,128]{1,0:T(8,128)(2,1)S(1)}, bf16[560,128]{1,0:T(8,128)(2,1)S(1)}, u32[]{:S(2)}, u32[]{:S(2)}) %collective-permute-start.1) | collective-permute-done | bytes 143392 | tf_op jit(solution)/shard_map/ppermute | solution.py:735
  18.9 0.0 collective-permute-start.2
  18.9 2.4 %collective-permute-start.6 = (bf16[560,128]{1,0:T(8,128)(2,1)S(1)}, bf16[560,128]{1,0:T(8,128)(2,1)S(1)}, u32[]{:S(2)}, u32[]{:S(2)}) collective-permute-start(bf16[560,128]{1,0:T(8,128)(2,1)S(1)} %collective-permute-done.1.refs_3_), channel_id=1, source_target_pairs={{0,16},{16,0},{1,17},{17,1},{2,18},{18,2},{3,19},{19,3},{4,20},{20... | collective-permute-start | bytes 430088 | tf_op jit(solution)/shard_map/ppermute | solution.py:722
  21.3 0.0 collective-permute-done.4.refs_2_
  21.3 0.0 collective-permute-done.3.refs_1_.refs_2_
  21.3 2.1 %forward_b.1.refs_5_ = f32[9344,128]{1,0:T(8,128)S(1)} custom-call(bf16[2800,128]{1,0:T(8,128)(2,1)S(1)} %pack.1.refs_0_, bf16[560,128]{1,0:T(8,128)(2,1)S(1)} %collective-permute-done.3.refs_1_.refs_2_, bf16[560,128]{1,0:T(8,128)(2,1)S(1)} %collective-permute-done.4.refs_2_, bf16[560,128]{1,0:T(8,128)(2,1)S(1)} %collective-permute-done.refs_3_, ...), custom_call_target="tpu_custom_call" | custom-call | flops 805306368 | bytes 6291456 | tf_op jit(solution)/shard_map/forward_b/pallas_call | solution.py:468
  23.5 0.6 collective-permute-done.2.refs_3_
  24.1 0.0 collective-permute-start.5
  24.1 3.5 %collective-permute-start.8 = (bf16[560,128]{1,0:T(8,128)(2,1)S(1)}, bf16[560,128]{1,0:T(8,128)(2,1)S(1)}, u32[]{:S(2)}, u32[]{:S(2)}) collective-permute-start(bf16[560,128]{1,0:T(8,128)(2,1)S(1)} %collective-permute-done.2.refs_3_), channel_id=1, source_target_pairs={{0,16},{16,0},{1,17},{17,1},{2,18},{18,2},{3,19},{19,3},{4,20},{20... | collective-permute-start | bytes 430088 | tf_op jit(solution)/shard_map/ppermute | solution.py:722
  27.6 0.0 collective-permute-done.6.refs_1_.refs_2_
  27.6 2.4 %forward_c.1.refs_6_.refs_2_ = f32[11392,128]{1,0:T(8,128)S(1)} custom-call(bf16[2800,128]{1,0:T(8,128)(2,1)S(1)} %pack.1.refs_0_, bf16[560,128]{1,0:T(8,128)(2,1)S(1)} %collective-permute-done.6.refs_1_.refs_2_, bf16[560,128]{1,0:T(8,128)(2,1)S(1)} %collective-permute-done.3.refs_1_.refs_2_, bf16[560,128]{1,0:T(8,128)(2,1)S(1)} %collective-permute-done.1.refs_3_, ...), custom_call_target="tpu_custom_call" | custom-call | flops 805306368 | bytes 6291456 | tf_op jit(solution)/shard_map/forward_c/pallas_call | solution.py:468
  30.1 0.0 collective-permute-done.5.refs_3_
  30.1 3.9 %collective-permute-start.7 = (bf16[560,128]{1,0:T(8,128)(2,1)S(1)}, bf16[560,128]{1,0:T(8,128)(2,1)S(1)}, u32[]{:S(2)}, u32[]{:S(2)}) collective-permute-start(bf16[560,128]{1,0:T(8,128)(2,1)S(1)} %collective-permute-done.5.refs_3_), channel_id=1, source_target_pairs={{0,16},{16,0},{1,17},{17,1},{2,18},{18,2},{3,19},{19,3},{4,20},{20... | collective-permute-start | bytes 430088 | tf_op jit(solution)/shard_map/ppermute | solution.py:722
  33.9 0.0 collective-permute-done.8.refs_1_.refs_2_
  33.9 2.2 %forward_d.1.refs_7_ = f32[9344,128]{1,0:T(8,128)S(1)} custom-call(bf16[2800,128]{1,0:T(8,128)(2,1)S(1)} %pack.1.refs_0_, bf16[560,128]{1,0:T(8,128)(2,1)S(1)} %collective-permute-done.8.refs_1_.refs_2_, bf16[560,128]{1,0:T(8,128)(2,1)S(1)} %collective-permute-done.6.refs_1_.refs_2_, bf16[560,128]{1,0:T(8,128)(2,1)S(1)} %collective-permute-done.2.refs_3_, ...), custom_call_target="tpu_custom_call" | custom-call | flops 805306368 | bytes 6291456 | tf_op jit(solution)/shard_map/forward_d/pallas_call | solution.py:468
  36.1 0.0 collective-permute-done.7.refs_1_
  36.1 0.0 copy-start
  36.2 0.0 copy-start.4
  36.2 4.6 %forward_e.1 = (f32[6912,128]{1,0:T(8,128)S(1)}, bf16[4352,128]{1,0:T(8,128)(2,1)S(1)}, f32[8,128]{1,0:T(8,128)S(1)}) custom-call(bf16[2800,128]{1,0:T(8,128)(2,1)S(1)} %pack.1.refs_0_, bf16[560,128]{1,0:T(8,128)(2,1)S(1)} %collective-permute-done.7.refs_1_, bf16[560,128]{1,0:T(8,128)(2,1)S(1)} %collective-permute-done.8.refs_1_.refs_2_, ...), custom_call_target="tpu_custom_call" | custom-call | flops 805306368 | bytes 6291456 | tf_op jit(solution)/shard_map/forward_e/pallas_call | solution.py:468
  40.8 0.0 copy-done
  40.8 0.1 collective-permute-start.14
  40.9 0.0 copy-done.4
  40.9 0.5 collective-permute-start.10
  41.4 1.3 %collective-permute-start.9 = (f32[8,128]{1,0:T(8,128)S(1)}, f32[8,128]{1,0:T(8,128)S(1)}, u32[]{:S(2)}, u32[]{:S(2)}) collective-permute-start(f32[8,128]{1,0:T(8,128)S(1)} %get-tuple-element.52.refs_5_), channel_id=1, source_target_pairs={{0,4},{4,8},{8,12},{12,0},{1,5},{5,9},{9,13},{13,1},{2,6},{6,10},{... | collective-permute-start | bytes 12296 | tf_op jit(solution)/shard_map/ppermute | solution.py:756
  42.7 1.4 %collective-permute-start.12 = (f32[8,128]{1,0:T(8,128)S(1)}, f32[8,128]{1,0:T(8,128)S(1)}, u32[]{:S(2)}, u32[]{:S(2)}) collective-permute-start(f32[8,128]{1,0:T(8,128)S(1)} %get-tuple-element.52.refs_5_), channel_id=1, source_target_pairs={{0,12},{4,0},{8,4},{12,8},{1,13},{5,1},{9,5},{13,9},{2,14},{6,2},{... | collective-permute-start | bytes 12296 | tf_op jit(solution)/shard_map/ppermute | solution.py:756
  44.1 1.7 %collective-permute-start.11 = (f32[8,128]{1,0:T(8,128)S(1)}, f32[8,128]{1,0:T(8,128)S(1)}, u32[]{:S(2)}, u32[]{:S(2)}) collective-permute-start(f32[8,128]{1,0:T(8,128)S(1)} %get-tuple-element.52.refs_5_), channel_id=1, source_target_pairs={{0,8},{4,12},{8,0},{12,4},{1,9},{5,13},{9,1},{13,5},{2,10},{6,14},... | collective-permute-start | bytes 12296 | tf_op jit(solution)/shard_map/ppermute | solution.py:756
  45.8 0.0 collective-permute-done.9.refs_6_
  45.8 0.0 collective-permute-done.10.slope_other
  45.8 0.0 collective-permute-done.12.refs_8_
  45.8 2.3 %collective-permute-done.11.refs_7_ = f32[8,128]{1,0:T(8,128)S(1)} collective-permute-done((f32[8,128]{1,0:T(8,128)S(1)}, f32[8,128]{1,0:T(8,128)S(1)}, u32[]{:S(2)}, u32[]{:S(2)}) %collective-permute-start.11) | collective-permute-done | bytes 4128 | tf_op jit(solution)/shard_map/ppermute | solution.py:756
  48.1 6.4 %backward.1 = (bf16[128,2048]{1,0:T(8,128)(2,1)}, f32[16,16,128]{2,1,0:T(8,128)S(1)}, f32[1,2048]{1,0:T(1,128)S(1)}, f32[8,128]{1,0:T(8,128)S(1)}) custom-call(bf16[2800,128]{1,0:T(8,128)(2,1)S(1)} %pack.1.refs_0_, f32[4864,128]{1,0:T(8,128)S(1)} %get-tuple-element.39.refs_8_.refs_1_, f32[11392,128]{1,0:T(8,128)S(1)} %forward_c.1.refs_6_.refs_2_, ...), custom_call_target="tpu_custom_call" | custom-call | tf_op jit(solution)/shard_map/backward/pallas_call | solution.py:761
  54.5 13.1 %all_to_all.15.grads = f32[8,32,128]{2,1,0:T(8,128)S(1)} all-to-all(f32[8,32,128]{2,1,0:T(8,128)S(1)} %bitcast.26), channel_id=1, replica_groups=mesh['z'=8,'core'=2,'grp'=4,'dp'=4] {'z'}, dimensions={0} | all-to-all | bytes 262144 | tf_op jit(solution)/shard_map/all_to_all | solution.py:783
  67.7 3.2 %collective-permute-start.13 = (f32[56,128]{1,0:T(8,128)S(1)}, f32[56,128]{1,0:T(8,128)S(1)}, u32[]{:S(2)}, u32[]{:S(2)}) collective-permute-start(f32[56,128]{1,0:T(8,128)S(1)} %fold.1.own), channel_id=1, source_target_pairs={{0,16},{16,0},{1,17},{17,1},{2,18},{18,2},{3,19},{19,3},{4,20},{20... | collective-permute-start | bytes 86024 | tf_op jit(solution)/shard_map/ppermute | solution.py:722
  70.8 0.9 collective-permute-done.13.other
  71.7 0.0 collective-permute-done.14.far
  71.7 0.7 weights.1
  72.4 13.8 %all_to_all.16 = bf16[32,9,2,128]{3,2,1,0:T(2,128)(2,1)S(1)} all-to-all(bf16[32,9,2,128]{3,2,1,0:T(2,128)(2,1)S(1)} %bitcast.23), channel_id=1, replica_groups=mesh['z'=8,'core'=2,'grp'=4,'dp'=4] {'z','dp'}, dimensions={0} | all-to-all | bytes 294912 | tf_op jit(solution)/shard_map/all_to_all | solution.py:805
  86.2 0.1 spread.1
  86.3 14.7 %all_to_all.17 = f32[32,17,1,128]{3,2,1,0:T(1,128)S(1)} all-to-all(f32[32,17,1,128]{3,2,1,0:T(1,128)S(1)} %bitcast.22), channel_id=1, replica_groups=mesh['z'=8,'core'=2,'grp'=4,'dp'=4] {'z','dp'}, dimensions={0} | all-to-all | bytes 557056 | tf_op jit(solution)/shard_map/all_to_all | solution.py:816
  100.9 3.5 %collective-permute-start.15 = (f32[544,128]{1,0:T(8,128)S(1)}, f32[544,128]{1,0:T(8,128)S(1)}, u32[]{:S(2)}, u32[]{:S(2)}) collective-permute-start(f32[544,128]{1,0:T(8,128)S(1)} %bitcast.20), channel_id=1, source_target_pairs={{0,16},{16,0},{1,17},{17,1},{2,18},{18,2},{3,19},{19,3},{4,20},{20... | collective-permute-start | bytes 835592 | tf_op jit(solution)/shard_map/ppermute | solution.py:818
  104.4 1.2 %collective-permute-done.15.other = f32[544,128]{1,0:T(8,128)S(1)} collective-permute-done((f32[544,128]{1,0:T(8,128)S(1)}, f32[544,128]{1,0:T(8,128)S(1)}, u32[]{:S(2)}, u32[]{:S(2)}) %collective-permute-start.15) | collective-permute-done | bytes 278560 | tf_op jit(solution)/shard_map/ppermute | solution.py:818
  105.6 0.8 finish.1
  (1 shorter events, 0.0 us)
Async XLA Ops:
  3.7 10.1 %collective-permute-start = (bf16[560,128]{1,0:T(8,128)(2,1)}, bf16[560,128]{1,0:T(8,128)(2,1)S(1)}, u32[]{:S(2)}, u32[]{:S(2)}) collective-permute-start(bf16[560,128]{1,0:T(8,128)(2,1)} %get-tuple-element.36.payload), channel_id=1, source_target_pairs={{0,32},{32,64},{64,96},{96,128},{128,160},{160,192},{192,224},{224... | collective-permute-start | bytes 430088 | tf_op jit(solution)/shard_map/ppermute | solution.py:724
  6.1 1.0 copy-start.1
  7.2 0.9 copy-start.2
  8.1 0.8 copy-start.3
  13.8 5.2 %collective-permute-start.1 = (bf16[560,128]{1,0:T(8,128)(2,1)S(1)}, bf16[560,128]{1,0:T(8,128)(2,1)S(1)}, u32[]{:S(2)}, u32[]{:S(2)}) collective-permute-start(bf16[560,128]{1,0:T(8,128)(2,1)S(1)} %collective-permute-done.refs_3_), channel_id=1, source_target_pairs={{0,32},{32,64},{64,96},{96,128},{128,160},{160,192},{192,224},{224... | collective-permute-start | bytes 430088 | tf_op jit(solution)/shard_map/ppermute | solution.py:735
  13.8 7.5 %collective-permute-start.4 = (bf16[560,128]{1,0:T(8,128)(2,1)S(1)}, bf16[560,128]{1,0:T(8,128)(2,1)S(1)}, u32[]{:S(2)}, u32[]{:S(2)}) collective-permute-start(bf16[560,128]{1,0:T(8,128)(2,1)S(1)} %copy-done.2), channel_id=1, source_target_pairs={{0,16},{16,0},{1,17},{17,1},{2,18},{18,2},{3,19},{19,3},{4,20},{20... | collective-permute-start | bytes 430088 | tf_op jit(solution)/shard_map/ppermute | solution.py:722
  15.0 6.3 %collective-permute-start.3 = (bf16[560,128]{1,0:T(8,128)(2,1)S(1)}, bf16[560,128]{1,0:T(8,128)(2,1)S(1)}, u32[]{:S(2)}, u32[]{:S(2)}) collective-permute-start(bf16[560,128]{1,0:T(8,128)(2,1)S(1)} %collective-permute-done.refs_3_), channel_id=1, source_target_pairs={{0,16},{16,0},{1,17},{17,1},{2,18},{18,2},{3,19},{19,3},{4,20},{20... | collective-permute-start | bytes 430088 | tf_op jit(solution)/shard_map/ppermute | solution.py:722
  18.9 5.2 %collective-permute-start.2 = (bf16[560,128]{1,0:T(8,128)(2,1)S(1)}, bf16[560,128]{1,0:T(8,128)(2,1)S(1)}, u32[]{:S(2)}, u32[]{:S(2)}) collective-permute-start(bf16[560,128]{1,0:T(8,128)(2,1)S(1)} %collective-permute-done.1.refs_3_), channel_id=1, source_target_pairs={{0,32},{32,64},{64,96},{96,128},{128,160},{160,192},{192,224},{224... | collective-permute-start | bytes 430088 | tf_op jit(solution)/shard_map/ppermute | solution.py:739
  18.9 8.7 %collective-permute-start.6 = (bf16[560,128]{1,0:T(8,128)(2,1)S(1)}, bf16[560,128]{1,0:T(8,128)(2,1)S(1)}, u32[]{:S(2)}, u32[]{:S(2)}) collective-permute-start(bf16[560,128]{1,0:T(8,128)(2,1)S(1)} %collective-permute-done.1.refs_3_), channel_id=1, source_target_pairs={{0,16},{16,0},{1,17},{17,1},{2,18},{18,2},{3,19},{19,3},{4,20},{20... | collective-permute-start | bytes 430088 | tf_op jit(solution)/shard_map/ppermute | solution.py:722
  24.1 6.0 %collective-permute-start.5 = (bf16[560,128]{1,0:T(8,128)(2,1)S(1)}, bf16[560,128]{1,0:T(8,128)(2,1)S(1)}, u32[]{:S(2)}, u32[]{:S(2)}) collective-permute-start(bf16[560,128]{1,0:T(8,128)(2,1)S(1)} %collective-permute-done.2.refs_3_), channel_id=1, source_target_pairs={{0,32},{32,64},{64,96},{96,128},{128,160},{160,192},{192,224},{224... | collective-permute-start | bytes 430088 | tf_op jit(solution)/shard_map/ppermute | solution.py:743
  24.1 9.8 %collective-permute-start.8 = (bf16[560,128]{1,0:T(8,128)(2,1)S(1)}, bf16[560,128]{1,0:T(8,128)(2,1)S(1)}, u32[]{:S(2)}, u32[]{:S(2)}) collective-permute-start(bf16[560,128]{1,0:T(8,128)(2,1)S(1)} %collective-permute-done.2.refs_3_), channel_id=1, source_target_pairs={{0,16},{16,0},{1,17},{17,1},{2,18},{18,2},{3,19},{19,3},{4,20},{20... | collective-permute-start | bytes 430088 | tf_op jit(solution)/shard_map/ppermute | solution.py:722
  30.1 6.1 %collective-permute-start.7 = (bf16[560,128]{1,0:T(8,128)(2,1)S(1)}, bf16[560,128]{1,0:T(8,128)(2,1)S(1)}, u32[]{:S(2)}, u32[]{:S(2)}) collective-permute-start(bf16[560,128]{1,0:T(8,128)(2,1)S(1)} %collective-permute-done.5.refs_3_), channel_id=1, source_target_pairs={{0,16},{16,0},{1,17},{17,1},{2,18},{18,2},{3,19},{19,3},{4,20},{20... | collective-permute-start | bytes 430088 | tf_op jit(solution)/shard_map/ppermute | solution.py:722
  36.1 4.6 %copy-start = (bf16[1,128,8192]{2,1,0:T(8,128)(2,1)S(1)}, bf16[1,128,8192]{2,1,0:T(8,128)(2,1)}, u32[]{:S(2)}) copy-start(bf16[1,128,8192]{2,1,0:T(8,128)(2,1)} %param.10) | copy-start | bytes 6291460
  36.2 4.7 %copy-start.4 = (f32[16,128]{1,0:T(8,128)S(1)}, f32[16,128]{1,0:T(8,128)}, u32[]{:S(2)}) copy-start(f32[16,128]{1,0:T(8,128)} %get-tuple-element.53.slope) | copy-start | bytes 24580
  40.8 30.9 %collective-permute-start.14 = (bf16[128,8192]{1,0:T(8,128)(2,1)S(1)}, bf16[128,8192]{1,0:T(8,128)(2,1)S(1)}, u32[]{:S(2)}, u32[]{:S(2)}) collective-permute-start(bf16[128,8192]{1,0:T(8,128)(2,1)S(1)} %bitcast.18), channel_id=1, source_target_pairs={{0,16},{16,0},{1,17},{17,1},{2,18},{18,2},{3,19},{19,3},{4,20},{20... | collective-permute-start | bytes 6291464 | tf_op jit(solution)/shard_map/ppermute | solution.py:722
  40.9 4.9 %collective-permute-start.10 = (f32[16,128]{1,0:T(8,128)S(1)}, f32[16,128]{1,0:T(8,128)S(1)}, u32[]{:S(2)}, u32[]{:S(2)}) collective-permute-start(f32[16,128]{1,0:T(8,128)S(1)} %copy-done.4), channel_id=1, source_target_pairs={{0,16},{16,0},{1,17},{17,1},{2,18},{18,2},{3,19},{19,3},{4,20},{20... | collective-permute-start | bytes 24584 | tf_op jit(solution)/shard_map/ppermute | solution.py:722
  41.4 4.4 %collective-permute-start.9 = (f32[8,128]{1,0:T(8,128)S(1)}, f32[8,128]{1,0:T(8,128)S(1)}, u32[]{:S(2)}, u32[]{:S(2)}) collective-permute-start(f32[8,128]{1,0:T(8,128)S(1)} %get-tuple-element.52.refs_5_), channel_id=1, source_target_pairs={{0,4},{4,8},{8,12},{12,0},{1,5},{5,9},{9,13},{13,1},{2,6},{6,10},{... | collective-permute-start | bytes 12296 | tf_op jit(solution)/shard_map/ppermute | solution.py:756
  42.7 3.1 %collective-permute-start.12 = (f32[8,128]{1,0:T(8,128)S(1)}, f32[8,128]{1,0:T(8,128)S(1)}, u32[]{:S(2)}, u32[]{:S(2)}) collective-permute-start(f32[8,128]{1,0:T(8,128)S(1)} %get-tuple-element.52.refs_5_), channel_id=1, source_target_pairs={{0,12},{4,0},{8,4},{12,8},{1,13},{5,1},{9,5},{13,9},{2,14},{6,2},{... | collective-permute-start | bytes 12296 | tf_op jit(solution)/shard_map/ppermute | solution.py:756
  44.1 4.0 %collective-permute-start.11 = (f32[8,128]{1,0:T(8,128)S(1)}, f32[8,128]{1,0:T(8,128)S(1)}, u32[]{:S(2)}, u32[]{:S(2)}) collective-permute-start(f32[8,128]{1,0:T(8,128)S(1)} %get-tuple-element.52.refs_5_), channel_id=1, source_target_pairs={{0,8},{4,12},{8,0},{12,4},{1,9},{5,13},{9,1},{13,5},{2,10},{6,14},... | collective-permute-start | bytes 12296 | tf_op jit(solution)/shard_map/ppermute | solution.py:756
  67.7 4.0 %collective-permute-start.13 = (f32[56,128]{1,0:T(8,128)S(1)}, f32[56,128]{1,0:T(8,128)S(1)}, u32[]{:S(2)}, u32[]{:S(2)}) collective-permute-start(f32[56,128]{1,0:T(8,128)S(1)} %fold.1.own), channel_id=1, source_target_pairs={{0,16},{16,0},{1,17},{17,1},{2,18},{18,2},{3,19},{19,3},{4,20},{20... | collective-permute-start | bytes 86024 | tf_op jit(solution)/shard_map/ppermute | solution.py:722
  100.9 4.7 %collective-permute-start.15 = (f32[544,128]{1,0:T(8,128)S(1)}, f32[544,128]{1,0:T(8,128)S(1)}, u32[]{:S(2)}, u32[]{:S(2)}) collective-permute-start(f32[544,128]{1,0:T(8,128)S(1)} %bitcast.20), channel_id=1, source_target_pairs={{0,16},{16,0},{1,17},{17,1},{2,18},{18,2},{3,19},{19,3},{4,20},{20... | collective-permute-start | bytes 835592 | tf_op jit(solution)/shard_map/ppermute | solution.py:818

commit v8 on v7

--- a/solution.py
+++ b/solution.py
@@ -30,11 +30,6 @@
     rows = a.shape[0]
     both = mm(jnp.concatenate(two_parts(a), axis=0), b)
     return both[:rows] + both[rows:]
-
-
-def mm_apart(a, b):
-    high, low = two_parts(a)
-    return mm(high, b) + mm(low, b)
 
 
 def mm_right(a, b):
@@ -380,7 +375,7 @@
                 axis=1,
             )
             mixed = mm(weights, vv[g])
-            state = mm_apart(key32[g] * weight_row, vv[g])
+            state = mm_two(key32[g] * weight_row, vv[g])
             scale = jnp.exp2(old - top)
             total = total + before_carry[slab(before_at[1], h), :] * scale
             mixed = mixed + before_carry[slab(before_at[2], h), :] * scale
@@ -427,7 +422,7 @@
         return sums
 
     nothing = tuple(jnp.zeros((128, 128), F32) for _ in range(3 if last else 0))
-    sums = lax.fori_loop(0, heads, one_head, nothing, unroll=(16, 8, 8, 16, 16)[part])
+    sums = lax.fori_loop(0, heads, one_head, nothing, unroll=16)
     if last:
         stats[...] = jnp.concatenate(
             [to_row(sums[0]), to_row(sums[1]), to_row(sums[2]), jnp.zeros((5, 128), F32)], axis=0

time: 107 us -> 109 us (1.019)
  Pallas kernels: 25.4 us -> 31 us
  starting transfers between devices: 25.1 us -> 22 us
    pallas_call x5, Pallas kernels: 14.2 us -> 19.7 us  [forward(): pl.pallas_call(functools.partial(forward_kernel, kv, heads, part), out_sh...]
    ppermute x8, starting transfers between devices: 14.8 us -> 11.6 us  [across(): return lax.ppermute(part, 'core', swap)]
  transfers between devices with their start and end apart: 16 -> 16, of which waited for: 6 -> 5; matrix products, arithmetic and copies ran while one was open for 0% -> 0% of each run, Pallas kernels for 15% -> 20%
where the time goes in v8:
time: 109 us; the launch traced here: 108 us
  blocking collectives  41.5 us (38%)
  Pallas kernels  31 us (28%)
  starting transfers between devices  22 us (20%)
  waiting for transfers between devices  10.2 us (9%)
  local copies, waits for them, and re-layouts  2.72 us (2%)
    pallas_call x5, Pallas kernels, forward(): pl.pallas_call(functools.partial(forward_kernel, kv, heads, part), out_sh...  19.7 us
    all_to_all x1, blocking collectives, body(): mine = lax.all_to_all(spread, axes, 0, 0, tiled=True)  14.7 us
    all_to_all x1, blocking collectives, body(): got = lax.all_to_all(half, axes, 0, 0, tiled=True)  13.8 us
    all_to_all x1, blocking collectives, body(): lax.all_to_all(grads.reshape(chips, 2 * heads, 128), 'z', 0, 0, tiled=True)  13.1 us
    ppermute x8, starting transfers between devices, across(): return lax.ppermute(part, 'core', swap)  11.6 us
    pallas_call x1, Pallas kernels, body(): pl.pallas_call(functools.partial(backward_kernel, kv, heads, len(all_stat...  6.44 us
    ppermute x1, waiting for transfers between devices, body(): hop1 = lax.ppermute(payload, 'z', hop)  4.81 us
    ppermute x3, starting transfers between devices, body(): lax.ppermute(stats, 'grp', [(i, (i + k) % groups) for i in range(groups)])  4.41 us
  transfers between devices with their start and end apart: 16, of which 5 were waited for; matrix products, arithmetic and copies ran while one was open for 0% of the time, Pallas kernels for 20%

profile of v8, /device:TPU:1, one launch (start us, length us, event | category | flops | bytes accessed | tf_op | source)
XLA Modules:
  0.0 108.2 jit_solution(12115701211955785033)
XLA Ops:
  0.6 3.0 %prep.1 = (bf16[560,128]{1,0:T(8,128)(2,1)}, f32[16,128]{1,0:T(8,128)}, f32[64,128]{1,0:T(8,128)}) custom-call(s32[1,4]{1,0:T(1,128)} %lengths.1, f32[16]{0:T(128)} %bias.1, f32[16]{0:T(128)} %decay.1, f32[16]{0:T(128)} %skip.1, f32[1,2048]{1,0:T(1,128)} %bitcast.30, bf16[128,8192]{1,0:T(8,128)(2,1)} %bitcast.17, bf16[16,8192]{1,0:T(8,128)(2,1)} %bitcast.27, ...), custom_call_target="tpu_custom_call" | custom-call | tf_op jit(solution)/shard_map/prep/pallas_call | solution.py:696
  3.7 2.5 %collective-permute-start = (bf16[560,128]{1,0:T(8,128)(2,1)}, bf16[560,128]{1,0:T(8,128)(2,1)S(1)}, u32[]{:S(2)}, u32[]{:S(2)}) collective-permute-start(bf16[560,128]{1,0:T(8,128)(2,1)} %get-tuple-element.36.payload), channel_id=1, source_target_pairs={{0,32},{32,64},{64,96},{96,128},{128,160},{160,192},{192,224},{224... | collective-permute-start | bytes 430088 | tf_op jit(solution)/shard_map/ppermute | solution.py:719
  6.1 0.0 copy-start.1
  6.1 1.0 copy-done.1
  7.2 0.0 copy-start.2
  7.2 0.9 copy-done.2
  8.1 0.0 copy-start.3
  8.1 0.8 copy-done.3
  8.9 0.1 pack.1.refs_0_
  9.0 4.8 %collective-permute-done.refs_3_ = bf16[560,128]{1,0:T(8,128)(2,1)S(1)} collective-permute-done((bf16[560,128]{1,0:T(8,128)(2,1)}, bf16[560,128]{1,0:T(8,128)(2,1)S(1)}, u32[]{:S(2)}, u32[]{:S(2)}) %collective-permute-start) | collective-permute-done | bytes 143392 | tf_op jit(solution)/shard_map/ppermute | solution.py:719
  13.8 0.0 collective-permute-start.1
  13.8 1.2 %collective-permute-start.4 = (bf16[560,128]{1,0:T(8,128)(2,1)S(1)}, bf16[560,128]{1,0:T(8,128)(2,1)S(1)}, u32[]{:S(2)}, u32[]{:S(2)}) collective-permute-start(bf16[560,128]{1,0:T(8,128)(2,1)S(1)} %copy-done.2), channel_id=1, source_target_pairs={{0,16},{16,0},{1,17},{17,1},{2,18},{18,2},{3,19},{19,3},{4,20},{20... | collective-permute-start | bytes 430088 | tf_op jit(solution)/shard_map/ppermute | solution.py:717
  15.0 0.0 collective-permute-start.3
  15.0 2.8 %forward_a.1 = (f32[6400,128]{1,0:T(8,128)S(1)}, f32[4864,128]{1,0:T(8,128)S(1)}) custom-call(bf16[2800,128]{1,0:T(8,128)(2,1)S(1)} %pack.1.refs_0_), custom_call_target="tpu_custom_call" | custom-call | flops 402653184 | bytes 3145728 | tf_op jit(solution)/shard_map/forward_a/pallas_call | solution.py:463
  17.9 1.1 collective-permute-done.1.refs_3_
  18.9 0.0 collective-permute-start.2
  18.9 2.4 %collective-permute-start.6 = (bf16[560,128]{1,0:T(8,128)(2,1)S(1)}, bf16[560,128]{1,0:T(8,128)(2,1)S(1)}, u32[]{:S(2)}, u32[]{:S(2)}) collective-permute-start(bf16[560,128]{1,0:T(8,128)(2,1)S(1)} %collective-permute-done.1.refs_3_), channel_id=1, source_target_pairs={{0,16},{16,0},{1,17},{17,1},{2,18},{18,2},{3,19},{19,3},{4,20},{20... | collective-permute-start | bytes 430088 | tf_op jit(solution)/shard_map/ppermute | solution.py:717
  21.3 0.0 collective-permute-done.4.refs_2_
  21.3 0.0 collective-permute-done.3.refs_1_.refs_2_
  21.3 4.1 %forward_b.1.refs_5_ = f32[9344,128]{1,0:T(8,128)S(1)} custom-call(bf16[2800,128]{1,0:T(8,128)(2,1)S(1)} %pack.1.refs_0_, bf16[560,128]{1,0:T(8,128)(2,1)S(1)} %collective-permute-done.3.refs_1_.refs_2_, bf16[560,128]{1,0:T(8,128)(2,1)S(1)} %collective-permute-done.4.refs_2_, bf16[560,128]{1,0:T(8,128)(2,1)S(1)} %collective-permute-done.refs_3_, ...), custom_call_target="tpu_custom_call" | custom-call | flops 805306368 | bytes 6291456 | tf_op jit(solution)/shard_map/forward_b/pallas_call | solution.py:463
  25.4 0.0 collective-permute-done.2.refs_3_
  25.4 0.1 collective-permute-start.5
  25.5 2.1 %collective-permute-start.8 = (bf16[560,128]{1,0:T(8,128)(2,1)S(1)}, bf16[560,128]{1,0:T(8,128)(2,1)S(1)}, u32[]{:S(2)}, u32[]{:S(2)}) collective-permute-start(bf16[560,128]{1,0:T(8,128)(2,1)S(1)} %collective-permute-done.2.refs_3_), channel_id=1, source_target_pairs={{0,16},{16,0},{1,17},{17,1},{2,18},{18,2},{3,19},{19,3},{4,20},{20... | collective-permute-start | bytes 430088 | tf_op jit(solution)/shard_map/ppermute | solution.py:717
  27.6 0.0 collective-permute-done.6.refs_1_.refs_2_
  27.6 4.2 %forward_c.1.refs_6_.refs_2_ = f32[11392,128]{1,0:T(8,128)S(1)} custom-call(bf16[2800,128]{1,0:T(8,128)(2,1)S(1)} %pack.1.refs_0_, bf16[560,128]{1,0:T(8,128)(2,1)S(1)} %collective-permute-done.6.refs_1_.refs_2_, bf16[560,128]{1,0:T(8,128)(2,1)S(1)} %collective-permute-done.3.refs_1_.refs_2_, bf16[560,128]{1,0:T(8,128)(2,1)S(1)} %collective-permute-done.1.refs_3_, ...), custom_call_target="tpu_custom_call" | custom-call | flops 805306368 | bytes 6291456 | tf_op jit(solution)/shard_map/forward_c/pallas_call | solution.py:463
  31.8 0.0 collective-permute-done.5.refs_3_
  31.8 2.1 %collective-permute-start.7 = (bf16[560,128]{1,0:T(8,128)(2,1)S(1)}, bf16[560,128]{1,0:T(8,128)(2,1)S(1)}, u32[]{:S(2)}, u32[]{:S(2)}) collective-permute-start(bf16[560,128]{1,0:T(8,128)(2,1)S(1)} %collective-permute-done.5.refs_3_), channel_id=1, source_target_pairs={{0,16},{16,0},{1,17},{17,1},{2,18},{18,2},{3,19},{19,3},{4,20},{20... | collective-permute-start | bytes 430088 | tf_op jit(solution)/shard_map/ppermute | solution.py:717
  33.9 0.0 collective-permute-done.8.refs_1_.refs_2_
  33.9 4.2 %forward_d.1.refs_7_ = f32[9344,128]{1,0:T(8,128)S(1)} custom-call(bf16[2800,128]{1,0:T(8,128)(2,1)S(1)} %pack.1.refs_0_, bf16[560,128]{1,0:T(8,128)(2,1)S(1)} %collective-permute-done.8.refs_1_.refs_2_, bf16[560,128]{1,0:T(8,128)(2,1)S(1)} %collective-permute-done.6.refs_1_.refs_2_, bf16[560,128]{1,0:T(8,128)(2,1)S(1)} %collective-permute-done.2.refs_3_, ...), custom_call_target="tpu_custom_call" | custom-call | flops 805306368 | bytes 6291456 | tf_op jit(solution)/shard_map/forward_d/pallas_call | solution.py:463
  38.1 0.0 collective-permute-done.7.refs_1_
  38.1 0.0 copy-start
  38.1 0.0 copy-start.4
  38.2 4.4 %forward_e.1 = (f32[6912,128]{1,0:T(8,128)S(1)}, bf16[4352,128]{1,0:T(8,128)(2,1)S(1)}, f32[8,128]{1,0:T(8,128)S(1)}) custom-call(bf16[2800,128]{1,0:T(8,128)(2,1)S(1)} %pack.1.refs_0_, bf16[560,128]{1,0:T(8,128)(2,1)S(1)} %collective-permute-done.7.refs_1_, bf16[560,128]{1,0:T(8,128)(2,1)S(1)} %collective-permute-done.8.refs_1_.refs_2_, ...), custom_call_target="tpu_custom_call" | custom-call | flops 805306368 | bytes 6291456 | tf_op jit(solution)/shard_map/forward_e/pallas_call | solution.py:463
  42.6 0.0 copy-done
  42.6 0.1 collective-permute-start.14
  42.7 0.0 copy-done.4
  42.7 0.5 collective-permute-start.10
  43.2 1.3 %collective-permute-start.9 = (f32[8,128]{1,0:T(8,128)S(1)}, f32[8,128]{1,0:T(8,128)S(1)}, u32[]{:S(2)}, u32[]{:S(2)}) collective-permute-start(f32[8,128]{1,0:T(8,128)S(1)} %get-tuple-element.52.refs_5_), channel_id=1, source_target_pairs={{0,4},{4,8},{8,12},{12,0},{1,5},{5,9},{9,13},{13,1},{2,6},{6,10},{... | collective-permute-start | bytes 12296 | tf_op jit(solution)/shard_map/ppermute | solution.py:751
  44.5 1.4 %collective-permute-start.12 = (f32[8,128]{1,0:T(8,128)S(1)}, f32[8,128]{1,0:T(8,128)S(1)}, u32[]{:S(2)}, u32[]{:S(2)}) collective-permute-start(f32[8,128]{1,0:T(8,128)S(1)} %get-tuple-element.52.refs_5_), channel_id=1, source_target_pairs={{0,12},{4,0},{8,4},{12,8},{1,13},{5,1},{9,5},{13,9},{2,14},{6,2},{... | collective-permute-start | bytes 12296 | tf_op jit(solution)/shard_map/ppermute | solution.py:751
  45.9 1.7 %collective-permute-start.11 = (f32[8,128]{1,0:T(8,128)S(1)}, f32[8,128]{1,0:T(8,128)S(1)}, u32[]{:S(2)}, u32[]{:S(2)}) collective-permute-start(f32[8,128]{1,0:T(8,128)S(1)} %get-tuple-element.52.refs_5_), channel_id=1, source_target_pairs={{0,8},{4,12},{8,0},{12,4},{1,9},{5,13},{9,1},{13,5},{2,10},{6,14},... | collective-permute-start | bytes 12296 | tf_op jit(solution)/shard_map/ppermute | solution.py:751
  47.6 0.0 collective-permute-done.9.refs_6_
  47.6 0.0 collective-permute-done.10.slope_other
  47.6 0.0 collective-permute-done.12.refs_8_
  47.6 2.3 %collective-permute-done.11.refs_7_ = f32[8,128]{1,0:T(8,128)S(1)} collective-permute-done((f32[8,128]{1,0:T(8,128)S(1)}, f32[8,128]{1,0:T(8,128)S(1)}, u32[]{:S(2)}, u32[]{:S(2)}) %collective-permute-start.11) | collective-permute-done | bytes 4128 | tf_op jit(solution)/shard_map/ppermute | solution.py:751
  49.9 6.4 %backward.1 = (bf16[128,2048]{1,0:T(8,128)(2,1)}, f32[16,16,128]{2,1,0:T(8,128)S(1)}, f32[1,2048]{1,0:T(1,128)S(1)}, f32[8,128]{1,0:T(8,128)S(1)}) custom-call(bf16[2800,128]{1,0:T(8,128)(2,1)S(1)} %pack.1.refs_0_, f32[4864,128]{1,0:T(8,128)S(1)} %get-tuple-element.39.refs_8_.refs_1_, f32[11392,128]{1,0:T(8,128)S(1)} %forward_c.1.refs_6_.refs_2_, ...), custom_call_target="tpu_custom_call" | custom-call | tf_op jit(solution)/shard_map/backward/pallas_call | solution.py:756
  56.3 13.1 %all_to_all.15.grads = f32[8,32,128]{2,1,0:T(8,128)S(1)} all-to-all(f32[8,32,128]{2,1,0:T(8,128)S(1)} %bitcast.26), channel_id=1, replica_groups=mesh['z'=8,'core'=2,'grp'=4,'dp'=4] {'z'}, dimensions={0} | all-to-all | bytes 262144 | tf_op jit(solution)/shard_map/all_to_all | solution.py:778
  69.5 3.2 %collective-permute-start.13 = (f32[56,128]{1,0:T(8,128)S(1)}, f32[56,128]{1,0:T(8,128)S(1)}, u32[]{:S(2)}, u32[]{:S(2)}) collective-permute-start(f32[56,128]{1,0:T(8,128)S(1)} %fold.1.own), channel_id=1, source_target_pairs={{0,16},{16,0},{1,17},{17,1},{2,18},{18,2},{3,19},{19,3},{4,20},{20... | collective-permute-start | bytes 86024 | tf_op jit(solution)/shard_map/ppermute | solution.py:717
  72.6 0.9 collective-permute-done.13.other
  73.5 0.0 collective-permute-done.14.far
  73.5 0.7 weights.1
  74.2 13.8 %all_to_all.16 = bf16[32,9,2,128]{3,2,1,0:T(2,128)(2,1)S(1)} all-to-all(bf16[32,9,2,128]{3,2,1,0:T(2,128)(2,1)S(1)} %bitcast.23), channel_id=1, replica_groups=mesh['z'=8,'core'=2,'grp'=4,'dp'=4] {'z','dp'}, dimensions={0} | all-to-all | bytes 294912 | tf_op jit(solution)/shard_map/all_to_all | solution.py:800
  88.0 0.1 spread.1
  88.0 14.7 %all_to_all.17 = f32[32,17,1,128]{3,2,1,0:T(1,128)S(1)} all-to-all(f32[32,17,1,128]{3,2,1,0:T(1,128)S(1)} %bitcast.22), channel_id=1, replica_groups=mesh['z'=8,'core'=2,'grp'=4,'dp'=4] {'z','dp'}, dimensions={0} | all-to-all | bytes 557056 | tf_op jit(solution)/shard_map/all_to_all | solution.py:811
  102.7 3.5 %collective-permute-start.15 = (f32[544,128]{1,0:T(8,128)S(1)}, f32[544,128]{1,0:T(8,128)S(1)}, u32[]{:S(2)}, u32[]{:S(2)}) collective-permute-start(f32[544,128]{1,0:T(8,128)S(1)} %bitcast.20), channel_id=1, source_target_pairs={{0,16},{16,0},{1,17},{17,1},{2,18},{18,2},{3,19},{19,3},{4,20},{20... | collective-permute-start | bytes 835592 | tf_op jit(solution)/shard_map/ppermute | solution.py:813
  106.2 1.2 %collective-permute-done.15.other = f32[544,128]{1,0:T(8,128)S(1)} collective-permute-done((f32[544,128]{1,0:T(8,128)S(1)}, f32[544,128]{1,0:T(8,128)S(1)}, u32[]{:S(2)}, u32[]{:S(2)}) %collective-permute-start.15) | collective-permute-done | bytes 278560 | tf_op jit(solution)/shard_map/ppermute | solution.py:813
  107.4 0.8 finish.1
  (1 shorter events, 0.0 us)
Async XLA Ops:
  3.7 10.1 %collective-permute-start = (bf16[560,128]{1,0:T(8,128)(2,1)}, bf16[560,128]{1,0:T(8,128)(2,1)S(1)}, u32[]{:S(2)}, u32[]{:S(2)}) collective-permute-start(bf16[560,128]{1,0:T(8,128)(2,1)} %get-tuple-element.36.payload), channel_id=1, source_target_pairs={{0,32},{32,64},{64,96},{96,128},{128,160},{160,192},{192,224},{224... | collective-permute-start | bytes 430088 | tf_op jit(solution)/shard_map/ppermute | solution.py:719
  6.1 1.0 copy-start.1
  7.2 0.9 copy-start.2
  8.1 0.8 copy-start.3
  13.8 5.2 %collective-permute-start.1 = (bf16[560,128]{1,0:T(8,128)(2,1)S(1)}, bf16[560,128]{1,0:T(8,128)(2,1)S(1)}, u32[]{:S(2)}, u32[]{:S(2)}) collective-permute-start(bf16[560,128]{1,0:T(8,128)(2,1)S(1)} %collective-permute-done.refs_3_), channel_id=1, source_target_pairs={{0,32},{32,64},{64,96},{96,128},{128,160},{160,192},{192,224},{224... | collective-permute-start | bytes 430088 | tf_op jit(solution)/shard_map/ppermute | solution.py:730
  13.8 7.5 %collective-permute-start.4 = (bf16[560,128]{1,0:T(8,128)(2,1)S(1)}, bf16[560,128]{1,0:T(8,128)(2,1)S(1)}, u32[]{:S(2)}, u32[]{:S(2)}) collective-permute-start(bf16[560,128]{1,0:T(8,128)(2,1)S(1)} %copy-done.2), channel_id=1, source_target_pairs={{0,16},{16,0},{1,17},{17,1},{2,18},{18,2},{3,19},{19,3},{4,20},{20... | collective-permute-start | bytes 430088 | tf_op jit(solution)/shard_map/ppermute | solution.py:717
  15.0 6.3 %collective-permute-start.3 = (bf16[560,128]{1,0:T(8,128)(2,1)S(1)}, bf16[560,128]{1,0:T(8,128)(2,1)S(1)}, u32[]{:S(2)}, u32[]{:S(2)}) collective-permute-start(bf16[560,128]{1,0:T(8,128)(2,1)S(1)} %collective-permute-done.refs_3_), channel_id=1, source_target_pairs={{0,16},{16,0},{1,17},{17,1},{2,18},{18,2},{3,19},{19,3},{4,20},{20... | collective-permute-start | bytes 430088 | tf_op jit(solution)/shard_map/ppermute | solution.py:717
  18.9 6.5 %collective-permute-start.2 = (bf16[560,128]{1,0:T(8,128)(2,1)S(1)}, bf16[560,128]{1,0:T(8,128)(2,1)S(1)}, u32[]{:S(2)}, u32[]{:S(2)}) collective-permute-start(bf16[560,128]{1,0:T(8,128)(2,1)S(1)} %collective-permute-done.1.refs_3_), channel_id=1, source_target_pairs={{0,32},{32,64},{64,96},{96,128},{128,160},{160,192},{192,224},{224... | collective-permute-start | bytes 430088 | tf_op jit(solution)/shard_map/ppermute | solution.py:734
  18.9 8.7 %collective-permute-start.6 = (bf16[560,128]{1,0:T(8,128)(2,1)S(1)}, bf16[560,128]{1,0:T(8,128)(2,1)S(1)}, u32[]{:S(2)}, u32[]{:S(2)}) collective-permute-start(bf16[560,128]{1,0:T(8,128)(2,1)S(1)} %collective-permute-done.1.refs_3_), channel_id=1, source_target_pairs={{0,16},{16,0},{1,17},{17,1},{2,18},{18,2},{3,19},{19,3},{4,20},{20... | collective-permute-start | bytes 430088 | tf_op jit(solution)/shard_map/ppermute | solution.py:717
  25.4 6.4 %collective-permute-start.5 = (bf16[560,128]{1,0:T(8,128)(2,1)S(1)}, bf16[560,128]{1,0:T(8,128)(2,1)S(1)}, u32[]{:S(2)}, u32[]{:S(2)}) collective-permute-start(bf16[560,128]{1,0:T(8,128)(2,1)S(1)} %collective-permute-done.2.refs_3_), channel_id=1, source_target_pairs={{0,32},{32,64},{64,96},{96,128},{128,160},{160,192},{192,224},{224... | collective-permute-start | bytes 430088 | tf_op jit(solution)/shard_map/ppermute | solution.py:738
  25.5 8.4 %collective-permute-start.8 = (bf16[560,128]{1,0:T(8,128)(2,1)S(1)}, bf16[560,128]{1,0:T(8,128)(2,1)S(1)}, u32[]{:S(2)}, u32[]{:S(2)}) collective-permute-start(bf16[560,128]{1,0:T(8,128)(2,1)S(1)} %collective-permute-done.2.refs_3_), channel_id=1, source_target_pairs={{0,16},{16,0},{1,17},{17,1},{2,18},{18,2},{3,19},{19,3},{4,20},{20... | collective-permute-start | bytes 430088 | tf_op jit(solution)/shard_map/ppermute | solution.py:717
  31.8 6.3 %collective-permute-start.7 = (bf16[560,128]{1,0:T(8,128)(2,1)S(1)}, bf16[560,128]{1,0:T(8,128)(2,1)S(1)}, u32[]{:S(2)}, u32[]{:S(2)}) collective-permute-start(bf16[560,128]{1,0:T(8,128)(2,1)S(1)} %collective-permute-done.5.refs_3_), channel_id=1, source_target_pairs={{0,16},{16,0},{1,17},{17,1},{2,18},{18,2},{3,19},{19,3},{4,20},{20... | collective-permute-start | bytes 430088 | tf_op jit(solution)/shard_map/ppermute | solution.py:717
  38.1 4.5 %copy-start = (bf16[1,128,8192]{2,1,0:T(8,128)(2,1)S(1)}, bf16[1,128,8192]{2,1,0:T(8,128)(2,1)}, u32[]{:S(2)}) copy-start(bf16[1,128,8192]{2,1,0:T(8,128)(2,1)} %param.10) | copy-start | bytes 6291460
  38.1 4.6 %copy-start.4 = (f32[16,128]{1,0:T(8,128)S(1)}, f32[16,128]{1,0:T(8,128)}, u32[]{:S(2)}) copy-start(f32[16,128]{1,0:T(8,128)} %get-tuple-element.53.slope) | copy-start | bytes 24580
  42.6 30.9 %collective-permute-start.14 = (bf16[128,8192]{1,0:T(8,128)(2,1)S(1)}, bf16[128,8192]{1,0:T(8,128)(2,1)S(1)}, u32[]{:S(2)}, u32[]{:S(2)}) collective-permute-start(bf16[128,8192]{1,0:T(8,128)(2,1)S(1)} %bitcast.18), channel_id=1, source_target_pairs={{0,16},{16,0},{1,17},{17,1},{2,18},{18,2},{3,19},{19,3},{4,20},{20... | collective-permute-start | bytes 6291464 | tf_op jit(solution)/shard_map/ppermute | solution.py:717
  42.7 4.9 %collective-permute-start.10 = (f32[16,128]{1,0:T(8,128)S(1)}, f32[16,128]{1,0:T(8,128)S(1)}, u32[]{:S(2)}, u32[]{:S(2)}) collective-permute-start(f32[16,128]{1,0:T(8,128)S(1)} %copy-done.4), channel_id=1, source_target_pairs={{0,16},{16,0},{1,17},{17,1},{2,18},{18,2},{3,19},{19,3},{4,20},{20... | collective-permute-start | bytes 24584 | tf_op jit(solution)/shard_map/ppermute | solution.py:717
  43.2 4.4 %collective-permute-start.9 = (f32[8,128]{1,0:T(8,128)S(1)}, f32[8,128]{1,0:T(8,128)S(1)}, u32[]{:S(2)}, u32[]{:S(2)}) collective-permute-start(f32[8,128]{1,0:T(8,128)S(1)} %get-tuple-element.52.refs_5_), channel_id=1, source_target_pairs={{0,4},{4,8},{8,12},{12,0},{1,5},{5,9},{9,13},{13,1},{2,6},{6,10},{... | collective-permute-start | bytes 12296 | tf_op jit(solution)/shard_map/ppermute | solution.py:751
  44.5 3.1 %collective-permute-start.12 = (f32[8,128]{1,0:T(8,128)S(1)}, f32[8,128]{1,0:T(8,128)S(1)}, u32[]{:S(2)}, u32[]{:S(2)}) collective-permute-start(f32[8,128]{1,0:T(8,128)S(1)} %get-tuple-element.52.refs_5_), channel_id=1, source_target_pairs={{0,12},{4,0},{8,4},{12,8},{1,13},{5,1},{9,5},{13,9},{2,14},{6,2},{... | collective-permute-start | bytes 12296 | tf_op jit(solution)/shard_map/ppermute | solution.py:751
  45.9 4.0 %collective-permute-start.11 = (f32[8,128]{1,0:T(8,128)S(1)}, f32[8,128]{1,0:T(8,128)S(1)}, u32[]{:S(2)}, u32[]{:S(2)}) collective-permute-start(f32[8,128]{1,0:T(8,128)S(1)} %get-tuple-element.52.refs_5_), channel_id=1, source_target_pairs={{0,8},{4,12},{8,0},{12,4},{1,9},{5,13},{9,1},{13,5},{2,10},{6,14},... | collective-permute-start | bytes 12296 | tf_op jit(solution)/shard_map/ppermute | solution.py:751
  69.5 4.0 %collective-permute-start.13 = (f32[56,128]{1,0:T(8,128)S(1)}, f32[56,128]{1,0:T(8,128)S(1)}, u32[]{:S(2)}, u32[]{:S(2)}) collective-permute-start(f32[56,128]{1,0:T(8,128)S(1)} %fold.1.own), channel_id=1, source_target_pairs={{0,16},{16,0},{1,17},{17,1},{2,18},{18,2},{3,19},{19,3},{4,20},{20... | collective-permute-start | bytes 86024 | tf_op jit(solution)/shard_map/ppermute | solution.py:717
  102.7 4.7 %collective-permute-start.15 = (f32[544,128]{1,0:T(8,128)S(1)}, f32[544,128]{1,0:T(8,128)S(1)}, u32[]{:S(2)}, u32[]{:S(2)}) collective-permute-start(f32[544,128]{1,0:T(8,128)S(1)} %bitcast.20), channel_id=1, source_target_pairs={{0,16},{16,0},{1,17},{17,1},{2,18},{18,2},{3,19},{19,3},{4,20},{20... | collective-permute-start | bytes 835592 | tf_op jit(solution)/shard_map/ppermute | solution.py:813
